TPU v7x, 32 devices: a whole 2x2x4 slice. The times are simulated.
32 devices in a mesh: section: 4 (over y, core), dp: 4 (over z), tensor: 2 (over x).
Axes of the slice: x: 2, y: 2, z: 4, core: 2. Of those that a mesh axis runs over, the one named last changes fastest.
Arguments:
- layer_input: bfloat16 [4, 8, 512, 1024], P('dp', None, 'tensor'), may hold values from -6 to 6
- output_grad: bfloat16 [4, 8, 512, 1024], P('dp', None, 'tensor'), may hold values from -6 to 6
- seg_blocks: int32 [8], replicated, may hold values from 2 to 4, as said below
- seg_group: int32 [8], replicated, may hold values from 0 to 3, as said below
- gain_a: bfloat16 [1024], replicated, may hold values from 0.5 to 1.5
- wqkv_a: bfloat16 [1024, 3, 1024], P(None, None, 'tensor'), may hold values from -0.1875 to 0.1875
- wout_a: bfloat16 [1024, 1024], P('tensor'), may hold values from -0.75 to 0.75
- gain_b: bfloat16 [1024], replicated, may hold values from 0.5 to 1.5
- up_b: bfloat16 [1024, 4096], P(None, 'tensor'), may hold values from -0.1875 to 0.1875
- down_b: bfloat16 [4096, 1024], P('tensor'), may hold values from -0.09375 to 0.09375
- gain_c: bfloat16 [1024], replicated, may hold values from 0.5 to 1.5
- gain_s: bfloat16 [1024], replicated, may hold values from 0.5 to 1.5
- wqkv_c: bfloat16 [1024, 3, 1024], P(None, None, 'tensor'), may hold values from -0.1875 to 0.1875
- sqkv_c: bfloat16 [1024, 3, 1024], P(None, None, 'tensor'), may hold values from -0.1875 to 0.1875
- wout_c: bfloat16 [1024, 1024], P('tensor'), may hold values from -0.75 to 0.75
- sout_c: bfloat16 [1024, 1024], P('tensor'), may hold values from -0.75 to 0.75
- gate_bias: bfloat16 [1024], replicated, may hold values from -1 to 3
- init_states: bfloat16 [512, 1024], P('tensor'), may hold values from -6 to 6
- gain_d: bfloat16 [1024], replicated, may hold values from 0.5 to 1.5
- up_d: bfloat16 [1024, 4096], P(None, 'tensor'), may hold values from -0.1875 to 0.1875
- down_d: bfloat16 [4096, 1024], P('tensor'), may hold values from -0.09375 to 0.09375
Outputs:
- layer_output: bfloat16 [4, 8, 512, 1024], P('dp', None, 'tensor', 'section')
- final_states: float32 [4, 512, 3, 1024], P('dp', 'tensor', None, 'section')
- input_grad: float32 [4, 8, 512, 1024], P('dp', None, 'tensor', 'section')
- grad_gain_a: float32 [1024], P('section')
- grad_wqkv_a: float32 [1024, 3, 1024], P('section', None, 'tensor')
- grad_wout_a: float32 [1024, 1024], P('tensor', 'section')
- grad_gain_b: float32 [1024], P('section')
- grad_up_b: float32 [1024, 4096], P('section', 'tensor')
- grad_down_b: float32 [4096, 1024], P('tensor', 'section')
- grad_gain_c: float32 [1024], P('section')
- grad_gain_s: float32 [1024], P('section')
- grad_wqkv_c: float32 [1024, 3, 1024], P('section', None, 'tensor')
- grad_sqkv_c: float32 [1024, 3, 1024], P('section', None, 'tensor')
- grad_wout_c: float32 [1024, 1024], P('tensor', 'section')
- grad_sout_c: float32 [1024, 1024], P('tensor', 'section')
- grad_gate_bias: float32 [1024], P('section')
- grad_init_states: float32 [512, 1024], P('tensor', 'section')
- grad_gain_d: float32 [1024], P('section')
- grad_up_d: float32 [1024, 4096], P('section', 'tensor')
- grad_down_d: float32 [4096, 1024], P('tensor', 'section')
Inputs may be any that keep to these rules, and one draw needn't show every extreme that they name: `seg_blocks`: every segment has 2 or 4 blocks, as many segments of each length. `seg_group`: each data group holds one segment of 4 blocks; half of the groups hold two segments of 2 blocks besides, so that a group holds at most 8 blocks and half of the groups are full.
All inputs are finite; a program needn't handle non-finite values.
Results may differ from a plain program's by a relative error of at most 0.034.
Values may be sent and summed in bfloat16 or wider, within the bound.
A program may use at most 576 MiB of HBM per device.

v0:
```python
import math

import jax
import jax.numpy as jnp
from jax import lax
from jax.sharding import PartitionSpec as P

HEAD_DIM = 128
SLOTS = 3


EPSILON = 1e-06
NEGATIVE = -1e30


def shifted(value, axis, by):
    devices = lax.axis_size(axis)
    pairs = [(i, i + by) for i in range(devices) if 0 <= i + by < devices]
    return lax.ppermute(value, axis, pairs)


def for_sending(value):
    return jax.tree.map(lambda a: a.astype(jnp.bfloat16) if a.dtype == jnp.float32 else a, value)


def layout(seg_blocks, seg_group, group_index, block_count):
    mine = seg_group == group_index
    lengths = jnp.where(mine, seg_blocks, 0)
    offsets = jnp.cumsum(lengths) - lengths
    ranking = jnp.cumsum(mine.astype(jnp.int32)) - mine.astype(jnp.int32)
    blocks = jnp.arange(block_count, dtype=jnp.int32)[None, :]
    inside = mine[:, None] & (blocks >= offsets[:, None]) & (blocks < (offsets + lengths)[:, None])
    begins = jnp.any(inside & (blocks == offsets[:, None]), axis=0)
    closes = jnp.any(inside & (blocks == (offsets + lengths - 1)[:, None]), axis=0)
    lively = jnp.any(inside, axis=0)
    numbers = jnp.sum(jnp.where(inside, ranking[:, None], 0), axis=0)
    return (begins, closes, lively, numbers)


def inverse_rms(values):
    return lax.rsqrt(jnp.mean(values * values, axis=-1, keepdims=True) + EPSILON)


def norm_back(values, gain, grad_normed):
    factor = inverse_rms(values)
    scaled = values * factor
    grad_scaled = grad_normed * gain
    grad_values = factor * (
        grad_scaled - scaled * jnp.mean(grad_scaled * scaled, axis=-1, keepdims=True)
    )
    return (grad_values, jnp.sum(grad_normed * scaled, axis=0))


def smooth(values):
    return jax.nn.gelu(values, approximate=True)


def split_heads(rows_in):
    return rows_in.reshape(rows_in.shape[0], -1, HEAD_DIM)


def attend_forward(queries, key_rows, value_rows, allowed):
    score_scale = 1.0 / math.sqrt(HEAD_DIM)
    scores = (
        jnp.einsum("rhd,khd->hrk", queries, key_rows, preferred_element_type=jnp.float32)
        * score_scale
    )
    scores = jnp.where(allowed[None], scores, NEGATIVE)
    largest = jnp.max(scores, axis=-1, keepdims=True)
    totals = jnp.sum(jnp.exp(scores - largest), axis=-1, keepdims=True)
    log_total = largest + jnp.log(totals)
    weights = jnp.exp(scores - log_total).astype(jnp.bfloat16)
    mixture_output = jnp.einsum(
        "hrk,khd->rhd", weights, value_rows, preferred_element_type=jnp.float32
    )
    return (mixture_output, log_total[..., 0])


def attend_backward(queries, key_rows, value_rows, allowed, log_total, grad_mixture):
    score_scale = 1.0 / math.sqrt(HEAD_DIM)
    scores = (
        jnp.einsum("rhd,khd->hrk", queries, key_rows, preferred_element_type=jnp.float32)
        * score_scale
    )
    scores = jnp.where(allowed[None], scores, NEGATIVE)
    weights = jnp.exp(scores - log_total[..., None])
    rounded = weights.astype(jnp.bfloat16)
    grad_weights = jnp.einsum(
        "rhd,khd->hrk", grad_mixture, value_rows, preferred_element_type=jnp.float32
    )
    grad_values = jnp.einsum(
        "hrk,rhd->khd", rounded, grad_mixture, preferred_element_type=jnp.float32
    )
    inner_sum = jnp.sum(weights * grad_weights, axis=-1, keepdims=True)
    grad_scores = (weights * (grad_weights - inner_sum)).astype(jnp.bfloat16)
    grad_queries = (
        jnp.einsum("hrk,khd->rhd", grad_scores, key_rows, preferred_element_type=jnp.float32)
        * score_scale
    )
    grad_keys = (
        jnp.einsum("hrk,rhd->khd", grad_scores, queries, preferred_element_type=jnp.float32)
        * score_scale
    )
    return (grad_queries, grad_keys, grad_values)


def place_row(store, position, value, active_tick):
    previous = lax.dynamic_index_in_dim(store, position, 0, False)
    return lax.dynamic_update_index_in_dim(
        store, jnp.where(active_tick, value, previous), position, 0
    )


def renewed(grad_sums, active_tick, changes):
    return tuple(
        (
            total + jnp.where(active_tick, changes[position], 0.0) if position in changes else total
            for position, total in enumerate(grad_sums)
        )
    )


def body(
    layer_input,
    output_grad,
    seg_blocks,
    seg_group,
    gain_a,
    wqkv_a,
    wout_a,
    gain_b,
    up_b,
    down_b,
    gain_c,
    gain_s,
    wqkv_c,
    sqkv_c,
    wout_c,
    sout_c,
    gate_bias,
    init_states,
    gain_d,
    up_d,
    down_d,
):
    block_count = layer_input.shape[1]
    shard_rows = layer_input.shape[2]
    model_width = layer_input.shape[3]
    tensor_count = lax.axis_size("tensor")
    token_rows = shard_rows * tensor_count
    state_shard = init_states.shape[0]
    state_count = state_shard * tensor_count
    local_width = wqkv_a.shape[2]
    local_heads = local_width // HEAD_DIM
    section_index = lax.axis_index("section")
    group_index = lax.axis_index("dp")
    on_cell_section = section_index == 2
    begins, closes, lively, numbers = layout(seg_blocks, seg_group, group_index, block_count)
    token_gains = jnp.stack([gain_a, gain_b, gain_c, gain_d]).astype(jnp.float32)
    state_gain = gain_s.astype(jnp.float32)
    retain = jax.nn.sigmoid(gate_bias.astype(jnp.float32))
    initial = init_states.astype(jnp.float32)
    empty_state = jnp.zeros((state_count, model_width), jnp.float32)
    empty_token_store = jnp.zeros((token_rows, 4, local_width), jnp.bfloat16)
    empty_state_store = jnp.zeros((state_count, 4, local_width), jnp.bfloat16)
    empty_token_lse = jnp.zeros((local_heads, token_rows), jnp.float32)
    empty_state_lse = jnp.zeros((local_heads, state_count), jnp.float32)
    empty_carry = jnp.zeros((token_rows, local_width), jnp.float32)
    every_key = jnp.ones((state_count, token_rows + state_count), bool)
    state_keys_all = jnp.ones((token_rows, state_count), bool)

    def token_masks(opening):
        later_keys = lax.broadcasted_iota(
            jnp.int32, (token_rows, token_rows), 1
        ) > lax.broadcasted_iota(jnp.int32, (token_rows, token_rows), 0)
        return (jnp.logical_and(later_keys, jnp.logical_not(opening)), jnp.logical_not(later_keys))

    def plain_forward(normed_tok, normed_st, prior_block, opening):
        projected = jnp.einsum(
            "rd,dcn->rcn", normed_tok, wqkv_a, preferred_element_type=jnp.float32
        ).astype(jnp.bfloat16)
        reach_prior, reach_current = token_masks(opening)
        allowed = jnp.concatenate([reach_prior, reach_current], axis=1)
        key_rows = jnp.concatenate([prior_block[:, 1], projected[:, 1]], axis=0)
        value_rows = jnp.concatenate([prior_block[:, 2], projected[:, 2]], axis=0)
        mixture_output, token_lse = attend_forward(
            split_heads(projected[:, 0]), split_heads(key_rows), split_heads(value_rows), allowed
        )
        mixture_output = mixture_output.reshape(token_rows, local_width).astype(jnp.bfloat16)
        branch = jnp.dot(mixture_output, wout_a, preferred_element_type=jnp.float32)
        stored = jnp.concatenate([projected, mixture_output[:, None]], axis=1)
        return (branch, empty_state, stored, empty_state_store, token_lse, empty_state_lse)

    def feed_forward(up_projection_weight, down_projection_weight):

        def forward_fn(normed_tok, normed_st, prior_block, opening):
            hidden_rows = jnp.dot(
                normed_tok, up_projection_weight, preferred_element_type=jnp.float32
            )
            active_flags = smooth(hidden_rows).astype(jnp.bfloat16)
            branch = jnp.dot(
                active_flags, down_projection_weight, preferred_element_type=jnp.float32
            )
            return (
                branch,
                empty_state,
                empty_token_store,
                empty_state_store,
                empty_token_lse,
                empty_state_lse,
            )

        return forward_fn

    def recurrent_forward(normed_tok, normed_st, prior_block, opening):
        projected = jnp.einsum(
            "rd,dcn->rcn", normed_tok, wqkv_c, preferred_element_type=jnp.float32
        ).astype(jnp.bfloat16)
        state_proj = jnp.einsum(
            "sd,dcn->scn", normed_st, sqkv_c, preferred_element_type=jnp.float32
        ).astype(jnp.bfloat16)
        reach_prior, reach_current = token_masks(opening)
        allowed = jnp.concatenate([reach_prior, reach_current, state_keys_all], axis=1)
        token_keys = jnp.concatenate([prior_block[:, 1], projected[:, 1], state_proj[:, 1]], axis=0)
        token_values = jnp.concatenate(
            [prior_block[:, 2], projected[:, 2], state_proj[:, 2]], axis=0
        )
        token_mixture, token_lse = attend_forward(
            split_heads(projected[:, 0]),
            split_heads(token_keys),
            split_heads(token_values),
            allowed,
        )
        state_keys = jnp.concatenate([projected[:, 1], state_proj[:, 1]], axis=0)
        state_values = jnp.concatenate([projected[:, 2], state_proj[:, 2]], axis=0)
        state_mixture, state_lse = attend_forward(
            split_heads(state_proj[:, 0]),
            split_heads(state_keys),
            split_heads(state_values),
            every_key,
        )
        token_mixture = token_mixture.reshape(token_rows, local_width).astype(jnp.bfloat16)
        state_mixture = state_mixture.reshape(state_count, local_width).astype(jnp.bfloat16)
        branch = jnp.dot(token_mixture, wout_c, preferred_element_type=jnp.float32)
        update_term = jnp.dot(state_mixture, sout_c, preferred_element_type=jnp.float32)
        stored = jnp.concatenate([projected, token_mixture[:, None]], axis=1)
        state_stored = jnp.concatenate([state_proj, state_mixture[:, None]], axis=1)
        return (branch, update_term, stored, state_stored, token_lse, state_lse)

    def plain_backward(
        grad_tok,
        grad_st,
        normed_tok,
        normed_st,
        tok_block,
        st_block,
        prior_block,
        token_lse,
        state_lse,
        opening,
        carry_keys,
        carry_values,
        grad_sums,
        active_tick,
    ):
        reach_prior, reach_current = token_masks(opening)
        allowed = jnp.concatenate([reach_prior, reach_current], axis=1)
        key_rows = jnp.concatenate([prior_block[:, 1], tok_block[:, 1]], axis=0)
        value_rows = jnp.concatenate([prior_block[:, 2], tok_block[:, 2]], axis=0)
        weight_out = jnp.einsum(
            "rn,rd->nd", tok_block[:, 3], grad_tok, preferred_element_type=jnp.float32
        )
        grad_mixture = jnp.einsum(
            "rd,nd->rn", grad_tok, wout_a, preferred_element_type=jnp.float32
        ).astype(jnp.bfloat16)
        grad_query, grad_keys, grad_values = attend_backward(
            split_heads(tok_block[:, 0]),
            split_heads(key_rows),
            split_heads(value_rows),
            allowed,
            token_lse,
            split_heads(grad_mixture),
        )
        grad_query = grad_query.reshape(token_rows, local_width)
        grad_keys = grad_keys.reshape(2 * token_rows, local_width)
        grad_values = grad_values.reshape(2 * token_rows, local_width)
        grad_proj = jnp.stack(
            [
                grad_query,
                grad_keys[token_rows:] + carry_keys,
                grad_values[token_rows:] + carry_values,
            ],
            axis=1,
        ).astype(jnp.bfloat16)
        weight_in = jnp.einsum(
            "rd,rcn->dcn", normed_tok, grad_proj, preferred_element_type=jnp.float32
        )
        grad_normed = jnp.einsum(
            "rcn,dcn->rd", grad_proj, wqkv_a, preferred_element_type=jnp.float32
        )
        return (
            grad_normed,
            empty_state,
            grad_keys[:token_rows],
            grad_values[:token_rows],
            renewed(grad_sums, active_tick, {0: weight_in, 1: weight_out}),
        )

    def feed_backward(up_projection_weight, down_projection_weight, up_slot, down_slot):

        def backward_fn(
            grad_tok,
            grad_st,
            normed_tok,
            normed_st,
            tok_block,
            st_block,
            prior_block,
            token_lse,
            state_lse,
            opening,
            carry_keys,
            carry_values,
            grad_sums,
            active_tick,
        ):
            hidden_rows = jnp.dot(
                normed_tok, up_projection_weight, preferred_element_type=jnp.float32
            )
            active_flags, gelu_back = jax.vjp(smooth, hidden_rows)
            weight_down = jnp.einsum(
                "rf,rd->fd",
                active_flags.astype(jnp.bfloat16),
                grad_tok,
                preferred_element_type=jnp.float32,
            )
            grad_active = jnp.einsum(
                "rd,fd->rf", grad_tok, down_projection_weight, preferred_element_type=jnp.float32
            )
            grad_hidden = gelu_back(grad_active)[0].astype(jnp.bfloat16)
            weight_up = jnp.einsum(
                "rd,rf->df", normed_tok, grad_hidden, preferred_element_type=jnp.float32
            )
            grad_normed = jnp.einsum(
                "rf,df->rd", grad_hidden, up_projection_weight, preferred_element_type=jnp.float32
            )
            return (
                grad_normed,
                empty_state,
                empty_carry,
                empty_carry,
                renewed(grad_sums, active_tick, {up_slot: weight_up, down_slot: weight_down}),
            )

        return backward_fn

    def recurrent_backward(
        grad_tok,
        grad_st,
        normed_tok,
        normed_st,
        tok_block,
        st_block,
        prior_block,
        token_lse,
        state_lse,
        opening,
        carry_keys,
        carry_values,
        grad_sums,
        active_tick,
    ):
        reach_prior, reach_current = token_masks(opening)
        allowed = jnp.concatenate([reach_prior, reach_current, state_keys_all], axis=1)
        token_keys = jnp.concatenate([prior_block[:, 1], tok_block[:, 1], st_block[:, 1]], axis=0)
        token_values = jnp.concatenate([prior_block[:, 2], tok_block[:, 2], st_block[:, 2]], axis=0)
        state_keys = jnp.concatenate([tok_block[:, 1], st_block[:, 1]], axis=0)
        state_values = jnp.concatenate([tok_block[:, 2], st_block[:, 2]], axis=0)
        weight_out = jnp.einsum(
            "rn,rd->nd", tok_block[:, 3], grad_tok, preferred_element_type=jnp.float32
        )
        weight_state_out = jnp.einsum(
            "sn,sd->nd", st_block[:, 3], grad_st, preferred_element_type=jnp.float32
        )
        grad_token_mixture = jnp.einsum(
            "rd,nd->rn", grad_tok, wout_c, preferred_element_type=jnp.float32
        ).astype(jnp.bfloat16)
        grad_state_mixture = jnp.einsum(
            "sd,nd->sn", grad_st, sout_c, preferred_element_type=jnp.float32
        ).astype(jnp.bfloat16)
        grad_query, grad_keys, grad_values = attend_backward(
            split_heads(tok_block[:, 0]),
            split_heads(token_keys),
            split_heads(token_values),
            allowed,
            token_lse,
            split_heads(grad_token_mixture),
        )
        state_query, state_grad_keys, state_grad_values = attend_backward(
            split_heads(st_block[:, 0]),
            split_heads(state_keys),
            split_heads(state_values),
            every_key,
            state_lse,
            split_heads(grad_state_mixture),
        )
        grad_query = grad_query.reshape(token_rows, local_width)
        grad_keys = grad_keys.reshape(2 * token_rows + state_count, local_width)
        grad_values = grad_values.reshape(2 * token_rows + state_count, local_width)
        state_query = state_query.reshape(state_count, local_width)
        state_grad_keys = state_grad_keys.reshape(token_rows + state_count, local_width)
        state_grad_values = state_grad_values.reshape(token_rows + state_count, local_width)
        own_keys = (
            grad_keys[token_rows : 2 * token_rows] + state_grad_keys[:token_rows] + carry_keys
        )
        own_values = (
            grad_values[token_rows : 2 * token_rows] + state_grad_values[:token_rows] + carry_values
        )
        cell_keys = grad_keys[2 * token_rows :] + state_grad_keys[token_rows:]
        cell_values = grad_values[2 * token_rows :] + state_grad_values[token_rows:]
        grad_proj = jnp.stack([grad_query, own_keys, own_values], axis=1).astype(jnp.bfloat16)
        grad_state_proj = jnp.stack([state_query, cell_keys, cell_values], axis=1).astype(
            jnp.bfloat16
        )
        weight_in = jnp.einsum(
            "rd,rcn->dcn", normed_tok, grad_proj, preferred_element_type=jnp.float32
        )
        weight_state_in = jnp.einsum(
            "sd,scn->dcn", normed_st, grad_state_proj, preferred_element_type=jnp.float32
        )
        grad_normed = jnp.einsum(
            "rcn,dcn->rd", grad_proj, wqkv_c, preferred_element_type=jnp.float32
        )
        grad_state_normed = jnp.einsum(
            "scn,dcn->sd", grad_state_proj, sqkv_c, preferred_element_type=jnp.float32
        )
        changes = {4: weight_in, 5: weight_state_in, 6: weight_out, 7: weight_state_out}
        return (
            grad_normed,
            grad_state_normed,
            grad_keys[:token_rows],
            grad_values[:token_rows],
            renewed(grad_sums, active_tick, changes),
        )

    forward_branches = [
        plain_forward,
        feed_forward(up_b, down_b),
        recurrent_forward,
        feed_forward(up_d, down_d),
    ]
    backward_branches = [
        plain_backward,
        feed_backward(up_b, down_b, 2, 3),
        recurrent_backward,
        feed_backward(up_d, down_d, 8, 9),
    ]

    def forward_tick(tick_number, carried):
        (
            received,
            state_carry,
            tok_normed,
            st_normed,
            tok_stored,
            st_stored,
            tok_lse_all,
            st_lse_all,
            entered,
            state_entered,
            updates,
            leaving_rows,
            finals,
        ) = carried
        block_number = tick_number - section_index
        active_tick = (block_number >= 0) & (block_number < block_count)
        block_index = jnp.clip(block_number, 0, block_count - 1)
        opening = begins[block_index]
        entering = jnp.where(
            section_index == 0, layer_input[0, block_index].astype(jnp.float32), received
        )
        state_in = jnp.where(opening, initial, state_carry)
        token_gain = token_gains[section_index]
        normed_shard = (entering * inverse_rms(entering) * token_gain).astype(jnp.bfloat16)
        state_normed_shard = (state_in * inverse_rms(state_in) * state_gain).astype(jnp.bfloat16)
        normed_tok, normed_st = (
            lax.all_gather(normed_shard, "tensor", axis=0, tiled=True),
            lax.all_gather(state_normed_shard, "tensor", axis=0, tiled=True),
        )
        prior_block = tok_stored[jnp.maximum(block_index - 1, 0)]
        branch, update_term, stored, state_stored, token_lse, state_lse = lax.switch(
            section_index, forward_branches, normed_tok, normed_st, prior_block, opening
        )
        branch_shard, update_shard = (
            lax.psum_scatter(
                branch.astype(jnp.bfloat16), "tensor", scatter_dimension=0, tiled=True
            ).astype(jnp.float32),
            lax.psum_scatter(
                update_term.astype(jnp.bfloat16), "tensor", scatter_dimension=0, tiled=True
            ).astype(jnp.float32),
        )
        leaving = entering + branch_shard
        state_new = retain * state_in + (1.0 - retain) * update_shard
        tok_normed = place_row(tok_normed, block_index, normed_tok, active_tick)
        st_normed = place_row(st_normed, block_index, normed_st, active_tick)
        tok_stored = place_row(tok_stored, block_index, stored, active_tick)
        st_stored = place_row(st_stored, block_index, state_stored, active_tick)
        tok_lse_all = place_row(tok_lse_all, block_index, token_lse, active_tick)
        st_lse_all = place_row(st_lse_all, block_index, state_lse, active_tick)
        entered = place_row(entered, block_index, entering, active_tick)
        state_entered = place_row(state_entered, block_index, state_in, active_tick)
        updates = place_row(updates, block_index, update_shard, active_tick)
        leaving_rows = place_row(leaving_rows, block_index, leaving, active_tick)
        on_cell = active_tick & on_cell_section
        state_carry = jnp.where(on_cell, state_new, state_carry)
        keep_final = on_cell & closes[block_index] & lively[block_index]
        slot_hit = (jnp.arange(SLOTS, dtype=jnp.int32) == numbers[block_index])[
            None, :, None
        ] & keep_final
        finals = jnp.where(slot_hit, state_new[:, None, :], finals)
        received = shifted(leaving.astype(jnp.bfloat16), "section", 1).astype(leaving.dtype)
        return (
            received,
            state_carry,
            tok_normed,
            st_normed,
            tok_stored,
            st_stored,
            tok_lse_all,
            st_lse_all,
            entered,
            state_entered,
            updates,
            leaving_rows,
            finals,
        )

    forward_start = (
        jnp.zeros((shard_rows, model_width), jnp.float32),
        jnp.zeros((state_shard, model_width), jnp.float32),
        jnp.zeros((block_count, token_rows, model_width), jnp.bfloat16),
        jnp.zeros((block_count, state_count, model_width), jnp.bfloat16),
        jnp.zeros((block_count, token_rows, 4, local_width), jnp.bfloat16),
        jnp.zeros((block_count, state_count, 4, local_width), jnp.bfloat16),
        jnp.zeros((block_count, local_heads, token_rows), jnp.float32),
        jnp.zeros((block_count, local_heads, state_count), jnp.float32),
        jnp.zeros((block_count, shard_rows, model_width), jnp.float32),
        jnp.zeros((block_count, state_shard, model_width), jnp.float32),
        jnp.zeros((block_count, state_shard, model_width), jnp.float32),
        jnp.zeros((block_count, shard_rows, model_width), jnp.float32),
        jnp.zeros((state_shard, SLOTS, model_width), jnp.float32),
    )
    (
        _,
        _,
        tok_normed,
        st_normed,
        tok_stored,
        st_stored,
        tok_lse_all,
        st_lse_all,
        entered,
        state_entered,
        updates,
        leaving_rows,
        finals,
    ) = lax.fori_loop(0, block_count + 3, forward_tick, forward_start)
    gain_rows_of_section = jnp.array([0, 1, 2, 4], dtype=jnp.int32)
    small_rows = jnp.arange(6, dtype=jnp.int32)[:, None]

    def backward_tick(tick_number, carried):
        (
            received,
            state_grad,
            carry_keys,
            carry_values,
            grad_sums,
            smalls,
            initial_grad,
            input_rows,
        ) = carried
        block_number = block_count - 1 - tick_number + 3 - section_index
        active_tick = (block_number >= 0) & (block_number < block_count)
        block_index = jnp.clip(block_number, 0, block_count - 1)
        opening = begins[block_index]
        arriving = jnp.where(
            section_index == 3,
            output_grad[0, block_index].astype(jnp.float32)
            * lively[block_index].astype(jnp.float32),
            received,
        )
        update_grad = (1.0 - retain) * state_grad
        grad_tok, grad_st = (
            lax.all_gather(arriving.astype(jnp.bfloat16), "tensor", axis=0, tiled=True),
            lax.all_gather(update_grad.astype(jnp.bfloat16), "tensor", axis=0, tiled=True),
        )
        grad_normed_tok, grad_normed_st, prior_keys, prior_values, grad_sums = lax.switch(
            section_index,
            backward_branches,
            grad_tok,
            grad_st,
            tok_normed[block_index],
            st_normed[block_index],
            tok_stored[block_index],
            st_stored[block_index],
            tok_stored[jnp.maximum(block_index - 1, 0)],
            tok_lse_all[block_index],
            st_lse_all[block_index],
            opening,
            carry_keys,
            carry_values,
            grad_sums,
            active_tick,
        )
        tok_shard, st_shard = (
            lax.psum_scatter(
                grad_normed_tok.astype(jnp.bfloat16), "tensor", scatter_dimension=0, tiled=True
            ).astype(jnp.float32),
            lax.psum_scatter(
                grad_normed_st.astype(jnp.bfloat16), "tensor", scatter_dimension=0, tiled=True
            ).astype(jnp.float32),
        )
        grad_entering, token_gain_term = norm_back(
            entered[block_index], token_gains[section_index], tok_shard
        )
        leaving_grad = arriving + grad_entering
        state_in = state_entered[block_index]
        grad_state_norm, state_gain_term = norm_back(state_in, state_gain, st_shard)
        grad_state_in = retain * state_grad + grad_state_norm
        bias_term = (
            jnp.sum(state_grad * (state_in - updates[block_index]), axis=0)
            * retain
            * (1.0 - retain)
        )
        on_cell = active_tick & on_cell_section
        gain_part = (small_rows == gain_rows_of_section[section_index]).astype(
            jnp.float32
        ) * token_gain_term[None, :]
        cell_part = (small_rows == 3).astype(jnp.float32) * state_gain_term[None, :] + (
            small_rows == 5
        ).astype(jnp.float32) * bias_term[None, :]
        smalls = (
            smalls + jnp.where(active_tick, gain_part, 0.0) + jnp.where(on_cell, cell_part, 0.0)
        )
        initial_grad = initial_grad + jnp.where(on_cell & opening, grad_state_in, 0.0)
        state_grad = jnp.where(on_cell, jnp.where(opening, 0.0, grad_state_in), state_grad)
        carry_keys = jnp.where(active_tick, prior_keys, carry_keys)
        carry_values = jnp.where(active_tick, prior_values, carry_values)
        input_rows = place_row(input_rows, block_index, leaving_grad, active_tick)
        received = shifted(for_sending(leaving_grad), "section", -1).astype(leaving_grad.dtype)
        return (
            received,
            state_grad,
            carry_keys,
            carry_values,
            grad_sums,
            smalls,
            initial_grad,
            input_rows,
        )

    zero_grads = (
        jnp.zeros(wqkv_a.shape, jnp.float32),
        jnp.zeros(wout_a.shape, jnp.float32),
        jnp.zeros(up_b.shape, jnp.float32),
        jnp.zeros(down_b.shape, jnp.float32),
        jnp.zeros(wqkv_c.shape, jnp.float32),
        jnp.zeros(sqkv_c.shape, jnp.float32),
        jnp.zeros(wout_c.shape, jnp.float32),
        jnp.zeros(sout_c.shape, jnp.float32),
        jnp.zeros(up_d.shape, jnp.float32),
        jnp.zeros(down_d.shape, jnp.float32),
    )
    backward_start = (
        jnp.zeros((shard_rows, model_width), jnp.float32),
        jnp.zeros((state_shard, model_width), jnp.float32),
        empty_carry,
        empty_carry,
        zero_grads,
        jnp.zeros((6, model_width), jnp.float32),
        jnp.zeros((state_shard, model_width), jnp.float32),
        jnp.zeros((block_count, shard_rows, model_width), jnp.float32),
    )
    _, _, _, _, grad_sums, smalls, initial_grad, input_rows = lax.fori_loop(
        0, block_count + 3, backward_tick, backward_start
    )
    out_term = jnp.where(
        section_index == 3, leaving_rows * lively[:, None, None].astype(jnp.float32), 0.0
    )[None]
    input_term = jnp.where(section_index == 0, input_rows, 0.0)[None]
    final_term = jnp.where(section_index == 2, finals, 0.0)[None]
    out_share, input_share, final_share = (
        lax.psum_scatter(
            out_term.astype(jnp.bfloat16), "section", scatter_dimension=3, tiled=True
        ).astype(jnp.float32),
        lax.psum_scatter(
            input_term.astype(jnp.bfloat16), "section", scatter_dimension=3, tiled=True
        ).astype(jnp.float32),
        lax.psum_scatter(
            final_term.astype(jnp.bfloat16), "section", scatter_dimension=3, tiled=True
        ).astype(jnp.float32),
    )
    (
        grad_qkv_a,
        grad_out_a,
        grad_upper_b,
        grad_lower_b,
        grad_qkv_c,
        grad_state_qkv,
        grad_out_c,
        grad_state_out,
        grad_upper_d,
        grad_lower_d,
    ) = grad_sums
    totals = (
        lax.psum(grad_qkv_a.astype(jnp.bfloat16), "dp").astype(jnp.float32),
        lax.psum(grad_out_a.astype(jnp.bfloat16), "dp").astype(jnp.float32),
        lax.psum(grad_upper_b.astype(jnp.bfloat16), "dp").astype(jnp.float32),
        lax.psum(grad_lower_b.astype(jnp.bfloat16), "dp").astype(jnp.float32),
        lax.psum(grad_qkv_c.astype(jnp.bfloat16), "dp").astype(jnp.float32),
        lax.psum(grad_state_qkv.astype(jnp.bfloat16), "dp").astype(jnp.float32),
        lax.psum(grad_out_c.astype(jnp.bfloat16), "dp").astype(jnp.float32),
        lax.psum(grad_state_out.astype(jnp.bfloat16), "dp").astype(jnp.float32),
        lax.psum(grad_upper_d.astype(jnp.bfloat16), "dp").astype(jnp.float32),
        lax.psum(grad_lower_d.astype(jnp.bfloat16), "dp").astype(jnp.float32),
        lax.psum(initial_grad.astype(jnp.bfloat16), "dp").astype(jnp.float32),
    )
    small_total = lax.psum(smalls, ("dp", "tensor"))
    shares = (
        lax.psum_scatter(
            totals[0].astype(jnp.bfloat16), "section", scatter_dimension=0, tiled=True
        ).astype(jnp.float32),
        lax.psum_scatter(
            totals[1].astype(jnp.bfloat16), "section", scatter_dimension=1, tiled=True
        ).astype(jnp.float32),
        lax.psum_scatter(
            totals[2].astype(jnp.bfloat16), "section", scatter_dimension=0, tiled=True
        ).astype(jnp.float32),
        lax.psum_scatter(
            totals[3].astype(jnp.bfloat16), "section", scatter_dimension=1, tiled=True
        ).astype(jnp.float32),
        lax.psum_scatter(
            totals[4].astype(jnp.bfloat16), "section", scatter_dimension=0, tiled=True
        ).astype(jnp.float32),
        lax.psum_scatter(
            totals[5].astype(jnp.bfloat16), "section", scatter_dimension=0, tiled=True
        ).astype(jnp.float32),
        lax.psum_scatter(
            totals[6].astype(jnp.bfloat16), "section", scatter_dimension=1, tiled=True
        ).astype(jnp.float32),
        lax.psum_scatter(
            totals[7].astype(jnp.bfloat16), "section", scatter_dimension=1, tiled=True
        ).astype(jnp.float32),
        lax.psum_scatter(
            totals[8].astype(jnp.bfloat16), "section", scatter_dimension=0, tiled=True
        ).astype(jnp.float32),
        lax.psum_scatter(
            totals[9].astype(jnp.bfloat16), "section", scatter_dimension=1, tiled=True
        ).astype(jnp.float32),
        lax.psum_scatter(
            totals[10].astype(jnp.bfloat16), "section", scatter_dimension=1, tiled=True
        ).astype(jnp.float32),
        lax.psum_scatter(
            small_total.astype(jnp.bfloat16), "section", scatter_dimension=1, tiled=True
        ).astype(jnp.float32),
    )
    small_share = shares[11]
    return (
        out_share.astype(jnp.bfloat16),
        final_share,
        input_share,
        small_share[0],
        shares[0],
        shares[1],
        small_share[1],
        shares[2],
        shares[3],
        small_share[2],
        small_share[3],
        shares[4],
        shares[5],
        shares[6],
        shares[7],
        small_share[5],
        shares[10],
        small_share[4],
        shares[8],
        shares[9],
    )


def solution(mesh):
    in_specs = (
        P("dp", None, "tensor", None),
        P("dp", None, "tensor", None),
        P(),
        P(),
        P(),
        P(None, None, "tensor"),
        P("tensor", None),
        P(),
        P(None, "tensor"),
        P("tensor", None),
        P(),
        P(),
        P(None, None, "tensor"),
        P(None, None, "tensor"),
        P("tensor", None),
        P("tensor", None),
        P(),
        P("tensor", None),
        P(),
        P(None, "tensor"),
        P("tensor", None),
    )
    out_specs = (
        P("dp", None, "tensor", "section"),
        P("dp", "tensor", None, "section"),
        P("dp", None, "tensor", "section"),
        P("section"),
        P("section", None, "tensor"),
        P("tensor", "section"),
        P("section"),
        P("section", "tensor"),
        P("tensor", "section"),
        P("section"),
        P("section"),
        P("section", None, "tensor"),
        P("section", None, "tensor"),
        P("tensor", "section"),
        P("tensor", "section"),
        P("section"),
        P("tensor", "section"),
        P("section"),
        P("section", "tensor"),
        P("tensor", "section"),
    )
    return jax.shard_map(body, mesh=mesh, in_specs=in_specs, out_specs=out_specs, check_vma=False)
```

profile of v0, /device:TPU:0, one launch (start us, length us, event | category | flops | bytes accessed | tf_op | source)
XLA Modules:
  0.0 5701.9 jit_solution(15444458187994090)
XLA Ops:
  60.9 1770.1 %while.89 = (s32[]{:T(128)}, f32[256,1024]{1,0:T(8,128)}, f32[256,1024]{1,0:T(8,128)S(1)}, bf16[8,512,1024]{2,1,0:T(8,128)(2,1)}, bf16[8,512,1024]{1,2,0:T(8,128...) while((s32[]{:T(128)}, f32[256,1024]{1,0:T(8,128)}, ...), condition=%wide.region_21.22_spmd.clone, body=%wide.region_6.21_spmd.clone.sunk | while | flops 7064258048 | bytes 304978432 | solution.py:567
  113.6 45.6 conditional.7
  273.8 45.7 conditional.7
  1864.5 2996.5 %while.90 = (s32[]{:T(128)}, f32[256,1024]{1,0:T(8,128)S(1)}, f32[256,1024]{1,0:T(8,128)S(1)}, f32[512,512]{0,1:T(8,128)}, f32[512,512]{0,1:T(8,128)}, /*index=5...) while((s32[]{:T(128)}, f32[256,1024]{1,0:T(8,128)S(1)}, ...), condition=%wide.region_41.42_spmd.clone.clone, body=%wide.region_24.41_spmd.clone.clone.sunk | while | flops 15417005056 | bytes 646955456 | solution.py:684
  1914.0 117.7 %conditional.8 = (bf16[512,1024]{1,0:T(8,128)(2,1)}, f32[512,1024]{1,0:T(8,128)}, f32[512,512]{0,1:T(8,128)}, f32[512,512]{0,1:T(8,128)}, f32[1024,3,512]{2,1,0:...) conditional(s32[]{:T(128)} %get-tuple-element.4737, ...), branch_computations={%region_26.27_spmd, %region_28.28_spmd, %region_29.31_spmd, %regio... | conditional | flops 15400431616 | bytes 539057088 | solution.py:597
  2042.4 64.8 %reduce-scatter.54.cloned.1.call-done = bf16[256,1024]{1,0:T(8,128)(2,1)} async-done(((bf16[512,1024]{1,0:T(8,128)(2,1)}), bf16[256,1024]{1,0:T(8,128)(2,1)}) %reduce-scatter.54.cloned.1.call-update) | async-done | bytes 524304 | tf_op jit(solution)/shard_map/while/body/eval_jaxpr/reduce_scatter | solution.py:616
  2185.6 117.5 %conditional.8 = (bf16[512,1024]{1,0:T(8,128)(2,1)}, f32[512,1024]{1,0:T(8,128)}, f32[512,512]{0,1:T(8,128)}, f32[512,512]{0,1:T(8,128)}, f32[1024,3,512]{2,1,0:...) conditional(s32[]{:T(128)} %get-tuple-element.4737, ...), branch_computations={%region_26.27_spmd, %region_28.28_spmd, %region_29.31_spmd, %regio... | conditional | flops 15400431616 | bytes 539057088 | solution.py:597
  2313.8 64.9 %reduce-scatter.54.cloned.1.call-done = bf16[256,1024]{1,0:T(8,128)(2,1)} async-done(((bf16[512,1024]{1,0:T(8,128)(2,1)}), bf16[256,1024]{1,0:T(8,128)(2,1)}) %reduce-scatter.54.cloned.1.call-update) | async-done | bytes 524304 | tf_op jit(solution)/shard_map/while/body/eval_jaxpr/reduce_scatter | solution.py:616
  2457.4 117.9 %conditional.8 = (bf16[512,1024]{1,0:T(8,128)(2,1)}, f32[512,1024]{1,0:T(8,128)}, f32[512,512]{0,1:T(8,128)}, f32[512,512]{0,1:T(8,128)}, f32[1024,3,512]{2,1,0:...) conditional(s32[]{:T(128)} %get-tuple-element.4737, ...), branch_computations={%region_26.27_spmd, %region_28.28_spmd, %region_29.31_spmd, %regio... | conditional | flops 15400431616 | bytes 539057088 | solution.py:597
  2585.9 64.7 %reduce-scatter.54.cloned.1.call-done = bf16[256,1024]{1,0:T(8,128)(2,1)} async-done(((bf16[512,1024]{1,0:T(8,128)(2,1)}), bf16[256,1024]{1,0:T(8,128)(2,1)}) %reduce-scatter.54.cloned.1.call-update) | async-done | bytes 524304 | tf_op jit(solution)/shard_map/while/body/eval_jaxpr/reduce_scatter | solution.py:616
  2729.1 116.9 %conditional.8 = (bf16[512,1024]{1,0:T(8,128)(2,1)}, f32[512,1024]{1,0:T(8,128)}, f32[512,512]{0,1:T(8,128)}, f32[512,512]{0,1:T(8,128)}, f32[1024,3,512]{2,1,0:...) conditional(s32[]{:T(128)} %get-tuple-element.4737, ...), branch_computations={%region_26.27_spmd, %region_28.28_spmd, %region_29.31_spmd, %regio... | conditional | flops 15400431616 | bytes 539057088 | solution.py:597
  2859.1 63.1 %reduce-scatter.54.cloned.1.call-done = bf16[256,1024]{1,0:T(8,128)(2,1)} async-done(((bf16[512,1024]{1,0:T(8,128)(2,1)}), bf16[256,1024]{1,0:T(8,128)(2,1)}) %reduce-scatter.54.cloned.1.call-update) | async-done | bytes 524304 | tf_op jit(solution)/shard_map/while/body/eval_jaxpr/reduce_scatter | solution.py:616
  3000.9 116.9 %conditional.8 = (bf16[512,1024]{1,0:T(8,128)(2,1)}, f32[512,1024]{1,0:T(8,128)}, f32[512,512]{0,1:T(8,128)}, f32[512,512]{0,1:T(8,128)}, f32[1024,3,512]{2,1,0:...) conditional(s32[]{:T(128)} %get-tuple-element.4737, ...), branch_computations={%region_26.27_spmd, %region_28.28_spmd, %region_29.31_spmd, %regio... | conditional | flops 15400431616 | bytes 539057088 | solution.py:597
  3130.9 63.2 %reduce-scatter.54.cloned.1.call-done = bf16[256,1024]{1,0:T(8,128)(2,1)} async-done(((bf16[512,1024]{1,0:T(8,128)(2,1)}), bf16[256,1024]{1,0:T(8,128)(2,1)}) %reduce-scatter.54.cloned.1.call-update) | async-done | bytes 524304 | tf_op jit(solution)/shard_map/while/body/eval_jaxpr/reduce_scatter | solution.py:616
  3272.4 117.2 %conditional.8 = (bf16[512,1024]{1,0:T(8,128)(2,1)}, f32[512,1024]{1,0:T(8,128)}, f32[512,512]{0,1:T(8,128)}, f32[512,512]{0,1:T(8,128)}, f32[1024,3,512]{2,1,0:...) conditional(s32[]{:T(128)} %get-tuple-element.4737, ...), branch_computations={%region_26.27_spmd, %region_28.28_spmd, %region_29.31_spmd, %regio... | conditional | flops 15400431616 | bytes 539057088 | solution.py:597
  3402.7 62.9 %reduce-scatter.54.cloned.1.call-done = bf16[256,1024]{1,0:T(8,128)(2,1)} async-done(((bf16[512,1024]{1,0:T(8,128)(2,1)}), bf16[256,1024]{1,0:T(8,128)(2,1)}) %reduce-scatter.54.cloned.1.call-update) | async-done | bytes 524304 | tf_op jit(solution)/shard_map/while/body/eval_jaxpr/reduce_scatter | solution.py:616
  3544.1 116.9 %conditional.8 = (bf16[512,1024]{1,0:T(8,128)(2,1)}, f32[512,1024]{1,0:T(8,128)}, f32[512,512]{0,1:T(8,128)}, f32[512,512]{0,1:T(8,128)}, f32[1024,3,512]{2,1,0:...) conditional(s32[]{:T(128)} %get-tuple-element.4737, ...), branch_computations={%region_26.27_spmd, %region_28.28_spmd, %region_29.31_spmd, %regio... | conditional | flops 15400431616 | bytes 539057088 | solution.py:597
  3674.1 63.1 %reduce-scatter.54.cloned.1.call-done = bf16[256,1024]{1,0:T(8,128)(2,1)} async-done(((bf16[512,1024]{1,0:T(8,128)(2,1)}), bf16[256,1024]{1,0:T(8,128)(2,1)}) %reduce-scatter.54.cloned.1.call-update) | async-done | bytes 524304 | tf_op jit(solution)/shard_map/while/body/eval_jaxpr/reduce_scatter | solution.py:616
  3815.6 116.9 %conditional.8 = (bf16[512,1024]{1,0:T(8,128)(2,1)}, f32[512,1024]{1,0:T(8,128)}, f32[512,512]{0,1:T(8,128)}, f32[512,512]{0,1:T(8,128)}, f32[1024,3,512]{2,1,0:...) conditional(s32[]{:T(128)} %get-tuple-element.4737, ...), branch_computations={%region_26.27_spmd, %region_28.28_spmd, %region_29.31_spmd, %regio... | conditional | flops 15400431616 | bytes 539057088 | solution.py:597
  3945.6 63.2 %reduce-scatter.54.cloned.1.call-done = bf16[256,1024]{1,0:T(8,128)(2,1)} async-done(((bf16[512,1024]{1,0:T(8,128)(2,1)}), bf16[256,1024]{1,0:T(8,128)(2,1)}) %reduce-scatter.54.cloned.1.call-update) | async-done | bytes 524304 | tf_op jit(solution)/shard_map/while/body/eval_jaxpr/reduce_scatter | solution.py:616
  4087.3 117.2 %conditional.8 = (bf16[512,1024]{1,0:T(8,128)(2,1)}, f32[512,1024]{1,0:T(8,128)}, f32[512,512]{0,1:T(8,128)}, f32[512,512]{0,1:T(8,128)}, f32[1024,3,512]{2,1,0:...) conditional(s32[]{:T(128)} %get-tuple-element.4737, ...), branch_computations={%region_26.27_spmd, %region_28.28_spmd, %region_29.31_spmd, %regio... | conditional | flops 15400431616 | bytes 539057088 | solution.py:597
  4217.6 62.9 %reduce-scatter.54.cloned.1.call-done = bf16[256,1024]{1,0:T(8,128)(2,1)} async-done(((bf16[512,1024]{1,0:T(8,128)(2,1)}), bf16[256,1024]{1,0:T(8,128)(2,1)}) %reduce-scatter.54.cloned.1.call-update) | async-done | bytes 524304 | tf_op jit(solution)/shard_map/while/body/eval_jaxpr/reduce_scatter | solution.py:616
  4358.9 116.9 %conditional.8 = (bf16[512,1024]{1,0:T(8,128)(2,1)}, f32[512,1024]{1,0:T(8,128)}, f32[512,512]{0,1:T(8,128)}, f32[512,512]{0,1:T(8,128)}, f32[1024,3,512]{2,1,0:...) conditional(s32[]{:T(128)} %get-tuple-element.4737, ...), branch_computations={%region_26.27_spmd, %region_28.28_spmd, %region_29.31_spmd, %regio... | conditional | flops 15400431616 | bytes 539057088 | solution.py:597
  4489.0 63.1 %reduce-scatter.54.cloned.1.call-done = bf16[256,1024]{1,0:T(8,128)(2,1)} async-done(((bf16[512,1024]{1,0:T(8,128)(2,1)}), bf16[256,1024]{1,0:T(8,128)(2,1)}) %reduce-scatter.54.cloned.1.call-update) | async-done | bytes 524304 | tf_op jit(solution)/shard_map/while/body/eval_jaxpr/reduce_scatter | solution.py:616
  4630.5 116.9 %conditional.8 = (bf16[512,1024]{1,0:T(8,128)(2,1)}, f32[512,1024]{1,0:T(8,128)}, f32[512,512]{0,1:T(8,128)}, f32[512,512]{0,1:T(8,128)}, f32[1024,3,512]{2,1,0:...) conditional(s32[]{:T(128)} %get-tuple-element.4737, ...), branch_computations={%region_26.27_spmd, %region_28.28_spmd, %region_29.31_spmd, %regio... | conditional | flops 15400431616 | bytes 539057088 | solution.py:597
  4760.5 63.2 %reduce-scatter.54.cloned.1.call-done = bf16[256,1024]{1,0:T(8,128)(2,1)} async-done(((bf16[512,1024]{1,0:T(8,128)(2,1)}), bf16[256,1024]{1,0:T(8,128)(2,1)}) %reduce-scatter.54.cloned.1.call-update) | async-done | bytes 524304 | tf_op jit(solution)/shard_map/while/body/eval_jaxpr/reduce_scatter | solution.py:616
  5091.2 47.0 reduce-scatter.32.cloned.1.call-done
  5138.3 46.9 reduce-scatter.34.cloned.1.call-done
  5185.1 47.1 reduce-scatter.46.cloned.1.call-done
  5232.3 46.8 reduce-scatter.48.cloned.1.call-done
  5334.6 45.2 reduce-scatter.24.cloned.1.call-done
  5382.5 265.0 %all-reduce.3.cloned.1.call-done = (bf16[256,3,512]{2,0,1:T(8,128)(2,1)}, bf16[512,256]{1,0:T(8,128)(2,1)}, bf16[256,2048]{1,0:T(8,128)(2,1)}, bf16[2048,256]{1,...) async-done(((bf16[256,3,512]{2,0,1:T(8,128)(2,1)}, ...) | async-done | bytes 7471120 | tf_op jit(solution)/shard_map/psum | solution.py:716
  (2489 shorter events, 4469.1 us)
Async XLA Ops:
  72.8 119.9 %reduce-scatter.50.cloned.1.call-start = ((), (), s32[]{:S(2)}) async-start(), calls=%async_computation.37 | async-start | bytes 1572864 | tf_op jit(solution)/shard_map/while/body/eval_jaxpr/reduce_scatter | solution.py:495
  234.3 118.6 %reduce-scatter.50.cloned.1.call-start = ((), (), s32[]{:S(2)}) async-start(), calls=%async_computation.37 | async-start | bytes 1572864 | tf_op jit(solution)/shard_map/while/body/eval_jaxpr/reduce_scatter | solution.py:495
  554.8 118.4 %reduce-scatter.50.cloned.1.call-start = ((), (), s32[]{:S(2)}) async-start(), calls=%async_computation.37 | async-start | bytes 1572864 | tf_op jit(solution)/shard_map/while/body/eval_jaxpr/reduce_scatter | solution.py:495
  875.3 118.8 %reduce-scatter.50.cloned.1.call-start = ((), (), s32[]{:S(2)}) async-start(), calls=%async_computation.37 | async-start | bytes 1572864 | tf_op jit(solution)/shard_map/while/body/eval_jaxpr/reduce_scatter | solution.py:495
  1035.7 118.5 %reduce-scatter.50.cloned.1.call-start = ((), (), s32[]{:S(2)}) async-start(), calls=%async_computation.37 | async-start | bytes 1572864 | tf_op jit(solution)/shard_map/while/body/eval_jaxpr/reduce_scatter | solution.py:495
  1196.0 118.6 %reduce-scatter.50.cloned.1.call-start = ((), (), s32[]{:S(2)}) async-start(), calls=%async_computation.37 | async-start | bytes 1572864 | tf_op jit(solution)/shard_map/while/body/eval_jaxpr/reduce_scatter | solution.py:495
  1356.3 118.5 %reduce-scatter.50.cloned.1.call-start = ((), (), s32[]{:S(2)}) async-start(), calls=%async_computation.37 | async-start | bytes 1572864 | tf_op jit(solution)/shard_map/while/body/eval_jaxpr/reduce_scatter | solution.py:495
  1516.4 119.1 %reduce-scatter.50.cloned.1.call-start = ((), (), s32[]{:S(2)}) async-start(), calls=%async_computation.37 | async-start | bytes 1572864 | tf_op jit(solution)/shard_map/while/body/eval_jaxpr/reduce_scatter | solution.py:495
  1677.3 118.7 %reduce-scatter.50.cloned.1.call-start = ((), (), s32[]{:S(2)}) async-start(), calls=%async_computation.37 | async-start | bytes 1572864 | tf_op jit(solution)/shard_map/while/body/eval_jaxpr/reduce_scatter | solution.py:495
  1869.8 237.4 %reduce-scatter.54.cloned.1.call-start = ((), (), s32[]{:S(2)}) async-start(), calls=%async_computation.41 | async-start | bytes 1572864 | tf_op jit(solution)/shard_map/while/body/eval_jaxpr/reduce_scatter | solution.py:616
  2141.9 236.8 %reduce-scatter.54.cloned.1.call-start = ((), (), s32[]{:S(2)}) async-start(), calls=%async_computation.41 | async-start | bytes 1572864 | tf_op jit(solution)/shard_map/while/body/eval_jaxpr/reduce_scatter | solution.py:616
  2413.4 237.2 %reduce-scatter.54.cloned.1.call-start = ((), (), s32[]{:S(2)}) async-start(), calls=%async_computation.41 | async-start | bytes 1572864 | tf_op jit(solution)/shard_map/while/body/eval_jaxpr/reduce_scatter | solution.py:616
  2685.2 237.1 %reduce-scatter.54.cloned.1.call-start = ((), (), s32[]{:S(2)}) async-start(), calls=%async_computation.41 | async-start | bytes 1572864 | tf_op jit(solution)/shard_map/while/body/eval_jaxpr/reduce_scatter | solution.py:616
  2957.1 237.0 %reduce-scatter.54.cloned.1.call-start = ((), (), s32[]{:S(2)}) async-start(), calls=%async_computation.41 | async-start | bytes 1572864 | tf_op jit(solution)/shard_map/while/body/eval_jaxpr/reduce_scatter | solution.py:616
  3228.6 237.0 %reduce-scatter.54.cloned.1.call-start = ((), (), s32[]{:S(2)}) async-start(), calls=%async_computation.41 | async-start | bytes 1572864 | tf_op jit(solution)/shard_map/while/body/eval_jaxpr/reduce_scatter | solution.py:616
  3500.2 237.1 %reduce-scatter.54.cloned.1.call-start = ((), (), s32[]{:S(2)}) async-start(), calls=%async_computation.41 | async-start | bytes 1572864 | tf_op jit(solution)/shard_map/while/body/eval_jaxpr/reduce_scatter | solution.py:616
  3772.0 236.8 %reduce-scatter.54.cloned.1.call-start = ((), (), s32[]{:S(2)}) async-start(), calls=%async_computation.41 | async-start | bytes 1572864 | tf_op jit(solution)/shard_map/while/body/eval_jaxpr/reduce_scatter | solution.py:616
  4043.3 237.1 %reduce-scatter.54.cloned.1.call-start = ((), (), s32[]{:S(2)}) async-start(), calls=%async_computation.41 | async-start | bytes 1572864 | tf_op jit(solution)/shard_map/while/body/eval_jaxpr/reduce_scatter | solution.py:616
  4315.0 237.1 %reduce-scatter.54.cloned.1.call-start = ((), (), s32[]{:S(2)}) async-start(), calls=%async_computation.41 | async-start | bytes 1572864 | tf_op jit(solution)/shard_map/while/body/eval_jaxpr/reduce_scatter | solution.py:616
  4586.8 236.8 %reduce-scatter.54.cloned.1.call-start = ((), (), s32[]{:S(2)}) async-start(), calls=%async_computation.41 | async-start | bytes 1572864 | tf_op jit(solution)/shard_map/while/body/eval_jaxpr/reduce_scatter | solution.py:616
  4870.2 140.2 %reduce-scatter.28.cloned.1.call-start = ((), (), s32[]{:S(2)}) async-start(), calls=%async_computation.23 | async-start | bytes 3932160 | tf_op jit(solution)/shard_map/reduce_scatter | solution.py:730
  4877.2 173.8 %reduce-scatter.36.cloned.1.call-start = ((), (), s32[]{:S(2)}) async-start(), calls=%async_computation.27 | async-start | bytes 3932160 | tf_op jit(solution)/shard_map/reduce_scatter | solution.py:742
  4882.8 208.4 %reduce-scatter.38.cloned.1.call-start = ((), (), s32[]{:S(2)}) async-start(), calls=%async_computation.28 | async-start | bytes 3932160 | tf_op jit(solution)/shard_map/reduce_scatter | solution.py:745
  4887.8 250.5 %reduce-scatter.32.cloned.1.call-start = ((), (), s32[]{:S(2)}) async-start(), calls=%async_computation.25 | async-start | bytes 5242880 | tf_op jit(solution)/shard_map/reduce_scatter | solution.py:736
  4893.9 291.3 %reduce-scatter.34.cloned.1.call-start = ((), (), s32[]{:S(2)}) async-start(), calls=%async_computation.26 | async-start | bytes 5242880 | tf_op jit(solution)/shard_map/reduce_scatter | solution.py:739
  4900.3 332.0 %reduce-scatter.46.cloned.1.call-start = ((), (), s32[]{:S(2)}) async-start(), calls=%async_computation.32 | async-start | bytes 5242880 | tf_op jit(solution)/shard_map/reduce_scatter | solution.py:754
  4906.4 372.7 %reduce-scatter.48.cloned.1.call-start = ((), (), s32[]{:S(2)}) async-start(), calls=%async_computation.33 | async-start | bytes 5242880 | tf_op jit(solution)/shard_map/reduce_scatter | solution.py:757
  4912.5 389.0 %reduce-scatter.26.cloned.1.call-start = ((), (), s32[]{:S(2)}) async-start(), calls=%async_computation.22 | async-start | bytes 20480 | tf_op jit(solution)/shard_map/reduce_scatter | solution.py:763
  4950.0 382.7 %reduce-scatter.22.cloned.1.call-start = ((), (), s32[]{:S(2)}) async-start(), calls=%async_computation.20 | async-start | bytes 1966080 | tf_op jit(solution)/shard_map/reduce_scatter | solution.py:699
  4951.9 427.9 %reduce-scatter.24.cloned.1.call-start = ((), (), s32[]{:S(2)}) async-start(), calls=%async_computation.21 | async-start | bytes 5242880 | tf_op jit(solution)/shard_map/reduce_scatter | solution.py:696
  4957.8 689.7 %all-reduce.3.cloned.1.call-start = ((), (), s32[]{:S(2)}) async-start(), calls=%async_computation.34 | async-start | bytes 14942208 | tf_op jit(solution)/shard_map/psum | solution.py:716
  5279.1 414.7 %reduce-scatter.20.cloned.1.call-start = ((), (), s32[]{:S(2)}) async-start(), calls=%async_computation.19 | async-start | bytes 5242880 | tf_op jit(solution)/shard_map/reduce_scatter | solution.py:693
  (526 other events, 9947.5 us)
Sparse Core Ops, SparseCore 0:
  66.1 23.9 all-gather.4
  159.3 33.3 reduce-scatter.49
  228.8 21.5 all-gather.4
  319.6 33.1 reduce-scatter.49
  468.3 44.7 reduce-scatter.49
  549.3 21.6 all-gather.4
  624.1 49.0 reduce-scatter.49
  709.2 21.9 all-gather.4
  784.4 49.3 reduce-scatter.49
  869.7 21.6 all-gather.4
  944.8 49.2 reduce-scatter.49
  1030.1 21.5 all-gather.4
  1104.9 49.2 reduce-scatter.49
  1190.4 21.5 all-gather.4
  1265.2 49.2 reduce-scatter.49
  1350.8 21.5 all-gather.4
  1425.8 49.0 reduce-scatter.49
  1510.9 21.8 all-gather.4
  1586.2 49.2 reduce-scatter.49
  1746.7 49.2 reduce-scatter.49
  1868.9 21.6 all-gather.8
  2031.9 75.2 reduce-scatter.53
  2303.3 75.3 reduce-scatter.53
  2575.4 75.1 reduce-scatter.53
  2846.2 76.0 reduce-scatter.53
  3118.0 76.0 reduce-scatter.53
  3389.8 75.7 reduce-scatter.53
  3661.2 76.0 reduce-scatter.53
  3932.7 76.0 reduce-scatter.53
  4204.7 75.7 reduce-scatter.53
  4476.0 76.0 reduce-scatter.53
  4747.5 76.0 reduce-scatter.53
  (56 shorter events, 1167.1 us)
Sparse Core Ops, SparseCore 1:
  4864.6 21.5 reduce-scatter.43
  4889.2 24.8 reduce-scatter.29
  4917.0 24.8 reduce-scatter.39
  4945.2 24.8 reduce-scatter.41
  4972.5 37.8 reduce-scatter.27
  5013.1 37.8 reduce-scatter.35
  5053.4 37.8 reduce-scatter.37
  5093.8 44.4 reduce-scatter.31
  5140.7 44.4 reduce-scatter.33
  5187.8 44.4 reduce-scatter.45
  5234.7 44.4 reduce-scatter.47
  5282.2 19.3 reduce-scatter.25
  5304.5 28.1 reduce-scatter.21
  5335.4 44.4 reduce-scatter.23
  5383.1 264.3 all-reduce.2
  5650.6 43.2 reduce-scatter.19
where the time goes:
time: 5730 us; the launch traced here: 5700 us
  waiting for transfers between devices  2680 us (47%)
  local copies, waits for them, and re-layouts  1150 us (20%)
  other arithmetic  863 us (15%)
  matrix products  620 us (11%)
  loops' own time  290 us (5%)
    reduce_scatter x11, waiting for transfers between devices, backward_tick(): lax.psum_scatter(grad_normed_tok.astype(jnp.bfloat16), 'tensor', scatter_...  699 us
    another operation x108, local copies, waits for them, and re-layouts  384 us
    psum x1, waiting for transfers between devices, body(): lax.psum(grad_qkv_a.astype(jnp.bfloat16), 'dp').astype(jnp.float32)  265 us
    all_gather x11, waiting for transfers between devices, forward_tick(): lax.all_gather(state_normed_shard, 'tensor', axis=0, tiled=True)  258 us
    all_gather x11, waiting for transfers between devices, backward_tick(): lax.all_gather(update_grad.astype(jnp.bfloat16), 'tensor', axis=0, tiled=...  258 us
    dynamic_slice x121, local copies, waits for them, and re-layouts, place_row(): previous = lax.dynamic_index_in_dim(store, position, 0, False)  236 us
    dynamic_update_slice x88, other arithmetic, place_row(): lax.dynamic_update_index_in_dim(store, jnp.where(active_tick, value, prev...  229 us
    another operation x11, loops' own time, backward_tick(): lax.switch(section_index, backward_branches, grad_tok, grad_st, tok_norme...  195 us
  transfers between devices with their start and end apart: 126, of which 100 were waited for; matrix products, arithmetic and copies ran while one was open for 18% of the time, Pallas kernels for 0%

commit v1 on v0

--- a/solution.py
+++ b/solution.py
@@ -1,8 +1,11 @@
+import functools
 import math
 
 import jax
 import jax.numpy as jnp
 from jax import lax
+from jax.experimental import pallas as pl
+from jax.experimental.pallas import tpu as pltpu
 from jax.sharding import PartitionSpec as P
 
 HEAD_DIM = 128
@@ -120,7 +123,7 @@
     )
 
 
-def body(
+def relay_body(
     layer_input,
     output_grad,
     seg_blocks,
@@ -789,6 +792,762 @@
     )
 
 
+CHAIN = 4
+SCALE = 1.0 / math.sqrt(HEAD_DIM)
+ALL_AXES = ("section", "dp", "tensor")
+GROUP = ("section", "tensor")
+VMEM_BYTES = 56 * 1024 * 1024
+
+
+def block_of(section, tensor):
+    high = section // 2
+    return 2 * (2 * high + (tensor ^ high)) + section % 2
+
+
+DEVICE_OF_BLOCK = [0] * 8
+for _section in range(4):
+    for _tensor in range(2):
+        DEVICE_OF_BLOCK[block_of(_section, _tensor)] = 2 * _section + _tensor
+TO_NEXT = [(DEVICE_OF_BLOCK[b], DEVICE_OF_BLOCK[b + 1]) for b in range(7)]
+TO_PRIOR = [(there, here) for here, there in TO_NEXT]
+SWAP = [(0, 1), (1, 0)]
+
+
+def params(**extra):
+    return pltpu.CompilerParams(vmem_limit_bytes=VMEM_BYTES, **extra)
+
+
+def nt(a, b):
+    return lax.dot_general(a, b, (((1,), (1,)), ((), ())), preferred_element_type=jnp.float32)
+
+
+def nn(a, b):
+    return lax.dot_general(a, b, (((1,), (0,)), ((), ())), preferred_element_type=jnp.float32)
+
+
+def tn(a, b):
+    return lax.dot_general(a, b, (((0,), (0,)), ((), ())), preferred_element_type=jnp.float32)
+
+
+def bf(a):
+    return a.astype(jnp.bfloat16)
+
+
+def later_mask(rows):
+    return lax.broadcasted_iota(jnp.int32, (rows, rows), 1) > lax.broadcasted_iota(
+        jnp.int32, (rows, rows), 0
+    )
+
+
+def attend_kernel(with_states, *refs):
+    if with_states:
+        open_ref, q, k, v, pk, pv, sk, sv, out, lse = refs
+    else:
+        open_ref, q, k, v, pk, pv, out, lse = refs
+    later = later_mask(q.shape[0])
+    query = q[...]
+    prior = jnp.where(open_ref[0] > 0, NEGATIVE, nt(query, pk[...]))
+    scores = jnp.where(later, prior, nt(query, k[...])) * SCALE
+    top = jnp.max(scores, axis=-1, keepdims=True)
+    if with_states:
+        more = nt(query, sk[...]) * SCALE
+        top = jnp.maximum(top, jnp.max(more, axis=-1, keepdims=True))
+    weights = jnp.exp(scores - top)
+    total = jnp.sum(weights, axis=-1, keepdims=True)
+    if with_states:
+        more_weights = jnp.exp(more - top)
+        total = total + jnp.sum(more_weights, axis=-1, keepdims=True)
+    share = 1.0 / total
+    weights = weights * share
+    mixed = nn(bf(jnp.where(later, weights, 0.0)), pv[...]) + nn(
+        bf(jnp.where(later, 0.0, weights)), v[...]
+    )
+    if with_states:
+        mixed = mixed + nn(bf(more_weights * share), sv[...])
+    out[...] = bf(mixed)
+    lse[0] = top + jnp.log(total)
+
+
+def head_block(rows, offset):
+    return pl.BlockSpec((rows, HEAD_DIM), lambda h: (0, offset + h))
+
+
+def attend(opening, proj, prior, states=None):
+    rows, width = proj.shape[0], proj.shape[1] // 3
+    heads = width // HEAD_DIM
+    specs = [pl.BlockSpec(memory_space=pltpu.SMEM)]
+    specs += [head_block(rows, i * heads) for i in range(3)]
+    specs += [head_block(rows, i * heads) for i in range(2)]
+    args = [opening, proj, proj, proj, prior, prior]
+    keys = 2 * rows
+    if states is not None:
+        specs += [head_block(states.shape[0], i * heads) for i in (1, 2)]
+        args += [states, states]
+        keys += states.shape[0]
+    return pl.pallas_call(
+        functools.partial(attend_kernel, states is not None),
+        grid=(heads,),
+        in_specs=specs,
+        out_specs=[
+            head_block(rows, 0),
+            pl.BlockSpec((1, rows, 1), lambda h: (h, 0, 0)),
+        ],
+        out_shape=[
+            jax.ShapeDtypeStruct((rows, width), jnp.bfloat16),
+            jax.ShapeDtypeStruct((heads, rows, 1), jnp.float32),
+        ],
+        compiler_params=params(),
+        cost_estimate=pl.CostEstimate(
+            flops=4 * rows * keys * width,
+            bytes_accessed=2 * rows * width * 8,
+            transcendentals=rows * keys * heads // 2,
+        ),
+        name="attend",
+    )(*args)
+
+
+def attend_back_kernel(with_states, *refs):
+    if with_states:
+        (open_ref, q, k, v, pk, pv, sk, sv, gmix, lse) = refs[:10]
+        (gq, gk, gv, gpk, gpv, gsk, gsv) = refs[10:]
+    else:
+        (open_ref, q, k, v, pk, pv, gmix, lse) = refs[:8]
+        (gq, gk, gv, gpk, gpv) = refs[8:]
+    later = later_mask(q.shape[0])
+    query, grad, log_total = q[...], gmix[...], lse[0]
+    prior = jnp.where(open_ref[0] > 0, NEGATIVE, nt(query, pk[...]))
+    scores = jnp.where(later, prior, nt(query, k[...])) * SCALE
+    weights = jnp.exp(scores - log_total)
+    grad_weights = jnp.where(later, nt(grad, pv[...]), nt(grad, v[...]))
+    inner = jnp.sum(weights * grad_weights, axis=-1, keepdims=True)
+    if with_states:
+        more_weights = jnp.exp(nt(query, sk[...]) * SCALE - log_total)
+        more_grad = nt(grad, sv[...])
+        inner = inner + jnp.sum(more_weights * more_grad, axis=-1, keepdims=True)
+    gpv[...] = tn(bf(jnp.where(later, weights, 0.0)), grad).astype(gpv.dtype)
+    gv[...] = tn(bf(jnp.where(later, 0.0, weights)), grad)
+    grad_scores = weights * (grad_weights - inner)
+    from_prior = bf(jnp.where(later, grad_scores, 0.0))
+    from_own = bf(jnp.where(later, 0.0, grad_scores))
+    grad_query = nn(from_prior, pk[...]) + nn(from_own, k[...])
+    gpk[...] = (tn(from_prior, query) * SCALE).astype(gpk.dtype)
+    gk[...] = tn(from_own, query) * SCALE
+    if with_states:
+        from_states = bf(more_weights * (more_grad - inner))
+        gsv[...] = tn(bf(more_weights), grad)
+        gsk[...] = tn(from_states, query) * SCALE
+        grad_query = grad_query + nn(from_states, sk[...])
+    gq[...] = bf(grad_query * SCALE)
+
+
+def attend_back(opening, proj, prior, grad_mixed, lse, states=None):
+    rows, width = proj.shape[0], proj.shape[1] // 3
+    heads = width // HEAD_DIM
+    specs = [pl.BlockSpec(memory_space=pltpu.SMEM)]
+    specs += [head_block(rows, i * heads) for i in range(3)]
+    specs += [head_block(rows, i * heads) for i in range(2)]
+    args = [opening, proj, proj, proj, prior, prior]
+    keys = 2 * rows
+    if states is not None:
+        specs += [head_block(states.shape[0], i * heads) for i in (1, 2)]
+        args += [states, states]
+        keys += states.shape[0]
+    specs += [head_block(rows, 0), pl.BlockSpec((1, rows, 1), lambda h: (h, 0, 0))]
+    args += [grad_mixed, lse]
+    kinds = [jnp.bfloat16, jnp.float32, jnp.float32, jnp.bfloat16, jnp.bfloat16]
+    if states is not None:
+        kinds += [jnp.float32, jnp.float32]
+    return pl.pallas_call(
+        functools.partial(attend_back_kernel, states is not None),
+        grid=(heads,),
+        in_specs=specs,
+        out_specs=[head_block(rows, 0) for _ in kinds],
+        out_shape=[jax.ShapeDtypeStruct((rows, width), kind) for kind in kinds],
+        compiler_params=params(),
+        cost_estimate=pl.CostEstimate(
+            flops=10 * rows * keys * width,
+            bytes_accessed=2 * rows * width * 24,
+            transcendentals=rows * keys * heads // 2,
+        ),
+        name="attend_back",
+    )(*args)
+
+
+def state_step_kernel(
+    state, gain, keep, own, other, own_v, other_v, sqkv, sout,
+    hs, proj, mixed, lse, update, fresh, hidden, mix_store,
+):
+    h = pl.program_id(0)
+    heads = pl.num_programs(0)
+    half = heads // 2
+
+    @pl.when(h == 0)
+    def _():
+        value = state[...]
+        hidden[...] = bf(value * inverse_rms(value) * gain[...])
+        hs[...] = hidden[...]
+
+    first = h < half
+    key = jnp.where(first, own[...], other[...])
+    val = jnp.where(first, own_v[...], other_v[...])
+    qkv = bf(nn(hidden[...], sqkv[0]))
+    sq, sk, sv = (qkv[:, i * HEAD_DIM : (i + 1) * HEAD_DIM] for i in range(3))
+    proj[0, 0], proj[0, 1], proj[0, 2] = sq, sk, sv
+    score_tok = nt(sq, key) * SCALE
+    score_st = nt(sq, sk) * SCALE
+    top = jnp.maximum(
+        jnp.max(score_tok, axis=-1, keepdims=True), jnp.max(score_st, axis=-1, keepdims=True)
+    )
+    p_tok = jnp.exp(score_tok - top)
+    p_st = jnp.exp(score_st - top)
+    total = jnp.sum(p_tok, axis=-1, keepdims=True) + jnp.sum(p_st, axis=-1, keepdims=True)
+    share = 1.0 / total
+    mix = bf(nn(bf(p_tok * share), val) + nn(bf(p_st * share), sv))
+    mixed[0] = mix
+    mix_store[h] = mix
+    lse[0] = top + jnp.log(total)
+
+    @pl.when(h == heads - 1)
+    def _():
+        term = jnp.zeros(state.shape, jnp.float32)
+        for i in range(mix_store.shape[0]):
+            term = term + nn(mix_store[i], sout[i])
+        update[...] = term
+        fresh[...] = keep[...] * state[...] + (1.0 - keep[...]) * term
+
+
+def half_block(rows, offset, half, second):
+    if second:
+        return pl.BlockSpec((rows, HEAD_DIM), lambda h: (0, offset + jnp.maximum(h - half, 0)))
+    return pl.BlockSpec((rows, HEAD_DIM), lambda h: (0, offset + jnp.minimum(h, half - 1)))
+
+
+def whole(shape):
+    return pl.BlockSpec(shape, lambda h: (0,) * len(shape))
+
+
+def per_head(half, rows):
+    return pl.BlockSpec((1, 3, rows, HEAD_DIM), lambda h: (h // half, 0, 0, h % half))
+
+
+def state_step(state, gain, keep, own, other, sqkv, sout):
+    count, width = state.shape
+    rows = own.shape[0]
+    heads = sqkv.shape[0]
+    half = heads // 2
+    return pl.pallas_call(
+        state_step_kernel,
+        grid=(heads,),
+        in_specs=[
+            whole((count, width)),
+            whole((1, width)),
+            whole((1, width)),
+            half_block(rows, half, half, False),
+            half_block(rows, half, half, True),
+            half_block(rows, 2 * half, half, False),
+            half_block(rows, 2 * half, half, True),
+            pl.BlockSpec((1, width, 3 * HEAD_DIM), lambda h: (h, 0, 0)),
+            whole(sout.shape),
+        ],
+        out_specs=[
+            whole((count, width)),
+            per_head(half, count),
+            pl.BlockSpec((1, count, HEAD_DIM), lambda h: (h // half, 0, h % half)),
+            pl.BlockSpec((1, count, 1), lambda h: (h, 0, 0)),
+            whole((count, width)),
+            whole((count, width)),
+        ],
+        out_shape=[
+            jax.ShapeDtypeStruct((count, width), jnp.bfloat16),
+            jax.ShapeDtypeStruct((2, 3, count, width // 2), jnp.bfloat16),
+            jax.ShapeDtypeStruct((2, count, width // 2), jnp.bfloat16),
+            jax.ShapeDtypeStruct((heads, count, 1), jnp.float32),
+            jax.ShapeDtypeStruct((count, width), jnp.float32),
+            jax.ShapeDtypeStruct((count, width), jnp.float32),
+        ],
+        scratch_shapes=[
+            pltpu.VMEM((count, width), jnp.bfloat16),
+            pltpu.VMEM((heads, count, HEAD_DIM), jnp.bfloat16),
+        ],
+        compiler_params=params(),
+        cost_estimate=pl.CostEstimate(
+            flops=count * width * (8 * width + 8 * count),
+            bytes_accessed=20 * 1024 * 1024,
+            transcendentals=count * count * 2 * heads,
+        ),
+        name="state_step",
+    )(state, gain, keep, own, other, own, other, sqkv, sout)
+
+
+def state_back_kernel(
+    grad_new, state, update, gain, keep, hs_unused, proj, lse, own, other, own_v, other_v,
+    tok_k0, tok_k1, tok_v0, tok_v1, sqkv, sout,
+    grad_in, gproj, gtok, gup, small, grad_hidden, gup_store,
+):
+    h = pl.program_id(0)
+    heads = pl.num_programs(0)
+    half = heads // 2
+
+    @pl.when(h == 0)
+    def _():
+        gup_store[...] = bf((1.0 - keep[...]) * grad_new[...])
+        gup[...] = gup_store[...]
+        grad_hidden[...] = jnp.zeros_like(grad_hidden)
+
+    first = h < half
+    key = jnp.where(first, own[...], other[...])
+    val = jnp.where(first, own_v[...], other_v[...])
+    grad = bf(nt(gup_store[...], sout[h]))
+    sq, sk, sv = proj[0, 0], proj[0, 1], proj[0, 2]
+    log_total = lse[0]
+    p_tok = jnp.exp(nt(sq, key) * SCALE - log_total)
+    p_st = jnp.exp(nt(sq, sk) * SCALE - log_total)
+    d_tok = nt(grad, val)
+    d_st = nt(grad, sv)
+    inner = jnp.sum(p_tok * d_tok, axis=-1, keepdims=True) + jnp.sum(
+        p_st * d_st, axis=-1, keepdims=True
+    )
+    s_tok = bf(p_tok * (d_tok - inner))
+    s_st = bf(p_st * (d_st - inner))
+    gtok[0, 1] = tn(bf(p_tok), grad)
+    gtok[0, 0] = tn(s_tok, sq) * SCALE
+    gsv = tn(bf(p_st), grad) + jnp.where(first, tok_v0[...], tok_v1[...])
+    gsk = tn(s_st, sq) * SCALE + jnp.where(first, tok_k0[...], tok_k1[...])
+    gsq = (nn(s_tok, key) + nn(s_st, sk)) * SCALE
+    gqkv = jnp.concatenate([bf(gsq), bf(gsk), bf(gsv)], axis=1)
+    for i in range(3):
+        gproj[0, i] = gqkv[:, i * HEAD_DIM : (i + 1) * HEAD_DIM]
+    grad_hidden[...] += nt(gqkv, sqkv[0])
+
+    @pl.when(h == heads - 1)
+    def _():
+        value, back, new = state[...], grad_hidden[...], grad_new[...]
+        factor = inverse_rms(value)
+        scaled = value * factor
+        through = back * gain[...]
+        grad_in[...] = keep[...] * new + factor * (
+            through - scaled * jnp.mean(through * scaled, axis=-1, keepdims=True)
+        )
+        small[0:1, :] = jnp.sum(back * scaled, axis=0, keepdims=True)
+        small[1:2, :] = jnp.sum(new * (value - update[...]), axis=0, keepdims=True) * (
+            keep[...] * (1.0 - keep[...])
+        )
+
+
+def state_back(
+    grad_new, state, update, gain, keep, hs, proj, lse, own, other,
+    tok_k0, tok_v0, tok_k1, tok_v1, sqkv, sout,
+):
+    count, width = state.shape
+    rows = own.shape[0]
+    heads = sqkv.shape[0]
+    half = heads // 2
+    return pl.pallas_call(
+        state_back_kernel,
+        grid=(heads,),
+        in_specs=[
+            whole((count, width)),
+            whole((count, width)),
+            whole((count, width)),
+            whole((1, width)),
+            whole((1, width)),
+            pl.BlockSpec(memory_space=pl.ANY),
+            per_head(half, count),
+            pl.BlockSpec((1, count, 1), lambda h: (h, 0, 0)),
+            half_block(rows, half, half, False),
+            half_block(rows, half, half, True),
+            half_block(rows, 2 * half, half, False),
+            half_block(rows, 2 * half, half, True),
+            half_block(count, 0, half, False),
+            half_block(count, 0, half, True),
+            half_block(count, 0, half, False),
+            half_block(count, 0, half, True),
+            pl.BlockSpec((1, width, 3 * HEAD_DIM), lambda h: (h, 0, 0)),
+            whole(sout.shape),
+        ],
+        out_specs=[
+            whole((count, width)),
+            per_head(half, count),
+            pl.BlockSpec((1, 2, rows, HEAD_DIM), lambda h: (h // half, 0, 0, h % half)),
+            whole((count, width)),
+            whole((2, width)),
+        ],
+        out_shape=[
+            jax.ShapeDtypeStruct((count, width), jnp.float32),
+            jax.ShapeDtypeStruct((2, 3, count, width // 2), jnp.bfloat16),
+            jax.ShapeDtypeStruct((2, 2, rows, width // 2), jnp.float32),
+            jax.ShapeDtypeStruct((count, width), jnp.bfloat16),
+            jax.ShapeDtypeStruct((2, width), jnp.float32),
+        ],
+        scratch_shapes=[
+            pltpu.VMEM((count, width), jnp.float32),
+            pltpu.VMEM((count, width), jnp.bfloat16),
+        ],
+        compiler_params=params(),
+        cost_estimate=pl.CostEstimate(
+            flops=count * width * (16 * width + 20 * count),
+            bytes_accessed=34 * 1024 * 1024,
+            transcendentals=count * count * 2 * heads,
+        ),
+        name="state_back",
+    )(
+        grad_new, state, update, gain, keep, hs, proj, lse, own, other, own, other,
+        tok_k0, tok_k1, tok_v0, tok_v1, sqkv, sout,
+    )
+
+
+def by_rows_kernel(place, buffer, a, g, out):
+    product = bf(tn(a[...], g[0]))
+    for i in range(product.shape[1] // 256):
+        out[0, 0, i] = product[:, i * 256 : (i + 1) * 256]
+
+
+def by_columns_kernel(place, buffer, a, g, out):
+    product = bf(tn(a[...], g[...]))
+    for i in range(product.shape[0] // 256):
+        out[0, 0, i] = product[i * 256 : (i + 1) * 256]
+
+
+def weight_grad(buffer, place, a, g, tile, by_rows):
+    rows = a.shape[0]
+    sections = buffer.shape[0]
+    if by_rows:
+        parts, width = g.shape[0], g.shape[2]
+        wide = min(width, 1024)
+        steps = width // wide
+        tiles = wide // 256
+        grid = (sections, parts * steps)
+        a_spec = pl.BlockSpec((rows, a.shape[1] // sections), lambda s, n, place: (0, s))
+        g_spec = pl.BlockSpec((1, rows, wide), lambda s, n, place: (n // steps, 0, n % steps))
+        kernel = by_rows_kernel
+    else:
+        wide = min(a.shape[1], 1024)
+        tiles = wide // 256
+        grid = (sections, a.shape[1] // wide)
+        a_spec = pl.BlockSpec((rows, wide), lambda s, n, place: (0, n))
+        g_spec = pl.BlockSpec((rows, g.shape[1] // sections), lambda s, n, place: (0, s))
+        kernel = by_columns_kernel
+    start = tile // tiles
+    size = grid[0] * grid[1] * tiles * 256 * 256
+    return pl.pallas_call(
+        kernel,
+        grid_spec=pltpu.PrefetchScalarGridSpec(
+            num_scalar_prefetch=1,
+            grid=grid,
+            in_specs=[pl.BlockSpec(memory_space=pl.ANY), a_spec, g_spec],
+            out_specs=pl.BlockSpec(
+                (1, 1, tiles, 256, 256), lambda s, n, place: (s, place[0], start + n, 0, 0)
+            ),
+        ),
+        out_shape=jax.ShapeDtypeStruct(buffer.shape, buffer.dtype),
+        input_output_aliases={1: 0},
+        compiler_params=params(),
+        cost_estimate=pl.CostEstimate(
+            flops=2 * rows * size, bytes_accessed=2 * size, transcendentals=0
+        ),
+        name="weight_grad",
+    )(place, buffer, a, g)
+
+
+def gelu_back(values, grad):
+    return jax.vjp(smooth, values)[1](grad)[0]
+
+
+def block_body(
+    layer_input, output_grad, seg_blocks, seg_group, gain_a, wqkv_a, wout_a, gain_b, up_b, down_b,
+    gain_c, gain_s, wqkv_c, sqkv_c, wout_c, sout_c, gate_bias, init_states, gain_d, up_d, down_d,
+):
+    sections, tensors = lax.axis_size("section"), lax.axis_size("tensor")
+    block_count, shard_rows, width = layer_input.shape[1:]
+    rows = shard_rows * tensors
+    section, tensor = lax.axis_index("section"), lax.axis_index("tensor")
+    block = block_of(section, tensor)
+    begins, closes, lively, numbers = layout(
+        seg_blocks, seg_group, lax.axis_index("dp"), block_count
+    )
+    alive = lively[block]
+    starts = begins[block] | jnp.logical_not(alive)
+    ends = closes[block] | jnp.logical_not(alive)
+    opening = starts.astype(jnp.int32)[None]
+    own_place = tensor[None]
+    other_place = 1 - own_place
+    f32 = jnp.float32
+    gains = {k: v.astype(f32) for k, v in dict(a=gain_a, b=gain_b, c=gain_c, d=gain_d).items()}
+
+    def in_order(own, other):
+        low = jnp.where(tensor == 0, own, other)
+        high = jnp.where(tensor == 0, other, own)
+        return low, high
+
+    partner = block_of(section, 1 - tensor)
+
+    def whole_block(stack, mine, theirs):
+        own = lax.dynamic_index_in_dim(stack[0], mine, 0, False)
+        other = lax.ppermute(lax.dynamic_index_in_dim(stack[0], theirs, 0, False), "tensor", SWAP)
+        return jnp.concatenate(in_order(own, other), axis=0)
+
+    def other_half(weight):
+        size = weight.shape[0] // sections
+        piece = lax.dynamic_slice_in_dim(weight, section * size, size, 0)
+        return lax.all_gather(lax.ppermute(piece, "tensor", SWAP), "section", axis=0, tiled=True)
+
+    def flat(weight):
+        return weight.reshape(weight.shape[0], -1)
+
+    tokens = whole_block(layer_input, block, partner)
+    before = whole_block(layer_input, jnp.maximum(block - 1, 0), jnp.maximum(partner - 1, 0))
+    wqkv_a0 = flat(wqkv_a)
+    wqkv_a1 = other_half(wqkv_a0)
+    wout_a1 = other_half(wout_a)
+    up_b1, down_b1 = other_half(up_b), other_half(down_b)
+    wqkv_c0, sqkv_c0 = flat(wqkv_c), flat(sqkv_c)
+    wqkv_c1, sqkv_c1 = other_half(wqkv_c0), other_half(sqkv_c0)
+    sout_c1 = other_half(sout_c)
+    wout_c1 = other_half(wout_c)
+    up_d1, down_d1 = other_half(up_d), other_half(down_d)
+    cotangent = whole_block(output_grad, block, partner)
+    initial = jnp.concatenate(
+        in_order(init_states, lax.ppermute(init_states, "tensor", SWAP)), axis=0
+    ).astype(f32)
+
+    def normed(values, gain):
+        return bf(values * inverse_rms(values) * gain)
+
+    def dot(a, b):
+        return jnp.dot(a, b, preferred_element_type=f32)
+
+    def dot_t(a, b):
+        return lax.dot_general(a, b, (((1,), (1,)), ((), ())), preferred_element_type=f32)
+
+    half = wout_a.shape[0]
+    r0 = tokens.astype(f32)
+    h0 = normed(r0, gains["a"])
+    h_before = normed(before.astype(f32), gains["a"])
+    pa0, pa1 = bf(dot(h0, wqkv_a0)), bf(dot(h0, wqkv_a1))
+    prior_a0 = bf(dot(h_before, wqkv_a0[:, half:]))
+    prior_a1 = bf(dot(h_before, wqkv_a1[:, half:]))
+    oa0, lse_a0 = attend(opening, pa0, prior_a0)
+    oa1, lse_a1 = attend(opening, pa1, prior_a1)
+    r1 = r0 + (dot(oa0, wout_a) + dot(oa1, wout_a1))
+
+    h1 = normed(r1, gains["b"])
+    ub0, ub1 = dot(h1, up_b), dot(h1, up_b1)
+    ab0, ab1 = bf(smooth(ub0)), bf(smooth(ub1))
+    r2 = r1 + (dot(ab0, down_b) + dot(ab1, down_b1))
+
+    h2 = normed(r2, gains["c"])
+    pc0, pc1 = bf(dot(h2, wqkv_c0)), bf(dot(h2, wqkv_c1))
+    halo = lax.ppermute(jnp.stack(in_order(pc0[:, half:], pc1[:, half:])), GROUP, TO_NEXT)
+    prior_c0, prior_c1 = in_order(halo[0], halo[1])
+
+    def by_head(own, other):
+        pieces = []
+        for weight in (own, other):
+            w = weight.reshape(width, 3, half // HEAD_DIM, HEAD_DIM).transpose(2, 0, 1, 3)
+            pieces.append(w.reshape(half // HEAD_DIM, width, 3 * HEAD_DIM))
+        return jnp.concatenate(pieces, axis=0)
+
+    sqkv_heads = by_head(sqkv_c0, sqkv_c1)
+    sout_heads = jnp.concatenate([sout_c, sout_c1], axis=0).reshape(-1, HEAD_DIM, width)
+    retain = jax.nn.sigmoid(gate_bias.astype(f32))[None, :]
+    state_gain = gain_s.astype(f32)[None, :]
+    state_in = initial
+    for step in range(CHAIN):
+        hs, ps, os, lse_s, update, state_new = state_step(
+            state_in, state_gain, retain, pc0, pc1, sqkv_heads, sout_heads
+        )
+        if step < CHAIN - 1:
+            carried = lax.ppermute(bf(state_new), GROUP, TO_NEXT).astype(f32)
+            state_in = jnp.where(starts, initial, carried)
+
+    def flat_states(i):
+        return jnp.concatenate([ps[i, 0], ps[i, 1], ps[i, 2]], axis=1)
+
+    ps0, ps1 = flat_states(0), flat_states(1)
+    oc0, lse_c0 = attend(opening, pc0, prior_c0, ps0)
+    oc1, lse_c1 = attend(opening, pc1, prior_c1, ps1)
+    r3 = r2 + (dot(oc0, wout_c) + dot(oc1, wout_c1))
+
+    h3 = normed(r3, gains["d"])
+    ud0, ud1 = dot(h3, up_d), dot(h3, up_d1)
+    ad0, ad1 = bf(smooth(ud0)), bf(smooth(ud1))
+    r4 = r3 + (dot(ad0, down_d) + dot(ad1, down_d1))
+    result = bf(jnp.where(alive, r4, 0.0))
+
+    def scattered(value):
+        tiles = value.reshape(tensors, shard_rows, sections, width // sections)
+        tiles = tiles.transpose(2, 0, 1, 3).reshape(sections * tensors, shard_rows, -1)
+        landed = lax.all_to_all(tiles, GROUP, 0, 0, tiled=True)
+        return jnp.stack([landed[DEVICE_OF_BLOCK[b]] for b in range(block_count)])
+
+    out_share = scattered(result)[None]
+    state_tiles = scattered(bf(state_new))
+    chosen = (
+        (numbers[:, None] == jnp.arange(SLOTS, dtype=jnp.int32)[None, :])
+        & (closes & lively)[:, None]
+    )
+    final_share = jnp.stack(
+        [
+            jnp.sum(jnp.where(chosen[:, i, None, None], state_tiles.astype(f32), 0.0), axis=0)
+            for i in range(SLOTS)
+        ],
+        axis=1,
+    )[None]
+
+    def reduced(buffer):
+        pieces = buffer.reshape((sections * tensors,) + buffer.shape[2:])
+        share = lax.psum_scatter(pieces, GROUP, scatter_dimension=0, tiled=True)
+        return lax.psum(share, "dp")[0].astype(f32)
+
+    def empty(tiles):
+        return jnp.zeros((sections, tensors, tiles, 256, 256), jnp.bfloat16)
+
+    def feed_back(grad, values, h, gain, u0, u1, a0, a1, up0, up1, down0, down1):
+        gy = bf(grad)
+        tiles = up0.shape[1] // 256
+        buffer = empty(2 * tiles)
+        g0 = bf(gelu_back(u0, dot_t(gy, down0)))
+        g1 = bf(gelu_back(u1, dot_t(gy, down1)))
+        buffer = weight_grad(buffer, own_place, a0, gy, tiles, False)
+        buffer = weight_grad(buffer, other_place, a1, gy, tiles, False)
+        buffer = weight_grad(buffer, own_place, h, g0[None], 0, True)
+        buffer = weight_grad(buffer, other_place, h, g1[None], 0, True)
+        through = dot_t(g0, up0) + dot_t(g1, up1)
+        back, gain_grad = norm_back(values, gain, through)
+        return grad + back, gain_grad, buffer
+
+    def up_share(share, tiles):
+        return share[:tiles].transpose(1, 0, 2).reshape(256, -1)
+
+    def down_share(share, tiles):
+        return share[tiles : 2 * tiles].reshape(-1, 256)
+
+    grad4 = jnp.where(alive, cotangent.astype(f32), 0.0)
+    grad3, gain_d_grad, buffer_d = feed_back(
+        grad4, r3, h3, gains["d"], ud0, ud1, ad0, ad1, up_d, up_d1, down_d, down_d1
+    )
+    share_d = reduced(buffer_d)
+
+    gy3 = bf(grad3)
+    tok0 = attend_back(opening, pc0, prior_c0, bf(dot_t(gy3, wout_c)), lse_c0, ps0)
+    tok1 = attend_back(opening, pc1, prior_c1, bf(dot_t(gy3, wout_c1)), lse_c1, ps1)
+
+    def halo_back(one, two):
+        pair = in_order(
+            jnp.concatenate([one[3], one[4]], axis=1), jnp.concatenate([two[3], two[4]], axis=1)
+        )
+        back = lax.ppermute(jnp.stack(pair), GROUP, TO_PRIOR).astype(f32)
+        return in_order(back[0], back[1])
+
+    halo_c0, halo_c1 = halo_back(tok0, tok1)
+    grad_new = jnp.zeros_like(initial)
+    for step in range(CHAIN):
+        grad_state, gproj, gtok, gup, small = state_back(
+            grad_new, state_in, update, state_gain, retain, hs, ps, lse_s, pc0, pc1,
+            tok0[5], tok0[6], tok1[5], tok1[6], sqkv_heads, sout_heads,
+        )
+        if step < CHAIN - 1:
+            carried = lax.ppermute(bf(grad_state), GROUP, TO_PRIOR).astype(f32)
+            grad_new = jnp.where(ends, 0.0, carried)
+
+    def projected_back(parts, halo_part, extra=None):
+        gk, gv = parts[1], parts[2]
+        if extra is not None:
+            gk, gv = gk + extra[0], gv + extra[1]
+        return jnp.stack([parts[0], bf(gk + halo_part[:, :half]), bf(gv + halo_part[:, half:])])
+
+    gc0 = projected_back(tok0, halo_c0, gtok[0])
+    gc1 = projected_back(tok1, halo_c1, gtok[1])
+    buffer_c = empty(17)
+    buffer_c = weight_grad(buffer_c, own_place, h2, gc0, 0, True)
+    buffer_c = weight_grad(buffer_c, other_place, h2, gc1, 0, True)
+    buffer_c = weight_grad(buffer_c, own_place, hs, gproj[0], 6, True)
+    buffer_c = weight_grad(buffer_c, other_place, hs, gproj[1], 6, True)
+    buffer_c = weight_grad(buffer_c, own_place, oc0, gy3, 12, False)
+    buffer_c = weight_grad(buffer_c, other_place, oc1, gy3, 12, False)
+    buffer_c = weight_grad(buffer_c, own_place, os[0], gup, 14, False)
+    buffer_c = weight_grad(buffer_c, other_place, os[1], gup, 14, False)
+    first_grad = bf(jnp.where(begins[block], grad_state, 0.0))
+    first_tiles = first_grad.reshape(tensors, -1, sections, 256).transpose(2, 0, 1, 3)
+    buffer_c = lax.dynamic_update_slice(buffer_c, first_tiles[:, :, None], (0, 0, 16, 0, 0))
+    share_c = reduced(buffer_c)
+
+    def through_qkv(g, w):
+        return sum(dot_t(g[i], w[:, i * half : (i + 1) * half]) for i in range(3))
+
+    back_c, gain_c_grad = norm_back(
+        r2, gains["c"], through_qkv(gc0, wqkv_c0) + through_qkv(gc1, wqkv_c1)
+    )
+    grad2 = grad3 + back_c
+
+    grad1, gain_b_grad, buffer_b = feed_back(
+        grad2, r1, h1, gains["b"], ub0, ub1, ab0, ab1, up_b, up_b1, down_b, down_b1
+    )
+    share_b = reduced(buffer_b)
+
+    gy1 = bf(grad1)
+    att0 = attend_back(opening, pa0, prior_a0, bf(dot_t(gy1, wout_a)), lse_a0)
+    att1 = attend_back(opening, pa1, prior_a1, bf(dot_t(gy1, wout_a1)), lse_a1)
+    halo_a0, halo_a1 = halo_back(att0, att1)
+    ga0, ga1 = projected_back(att0, halo_a0), projected_back(att1, halo_a1)
+    buffer_a = empty(8)
+    buffer_a = weight_grad(buffer_a, own_place, oa0, gy1, 6, False)
+    buffer_a = weight_grad(buffer_a, other_place, oa1, gy1, 6, False)
+    buffer_a = weight_grad(buffer_a, own_place, h0, ga0, 0, True)
+    buffer_a = weight_grad(buffer_a, other_place, h0, ga1, 0, True)
+    share_a = reduced(buffer_a)
+    back_a, gain_a_grad = norm_back(
+        r0, gains["a"], through_qkv(ga0, wqkv_a0) + through_qkv(ga1, wqkv_a1)
+    )
+    input_share = scattered(bf(grad1 + back_a)).astype(f32)[None]
+
+    smalls = jnp.stack(
+        [gain_a_grad, gain_b_grad, gain_c_grad, small[0], gain_d_grad, small[1]]
+    )
+    smalls = lax.psum(smalls, ALL_AXES)
+    small_share = lax.dynamic_slice_in_dim(
+        smalls, section * (width // sections), width // sections, 1
+    )
+
+    def qkv_share(share, tile):
+        return (
+            share[tile : tile + 6].reshape(3, 2, 256, 256).transpose(2, 0, 1, 3).reshape(256, 3, 512)
+        )
+
+    def out_rows(share, tile):
+        return share[tile : tile + 2].reshape(-1, 256)
+
+    return (
+        out_share,
+        final_share,
+        input_share,
+        small_share[0],
+        qkv_share(share_a, 0),
+        out_rows(share_a, 6),
+        small_share[1],
+        up_share(share_b, 8),
+        down_share(share_b, 8),
+        small_share[2],
+        small_share[3],
+        qkv_share(share_c, 0),
+        qkv_share(share_c, 6),
+        out_rows(share_c, 12),
+        out_rows(share_c, 14),
+        small_share[5],
+        share_c[16],
+        small_share[4],
+        up_share(share_d, 8),
+        down_share(share_d, 8),
+    )
+
+
+def chosen(*arrays):
+    devices = (lax.axis_size("section"), lax.axis_size("tensor"))
+    if devices == (4, 2) and arrays[0].shape[1] == 8:
+        return block_body(*arrays)
+    return relay_body(*arrays)
+
+
 def solution(mesh):
     in_specs = (
         P("dp", None, "tensor", None),
@@ -835,4 +1594,4 @@
         P("section", "tensor"),
         P("tensor", "section"),
     )
-    return jax.shard_map(body, mesh=mesh, in_specs=in_specs, out_specs=out_specs, check_vma=False)
+    return jax.shard_map(chosen, mesh=mesh, in_specs=in_specs, out_specs=out_specs, check_vma=False)

time: 5730 us -> 1620 us (0.28)
  waiting for transfers between devices: 2680 us -> 575 us
  local copies, waits for them, and re-layouts: 1150 us -> 151 us
  other arithmetic: 863 us -> 98.4 us
  Pallas kernels: 0 us -> 490 us
  matrix products: 620 us -> 131 us
  loops' own time: 290 us -> 0 us
    reduce_scatter x59 -> x4, waiting for transfers between devices: 1640 us -> 218 us  [reduced(): share = lax.psum_scatter(pieces, GROUP, scatter_dimension=0, tiled=True)]
    all_gather x44 -> x10, waiting for transfers between devices: 771 us -> 0.05 us  [other_half(): lax.all_gather(lax.ppermute(piece, 'tensor', SWAP), 'section', axis=0, ti...]
    pallas_call x0 -> x36, Pallas kernels: none -> 490 us  [the longest x20 168 us: weight_grad(): pl.pallas_call(kernel, grid_spec=pltpu.PrefetchScalarGridSpec(num_scalar_...]
    dot_general x143 -> x42, matrix products: 620 us -> 131 us  [the longest x18 74.8 us: dot(): return jnp.dot(a, b, preferred_element_type=f32)]
    another operation x112 -> x6, local copies, waits for them, and re-layouts: 384 us -> 12.8 us
    dynamic_slice x199 -> x13, local copies, waits for them, and re-layouts: 305 us -> 13.7 us  [the longest x10 11.9 us: other_half(): piece = lax.dynamic_slice_in_dim(weight, section * size, size, 0)]
    another operation x24 -> x0, loops' own time: 290 us -> none  [the longest x11 195 us: backward_tick(): lax.switch(section_index, backward_branches, grad_tok, grad_st, tok_norme...]
    dynamic_update_slice x88 -> x0, other arithmetic: 229 us -> none  [place_row(): lax.dynamic_update_index_in_dim(store, jnp.where(active_tick, value, prev...]
  transfers between devices with their start and end apart: 126 -> 41, of which waited for: 100 -> 20; matrix products, arithmetic and copies ran while one was open for 18% -> 15% of each run, Pallas kernels for 0% -> 20%
where the time goes in v1:
time: 1620 us; the launch traced here: 1610 us
  waiting for transfers between devices  575 us (35%)
  Pallas kernels  490 us (30%)
  local copies, waits for them, and re-layouts  151 us (9%)
  matrix products  131 us (8%)
  other arithmetic  98.4 us (6%)
  starting transfers between devices  92.8 us (6%)
  blocking collectives  54.1 us (3%)
  between operations  18.2 us (1%)
    reduce_scatter x4, waiting for transfers between devices, reduced(): share = lax.psum_scatter(pieces, GROUP, scatter_dimension=0, tiled=True)  218 us
    psum x1, waiting for transfers between devices, reduced(): return lax.psum(share, 'dp')[0].astype(f32)  190 us
    pallas_call x20, Pallas kernels, weight_grad(): pl.pallas_call(kernel, grid_spec=pltpu.PrefetchScalarGridSpec(num_scalar_...  168 us
    pallas_call x4, Pallas kernels, state_back(): pl.pallas_call(state_back_kernel, grid=(heads,), in_specs=[whole((count,...  135 us
    ppermute x10, waiting for transfers between devices, other_half(): lax.ppermute(piece, 'tensor', SWAP)  109 us
    pallas_call x4, Pallas kernels, state_step(): pl.pallas_call(state_step_kernel, grid=(heads,), in_specs=[whole((count,...  107 us
    dot_general x18, matrix products, dot(): return jnp.dot(a, b, preferred_element_type=f32)  74.8 us
    unnamed x346, local copies, waits for them, and re-layouts  57.5 us
  transfers between devices with their start and end apart: 41, of which 20 were waited for; matrix products, arithmetic and copies ran while one was open for 15% of the time, Pallas kernels for 20%

profile of v1, /device:TPU:0, one launch (start us, length us, event | category | flops | bytes accessed | tf_op | source)
XLA Modules:
  0.0 1611.0 jit_solution(11906747322407748489)
XLA Ops:
  26.1 17.0 %collective-permute-done.2 = bf16[256,1536]{0,1:T(8,128)(2,1)S(1)} collective-permute-done((bf16[256,1536]{0,1:T(8,128)(2,1)S(1)}, bf16[256,1536]{0,1:T(8,128)(2,1)S(1)}, u32[]{:S(2)}, u32[]{:S(2)}) %collective-permute-start.2) | collective-permute-done | bytes 786464 | tf_op jit(solution)/shard_map/ppermute | solution.py:1292
  59.7 15.7 collective-permute-done.9
  78.4 21.0 %collective-permute-done.4 = bf16[256,2048]{1,0:T(8,128)(2,1)S(1)} collective-permute-done((bf16[256,2048]{1,0:T(8,128)(2,1)S(1)}, bf16[256,2048]{1,0:T(8,128)(2,1)S(1)}, u32[]{:S(2)}, u32[]{:S(2)}) %collective-permute-start.4) | collective-permute-done | bytes 1048608 | tf_op jit(solution)/shard_map/ppermute | solution.py:1292
  102.1 20.5 %collective-permute-done.5 = bf16[512,1024]{1,0:T(8,128)(2,1)S(1)} collective-permute-done((bf16[512,1024]{1,0:T(8,128)(2,1)S(1)}, bf16[512,1024]{1,0:T(8,128)(2,1)S(1)}, u32[]{:S(2)}, u32[]{:S(2)}) %collective-permute-start.5) | collective-permute-done | bytes 1048608 | tf_op jit(solution)/shard_map/ppermute | solution.py:1292
  130.0 14.8 collective-permute-done.6
  274.4 26.7 %state_step.4 = (bf16[512,1024]{1,0:T(8,128)(2,1)}, bf16[2,3,512,512]{3,2,1,0:T(8,128)(2,1)}, bf16[2,512,512]{2,1,0:T(8,128)(2,1)}, f32[8,512,1]{2,1,0:T(8,128)}...) custom-call(f32[512,1024]{1,0:T(8,128)} %fusion.111.state, f32[1,1024]{1,0:T(1,128)} %bitcast.367, f32[1,1024]{1,0:T(1,128)} %bitcast.375, ...), custom_call_target="tpu_custom_call" | custom-call | flops 6442450944 | bytes 20971520 | tf_op jit(solution)/shard_map/state_step/pallas_call | solution.py:1038
  308.2 26.7 %state_step.5 = (bf16[512,1024]{1,0:T(8,128)(2,1)}, bf16[2,3,512,512]{3,2,1,0:T(8,128)(2,1)}, bf16[2,512,512]{2,1,0:T(8,128)(2,1)}, f32[8,512,1]{2,1,0:T(8,128)}...) custom-call(f32[512,1024]{1,0:T(8,128)} %convert_select_fusion.9.state, f32[1,1024]{1,0:T(1,128)} %bitcast.368, ...), custom_call_target="tpu_custom_call" | custom-call | flops 6442450944 | bytes 20971520 | tf_op jit(solution)/shard_map/state_step/pallas_call | solution.py:1038
  337.6 13.1 collective-permute-start.12
  363.4 19.3 %collective-permute-start.7 = (bf16[2,512,1024]{2,1,0:T(8,128)(2,1)}, bf16[2,512,1024]{2,1,0:T(8,128)(2,1)}, u32[]{:S(2)}, u32[]{:S(2)}) collective-permute-start(bf16[2,512,1024]{2,1,0:T(8,128)(2,1)} %pad_maximum_fusion.1), channel_id=1, source_target_pairs={{0,8},{8,1},{1,9},{9,17},{17,25},{25,16},{16,24},{2,10},{10,3},{3,... | collective-permute-start | bytes 6291464 | tf_op jit(solution)/shard_map/ppermute | solution.py:1340
  388.0 26.7 %state_step.6 = (bf16[512,1024]{1,0:T(8,128)(2,1)}, bf16[2,3,512,512]{3,2,1,0:T(8,128)(2,1)}, bf16[2,512,512]{2,1,0:T(8,128)(2,1)}, f32[8,512,1]{2,1,0:T(8,128)}...) custom-call(f32[512,1024]{1,0:T(8,128)} %convert_select_fusion.8.state, f32[1,1024]{1,0:T(1,128)} %bitcast.369, ...), custom_call_target="tpu_custom_call" | custom-call | flops 6442450944 | bytes 20971520 | tf_op jit(solution)/shard_map/state_step/pallas_call | solution.py:1038
  437.0 27.0 %state_step.7 = (bf16[512,1024]{1,0:T(8,128)(2,1)}, bf16[2,3,512,512]{3,2,1,0:T(8,128)(2,1)}, bf16[2,512,512]{2,1,0:T(8,128)(2,1)}, f32[8,512,1]{2,1,0:T(8,128)}...) custom-call(f32[512,1024]{1,0:T(8,128)} %convert_select_fusion.7.state, f32[1,1024]{1,0:T(1,128)} %bitcast.370, ...), custom_call_target="tpu_custom_call" | custom-call | flops 6442450944 | bytes 20971520 | tf_op jit(solution)/shard_map/state_step/pallas_call | solution.py:1038
  467.5 10.8 attend.6
  479.6 10.9 attend.7
  531.6 12.5 attend_back.5
  544.1 12.4 attend_back.4
  558.1 33.5 %state_back.4 = (f32[512,1024]{1,0:T(8,128)}, bf16[2,3,512,512]{3,2,1,0:T(8,128)(2,1)}, f32[2,2,512,512]{3,2,1,0:T(8,128)}, bf16[512,1024]{1,0:T(8,128)(2,1)}, f32[2,1024]{1,0:T(2,128)}) custom-call(f32[512,1024]{1,0:T(8,128)} %broadcast_in_dim.139.grad_new, f32[512,1024]{1,0:T(8,128)} %convert_select_fusion.7.state, f32[512,1024]{1,0:T(8,128)} %get-tuple-element.81.update, ...), custom_call_target="tpu_custom_call" | custom-call | flops 13958643712 | bytes 35651584 | tf_op jit(solution)/shard_map/state_back/pallas_call | solution.py:1145
  604.7 33.7 %state_back.5 = (f32[512,1024]{1,0:T(8,128)}, bf16[2,3,512,512]{3,2,1,0:T(8,128)(2,1)}, f32[2,2,512,512]{3,2,1,0:T(8,128)}, bf16[512,1024]{1,0:T(8,128)(2,1)}, f32[2,1024]{1,0:T(2,128)}) custom-call(f32[512,1024]{1,0:T(8,128)} %convert_select_fusion.5.grad_new, f32[512,1024]{1,0:T(8,128)} %convert_select_fusion.7.state, ...), custom_call_target="tpu_custom_call" | custom-call | flops 13958643712 | bytes 35651584 | tf_op jit(solution)/shard_map/state_back/pallas_call | solution.py:1145
  644.8 12.3 collective-permute-done.19
  658.7 33.5 %state_back.6 = (f32[512,1024]{1,0:T(8,128)}, bf16[2,3,512,512]{3,2,1,0:T(8,128)(2,1)}, f32[2,2,512,512]{3,2,1,0:T(8,128)}, bf16[512,1024]{1,0:T(8,128)(2,1)}, f32[2,1024]{1,0:T(2,128)}) custom-call(f32[512,1024]{1,0:T(8,128)} %convert_select_fusion.4.grad_new, f32[512,1024]{1,0:T(8,128)} %convert_select_fusion.7.state, ...), custom_call_target="tpu_custom_call" | custom-call | flops 13958643712 | bytes 35651584 | tf_op jit(solution)/shard_map/state_back/pallas_call | solution.py:1145
  712.0 34.1 %state_back.7 = (f32[512,1024]{1,0:T(8,128)}, bf16[2,3,512,512]{3,2,1,0:T(8,128)(2,1)}, f32[2,2,512,512]{3,2,1,0:T(8,128)}, bf16[512,1024]{1,0:T(8,128)(2,1)}, f32[2,1024]{1,0:T(2,128)}) custom-call(f32[512,1024]{1,0:T(8,128)} %convert_select_fusion.3.grad_new, f32[512,1024]{1,0:T(8,128)} %convert_select_fusion.7.state, ...), custom_call_target="tpu_custom_call" | custom-call | flops 13958643712 | bytes 35651584 | tf_op jit(solution)/shard_map/state_back/pallas_call | solution.py:1145
  826.0 10.7 weight_grad.22.buffer
  952.9 11.5 weight_grad.28.buffer
  965.7 11.4 weight_grad.29.buffer
  979.2 10.8 weight_grad.30.buffer
  989.9 10.7 weight_grad.31.buffer
  1030.3 25.2 %all-to-all-start = ((bf16[8,256,256]{2,1,0:T(8,128)(2,1)}), bf16[8,256,256]{2,1,0:T(8,128)(2,1)S(1)}, u32[]{:S(2)}, u32[]{:S(2)}) async-start(bf16[8,256,256]{2,1,0:T(8,128)(2,1)} %bitcast.32), calls=%async_computation | async-start | bytes 2097152 | tf_op jit(solution)/shard_map/all_to_all | solution.py:1380
  1059.4 12.4 all-to-all-done
  1079.6 10.6 all-to-all-done.1
  1090.3 93.2 %reduce-scatter.7.cloned.1.call-done = bf16[1,16,256,256]{3,2,1,0:T(8,128)(2,1)} async-done(((bf16[8,16,256,256]{3,2,1,0:T(8,128)(2,1)}), bf16[1,16,256,256]{3,2,1,0:T(8,128)(2,1)}) %reduce-scatter.7.cloned.1.call-update) | async-done | bytes 2097168 | tf_op jit(solution)/shard_map/reduce_scatter | solution.py:1399
  1183.5 124.9 %reduce-scatter.9.cloned.1.call-done = bf16[1,17,256,256]{3,2,1,0:T(8,128)(2,1)} async-done(((bf16[8,17,256,256]{3,2,1,0:T(8,128)(2,1)}), bf16[1,17,256,256]{3,2,1,0:T(8,128)(2,1)}) %reduce-scatter.9.cloned.1.call-update) | async-done | bytes 2228240 | tf_op jit(solution)/shard_map/reduce_scatter | solution.py:1399
  1328.0 54.1 %psum.35 = f32[6,1024]{1,0:T(8,128)S(1)} all-reduce(f32[6,1024]{1,0:T(8,128)S(1)} %stack.143), channel_id=1, replica_groups=mesh['section'=4,'dp'=4,'tensor'=2] {'section','dp','tensor'}, use_global_device_ids=true, to_apply=%region_22.23 | all-reduce | flops 6144 | bytes 49152 | tf_op jit(solution)/shard_map/psum | solution.py:1507
  1384.5 189.7 %all-reduce.3.cloned.1.call-done = (bf16[1,8,256,256]{3,2,1,0:T(8,128)(2,1)}, bf16[1,16,256,256]{3,2,1,0:T(8,128)(2,1)}, bf16[1,17,256,256]{3,2,1,0:T(8,128)(2,1)}, bf16[1,16,256,256]{3,2,1,0:T(8,128)(2,1)}) async-done(((bf16[1,8,256,256]{3,2,1,0:T(8,128)(2,1)}, bf16[1,16,256,256]{3,2,1,0:T(8,128)(2,1)}, bf16[1,17,256,256]{3,2,1,0:T(8,128)(2,1)}, bf16[1,16,256,256]{3,2,1,0:T(8,128)(2,1)}), ...) | async-done | bytes 7471120 | tf_op jit(solution)/shard_map/psum | solution.py:1400
  (625 shorter events, 605.4 us)
Async XLA Ops:
  7.2 193.3 %all-gather.23.cloned.1.call-start = ((), (), s32[]{:S(2)}) async-start(), calls=%async_computation.13 | async-start | bytes 1310720 | tf_op jit(solution)/shard_map/all_gather | solution.py:1292
  18.3 185.2 %all-gather.11.cloned.1.call-start = ((), (), s32[]{:S(2)}) async-start(), calls=%async_computation.7 | async-start | bytes 3932160 | tf_op jit(solution)/shard_map/all_gather | solution.py:1292
  24.2 18.8 %collective-permute-start.2 = (bf16[256,1536]{0,1:T(8,128)(2,1)S(1)}, bf16[256,1536]{0,1:T(8,128)(2,1)S(1)}, u32[]{:S(2)}, u32[]{:S(2)}) collective-permute-start(bf16[256,1536]{0,1:T(8,128)(2,1)S(1)} %constant_dynamic-slice_fusion.10), channel_id=1, source_target_pairs={{0,1},{1,0},{2,3},{3,2},{4,5},{5,4},{6,7},{7,6},{8,9},{9,8},{10,11... | collective-permute-start | bytes 2359304 | tf_op jit(solution)/shard_map/ppermute | solution.py:1292
  43.9 175.1 %all-gather.13.cloned.1.call-start = ((), (), s32[]{:S(2)}) async-start(), calls=%async_computation.8 | async-start | bytes 1310720 | tf_op jit(solution)/shard_map/all_gather | solution.py:1292
  52.3 181.5 %all-gather.21.cloned.1.call-start = ((), (), s32[]{:S(2)}) async-start(), calls=%async_computation.12 | async-start | bytes 3932160 | tf_op jit(solution)/shard_map/all_gather | solution.py:1292
  58.3 17.0 %collective-permute-start.9 = (bf16[256,1536]{0,1:T(8,128)(2,1)S(1)}, bf16[256,1536]{0,1:T(8,128)(2,1)S(1)}, u32[]{:S(2)}, u32[]{:S(2)}) collective-permute-start(bf16[256,1536]{0,1:T(8,128)(2,1)S(1)} %constant_dynamic-slice_fusion.5), channel_id=1, source_target_pairs={{0,1},{1,0},{2,3},{3,2},{4,5},{5,4},{6,7},{7,6},{8,9},{9,8},{10,11... | collective-permute-start | bytes 2359304 | tf_op jit(solution)/shard_map/ppermute | solution.py:1292
  76.2 173.2 %all-gather.15.cloned.1.call-start = ((), (), s32[]{:S(2)}) async-start(), calls=%async_computation.9 | async-start | bytes 5242880 | tf_op jit(solution)/shard_map/all_gather | solution.py:1292
  77.6 21.8 %collective-permute-start.4 = (bf16[256,2048]{1,0:T(8,128)(2,1)S(1)}, bf16[256,2048]{1,0:T(8,128)(2,1)S(1)}, u32[]{:S(2)}, u32[]{:S(2)}) collective-permute-start(bf16[256,2048]{1,0:T(8,128)(2,1)S(1)} %constant_dynamic-slice_fusion.8), channel_id=1, source_target_pairs={{0,1},{1,0},{2,3},{3,2},{4,5},{5,4},{6,7},{7,6},{8,9},{9,8},{10,11... | collective-permute-start | bytes 3145736 | tf_op jit(solution)/shard_map/ppermute | solution.py:1292
  100.4 157.0 %all-gather.17.cloned.1.call-start = ((), (), s32[]{:S(2)}) async-start(), calls=%async_computation.10 | async-start | bytes 5242880 | tf_op jit(solution)/shard_map/all_gather | solution.py:1292
  101.8 20.8 %collective-permute-start.5 = (bf16[512,1024]{1,0:T(8,128)(2,1)S(1)}, bf16[512,1024]{1,0:T(8,128)(2,1)S(1)}, u32[]{:S(2)}, u32[]{:S(2)}) collective-permute-start(bf16[512,1024]{1,0:T(8,128)(2,1)S(1)} %constant_dynamic-slice_fusion.7), channel_id=1, source_target_pairs={{0,1},{1,0},{2,3},{3,2},{4,5},{5,4},{6,7},{7,6},{8,9},{9,8},{10,11... | collective-permute-start | bytes 3145736 | tf_op jit(solution)/shard_map/ppermute | solution.py:1292
  123.6 145.6 %all-gather.19.cloned.1.call-start = ((), (), s32[]{:S(2)}) async-start(), calls=%async_computation.11 | async-start | bytes 3932160 | tf_op jit(solution)/shard_map/all_gather | solution.py:1292
  145.7 278.3 %all-gather.29.cloned.1.call-start = ((), (), s32[]{:S(2)}) async-start(), calls=%async_computation.16 | async-start | bytes 5242880 | tf_op jit(solution)/shard_map/all_gather | solution.py:1292
  147.2 20.9 %collective-permute-start.1 = (bf16[256,1024]{1,0:T(8,128)(2,1)S(1)}, bf16[256,1024]{1,0:T(8,128)(2,1)S(1)}, u32[]{:S(2)}, u32[]{:S(2)}) collective-permute-start(bf16[256,1024]{1,0:T(8,128)(2,1)S(1)} %get-tuple-element.166), channel_id=1, source_target_pairs={{0,1},{1,0},{2,3},{3,2},{4,5},{5,4},{6,7},{7,6},{8,9},{9,8},{10,11... | collective-permute-start | bytes 1572872 | tf_op jit(solution)/shard_map/ppermute | solution.py:1286
  147.7 25.6 %collective-permute-start = (bf16[256,1024]{1,0:T(8,128)(2,1)S(1)}, bf16[256,1024]{1,0:T(8,128)(2,1)S(1)}, u32[]{:S(2)}, u32[]{:S(2)}) collective-permute-start(bf16[256,1024]{1,0:T(8,128)(2,1)S(1)} %get-tuple-element.167), channel_id=1, source_target_pairs={{0,1},{1,0},{2,3},{3,2},{4,5},{5,4},{6,7},{7,6},{8,9},{9,8},{10,11... | collective-permute-start | bytes 1572872 | tf_op jit(solution)/shard_map/ppermute | solution.py:1286
  149.3 41.2 %collective-permute-start.8 = (bf16[256,1024]{1,0:T(8,128)(2,1)}, bf16[256,1024]{1,0:T(8,128)(2,1)}, u32[]{:S(2)}, u32[]{:S(2)}) collective-permute-start(bf16[256,1024]{1,0:T(8,128)(2,1)} %param.38), channel_id=1, source_target_pairs={{0,1},{1,0},{2,3},{3,2},{4,5},{5,4},{6,7},{7,6},{8,9},{9,8},{10,11... | collective-permute-start | bytes 1572872 | tf_op jit(solution)/shard_map/ppermute | solution.py:1310
  152.0 48.2 %collective-permute-start.16 = (bf16[512,1024]{1,0:T(8,128)(2,1)}, bf16[512,1024]{1,0:T(8,128)(2,1)}, u32[]{:S(2)}, u32[]{:S(2)}) collective-permute-start(bf16[512,1024]{1,0:T(8,128)(2,1)} %constant_dynamic-slice_fusion.1), channel_id=1, source_target_pairs={{0,1},{1,0},{2,3},{3,2},{4,5},{5,4},{6,7},{7,6},{8,9},{9,8},{10,11... | collective-permute-start | bytes 3145736 | tf_op jit(solution)/shard_map/ppermute | solution.py:1292
  200.2 292.3 %all-gather.25.cloned.1.call-start = ((), (), s32[]{:S(2)}) async-start(), calls=%async_computation.14 | async-start | bytes 1310720 | tf_op jit(solution)/shard_map/all_gather | solution.py:1292
  337.6 47.4 %collective-permute-start.12 = (bf16[512,1024]{1,0:T(8,128)(2,1)}, bf16[512,1024]{1,0:T(8,128)(2,1)}, u32[]{:S(2)}, u32[]{:S(2)}) collective-permute-start(bf16[512,1024]{1,0:T(8,128)(2,1)} %convert_element_type.244), channel_id=1, source_target_pairs={{0,8},{8,1},{1,9},{9,17},{17,25},{25,16},{16,24},{2,10},{10,3},{3,... | collective-permute-start | bytes 3145736 | tf_op jit(solution)/shard_map/ppermute | solution.py:1360
  354.1 65.9 %collective-permute-start.17 = (bf16[256,1024]{1,0:T(8,128)(2,1)}, bf16[256,1024]{1,0:T(8,128)(2,1)}, u32[]{:S(2)}, u32[]{:S(2)}) collective-permute-start(bf16[256,1024]{1,0:T(8,128)(2,1)} %dynamic-slice_bitcast_fusion), channel_id=1, source_target_pairs={{0,1},{1,0},{2,3},{3,2},{4,5},{5,4},{6,7},{7,6},{8,9},{9,8},{10,11... | collective-permute-start | bytes 1572872 | tf_op jit(solution)/shard_map/ppermute | solution.py:1286
  360.2 152.0 %all-gather.27.cloned.1.call-start = ((), (), s32[]{:S(2)}) async-start(), calls=%async_computation.15 | async-start | bytes 5242880 | tf_op jit(solution)/shard_map/all_gather | solution.py:1292
  363.4 67.5 %collective-permute-start.7 = (bf16[2,512,1024]{2,1,0:T(8,128)(2,1)}, bf16[2,512,1024]{2,1,0:T(8,128)(2,1)}, u32[]{:S(2)}, u32[]{:S(2)}) collective-permute-start(bf16[2,512,1024]{2,1,0:T(8,128)(2,1)} %pad_maximum_fusion.1), channel_id=1, source_target_pairs={{0,8},{8,1},{1,9},{9,17},{17,25},{25,16},{16,24},{2,10},{10,3},{3,... | collective-permute-start | bytes 6291464 | tf_op jit(solution)/shard_map/ppermute | solution.py:1340
  384.1 39.9 %collective-permute-start.15 = (bf16[256,2048]{1,0:T(8,128)(2,1)S(1)}, bf16[256,2048]{1,0:T(8,128)(2,1)}, u32[]{:S(2)}, u32[]{:S(2)}) collective-permute-start(bf16[256,2048]{1,0:T(8,128)(2,1)S(1)} %constant_dynamic-slice_fusion.2), channel_id=1, source_target_pairs={{0,1},{1,0},{2,3},{3,2},{4,5},{5,4},{6,7},{7,6},{8,9},{9,8},{10,11... | collective-permute-start | bytes 3145736 | tf_op jit(solution)/shard_map/ppermute | solution.py:1292
  424.0 666.3 %reduce-scatter.5.cloned.1.call-start = ((), (), s32[]{:S(2)}) async-start(), calls=%async_computation.17 | async-start | bytes 9437184 | tf_op jit(solution)/shard_map/reduce_scatter | solution.py:1399
  643.5 57.4 %collective-permute-start.21 = (bf16[2,512,1024]{2,1,0:T(8,128)(2,1)}, bf16[2,512,1024]{2,1,0:T(8,128)(2,1)}, u32[]{:S(2)}, u32[]{:S(2)}) collective-permute-start(bf16[2,512,1024]{2,1,0:T(8,128)(2,1)} %pad_maximum_fusion.3), channel_id=1, source_target_pairs={{8,0},{1,8},{9,1},{17,9},{25,17},{16,25},{24,16},{10,2},{3,10},{11... | collective-permute-start | bytes 6291464 | tf_op jit(solution)/shard_map/ppermute | solution.py:1439
  804.0 17.6 %collective-permute-start.22 = (bf16[2,512,1024]{2,1,0:T(8,128)(2,1)S(1)}, bf16[2,512,1024]{2,1,0:T(8,128)(2,1)S(1)}, u32[]{:S(2)}, u32[]{:S(2)}) collective-permute-start(bf16[2,512,1024]{2,1,0:T(8,128)(2,1)S(1)} %pad_maximum_fusion.4), channel_id=1, source_target_pairs={{8,0},{1,8},{9,1},{17,9},{25,17},{16,25},{24,16},{10,2},{3,10},{11... | collective-permute-start | bytes 6291464 | tf_op jit(solution)/shard_map/ppermute | solution.py:1439
  849.6 240.7 %reduce-scatter.11.cloned.1.call-start = ((), (), s32[]{:S(2)}) async-start(), calls=%async_computation.20 | async-start | bytes 18874368 | tf_op jit(solution)/shard_map/reduce_scatter | solution.py:1399
  894.4 289.0 %reduce-scatter.7.cloned.1.call-start = ((), (), s32[]{:S(2)}) async-start(), calls=%async_computation.18 | async-start | bytes 18874368 | tf_op jit(solution)/shard_map/reduce_scatter | solution.py:1399
  939.3 369.1 %reduce-scatter.9.cloned.1.call-start = ((), (), s32[]{:S(2)}) async-start(), calls=%async_computation.19 | async-start | bytes 20054016 | tf_op jit(solution)/shard_map/reduce_scatter | solution.py:1399
  1030.3 41.5 %all-to-all-start = ((bf16[8,256,256]{2,1,0:T(8,128)(2,1)}), bf16[8,256,256]{2,1,0:T(8,128)(2,1)S(1)}, u32[]{:S(2)}, u32[]{:S(2)}) async-start(bf16[8,256,256]{2,1,0:T(8,128)(2,1)} %bitcast.32), calls=%async_computation | async-start | bytes 2097152 | tf_op jit(solution)/shard_map/all_to_all | solution.py:1380
  1071.8 18.4 %all-to-all-start.1 = ((bf16[8,256,256]{2,1,0:T(8,128)(2,1)}), bf16[8,256,256]{2,1,0:T(8,128)(2,1)S(1)}, u32[]{:S(2)}, u32[]{:S(2)}) async-start(bf16[8,256,256]{2,1,0:T(8,128)(2,1)} %bitcast.38), calls=%async_computation.1 | async-start | bytes 2097152 | tf_op jit(solution)/shard_map/all_to_all | solution.py:1380
  1075.4 498.8 %all-reduce.3.cloned.1.call-start = ((), (), s32[]{:S(2)}) async-start(), calls=%async_computation.21 | async-start | bytes 14942208 | tf_op jit(solution)/shard_map/psum | solution.py:1400
  1321.9 60.9 %all-to-all-start.2 = ((bf16[8,256,256]{2,1,0:T(8,128)(2,1)}), bf16[8,256,256]{2,1,0:T(8,128)(2,1)S(1)}, u32[]{:S(2)}, u32[]{:S(2)}) async-start(bf16[8,256,256]{2,1,0:T(8,128)(2,1)} %bitcast.65), calls=%async_computation.2 | async-start | bytes 2097152 | tf_op jit(solution)/shard_map/all_to_all | solution.py:1380
  (169 other events, 1666.0 us)
Sparse Core Ops, SparseCore 0:
  18.5 18.2 all-gather.22
  44.1 30.1 all-gather.10
  76.4 16.7 all-gather.12
  95.1 28.9 all-gather.20
  126.0 34.4 all-gather.14
  162.0 34.4 all-gather.16
  198.0 28.9 all-gather.18
  228.6 34.4 all-gather.28
  360.3 32.0 all-gather.24
  424.1 37.0 all-gather.26
  849.7 91.7 reduce-scatter.4
  945.4 117.0 reduce-scatter.10
  1066.4 116.9 reduce-scatter.6
  1187.5 120.8 reduce-scatter.8
  1311.1 263.0 all-reduce.2

commit v2 on v0

--- a/solution.py
+++ b/solution.py
@@ -1,10 +1,14 @@
+import functools
 import math
 
 import jax
 import jax.numpy as jnp
 from jax import lax
+from jax.experimental import pallas as pl
+from jax.experimental.pallas import tpu as pltpu
 from jax.sharding import PartitionSpec as P
 
+SECTION, DP, TENSOR = "section", "dp", "tensor"
 HEAD_DIM = 128
 SLOTS = 3
 
@@ -120,7 +124,7 @@
     )
 
 
-def body(
+def relay_body(
     layer_input,
     output_grad,
     seg_blocks,
@@ -146,14 +150,14 @@
     block_count = layer_input.shape[1]
     shard_rows = layer_input.shape[2]
     model_width = layer_input.shape[3]
-    tensor_count = lax.axis_size("tensor")
+    tensor_count = lax.axis_size(TENSOR)
     token_rows = shard_rows * tensor_count
     state_shard = init_states.shape[0]
     state_count = state_shard * tensor_count
     local_width = wqkv_a.shape[2]
     local_heads = local_width // HEAD_DIM
-    section_index = lax.axis_index("section")
-    group_index = lax.axis_index("dp")
+    section_index = lax.axis_index(SECTION)
+    group_index = lax.axis_index(DP)
     on_cell_section = section_index == 2
     begins, closes, lively, numbers = layout(seg_blocks, seg_group, group_index, block_count)
     token_gains = jnp.stack([gain_a, gain_b, gain_c, gain_d]).astype(jnp.float32)
@@ -484,8 +488,8 @@
         normed_shard = (entering * inverse_rms(entering) * token_gain).astype(jnp.bfloat16)
         state_normed_shard = (state_in * inverse_rms(state_in) * state_gain).astype(jnp.bfloat16)
         normed_tok, normed_st = (
-            lax.all_gather(normed_shard, "tensor", axis=0, tiled=True),
-            lax.all_gather(state_normed_shard, "tensor", axis=0, tiled=True),
+            lax.all_gather(normed_shard, TENSOR, axis=0, tiled=True),
+            lax.all_gather(state_normed_shard, TENSOR, axis=0, tiled=True),
         )
         prior_block = tok_stored[jnp.maximum(block_index - 1, 0)]
         branch, update_term, stored, state_stored, token_lse, state_lse = lax.switch(
@@ -493,10 +497,10 @@
         )
         branch_shard, update_shard = (
             lax.psum_scatter(
-                branch.astype(jnp.bfloat16), "tensor", scatter_dimension=0, tiled=True
+                branch.astype(jnp.bfloat16), TENSOR, scatter_dimension=0, tiled=True
             ).astype(jnp.float32),
             lax.psum_scatter(
-                update_term.astype(jnp.bfloat16), "tensor", scatter_dimension=0, tiled=True
+                update_term.astype(jnp.bfloat16), TENSOR, scatter_dimension=0, tiled=True
             ).astype(jnp.float32),
         )
         leaving = entering + branch_shard
@@ -518,7 +522,7 @@
             None, :, None
         ] & keep_final
         finals = jnp.where(slot_hit, state_new[:, None, :], finals)
-        received = shifted(leaving.astype(jnp.bfloat16), "section", 1).astype(leaving.dtype)
+        received = shifted(leaving.astype(jnp.bfloat16), SECTION, 1).astype(leaving.dtype)
         return (
             received,
             state_carry,
@@ -591,8 +595,8 @@
         )
         update_grad = (1.0 - retain) * state_grad
         grad_tok, grad_st = (
-            lax.all_gather(arriving.astype(jnp.bfloat16), "tensor", axis=0, tiled=True),
-            lax.all_gather(update_grad.astype(jnp.bfloat16), "tensor", axis=0, tiled=True),
+            lax.all_gather(arriving.astype(jnp.bfloat16), TENSOR, axis=0, tiled=True),
+            lax.all_gather(update_grad.astype(jnp.bfloat16), TENSOR, axis=0, tiled=True),
         )
         grad_normed_tok, grad_normed_st, prior_keys, prior_values, grad_sums = lax.switch(
             section_index,
@@ -614,10 +618,10 @@
         )
         tok_shard, st_shard = (
             lax.psum_scatter(
-                grad_normed_tok.astype(jnp.bfloat16), "tensor", scatter_dimension=0, tiled=True
+                grad_normed_tok.astype(jnp.bfloat16), TENSOR, scatter_dimension=0, tiled=True
             ).astype(jnp.float32),
             lax.psum_scatter(
-                grad_normed_st.astype(jnp.bfloat16), "tensor", scatter_dimension=0, tiled=True
+                grad_normed_st.astype(jnp.bfloat16), TENSOR, scatter_dimension=0, tiled=True
             ).astype(jnp.float32),
         )
         grad_entering, token_gain_term = norm_back(
@@ -647,7 +651,7 @@
         carry_keys = jnp.where(active_tick, prior_keys, carry_keys)
         carry_values = jnp.where(active_tick, prior_values, carry_values)
         input_rows = place_row(input_rows, block_index, leaving_grad, active_tick)
-        received = shifted(for_sending(leaving_grad), "section", -1).astype(leaving_grad.dtype)
+        received = shifted(for_sending(leaving_grad), SECTION, -1).astype(leaving_grad.dtype)
         return (
             received,
             state_grad,
@@ -691,13 +695,13 @@
     final_term = jnp.where(section_index == 2, finals, 0.0)[None]
     out_share, input_share, final_share = (
         lax.psum_scatter(
-            out_term.astype(jnp.bfloat16), "section", scatter_dimension=3, tiled=True
+            out_term.astype(jnp.bfloat16), SECTION, scatter_dimension=3, tiled=True
         ).astype(jnp.float32),
         lax.psum_scatter(
-            input_term.astype(jnp.bfloat16), "section", scatter_dimension=3, tiled=True
+            input_term.astype(jnp.bfloat16), SECTION, scatter_dimension=3, tiled=True
         ).astype(jnp.float32),
         lax.psum_scatter(
-            final_term.astype(jnp.bfloat16), "section", scatter_dimension=3, tiled=True
+            final_term.astype(jnp.bfloat16), SECTION, scatter_dimension=3, tiled=True
         ).astype(jnp.float32),
     )
     (
@@ -713,55 +717,55 @@
         grad_lower_d,
     ) = grad_sums
     totals = (
-        lax.psum(grad_qkv_a.astype(jnp.bfloat16), "dp").astype(jnp.float32),
-        lax.psum(grad_out_a.astype(jnp.bfloat16), "dp").astype(jnp.float32),
-        lax.psum(grad_upper_b.astype(jnp.bfloat16), "dp").astype(jnp.float32),
-        lax.psum(grad_lower_b.astype(jnp.bfloat16), "dp").astype(jnp.float32),
-        lax.psum(grad_qkv_c.astype(jnp.bfloat16), "dp").astype(jnp.float32),
-        lax.psum(grad_state_qkv.astype(jnp.bfloat16), "dp").astype(jnp.float32),
-        lax.psum(grad_out_c.astype(jnp.bfloat16), "dp").astype(jnp.float32),
-        lax.psum(grad_state_out.astype(jnp.bfloat16), "dp").astype(jnp.float32),
-        lax.psum(grad_upper_d.astype(jnp.bfloat16), "dp").astype(jnp.float32),
-        lax.psum(grad_lower_d.astype(jnp.bfloat16), "dp").astype(jnp.float32),
-        lax.psum(initial_grad.astype(jnp.bfloat16), "dp").astype(jnp.float32),
-    )
-    small_total = lax.psum(smalls, ("dp", "tensor"))
+        lax.psum(grad_qkv_a.astype(jnp.bfloat16), DP).astype(jnp.float32),
+        lax.psum(grad_out_a.astype(jnp.bfloat16), DP).astype(jnp.float32),
+        lax.psum(grad_upper_b.astype(jnp.bfloat16), DP).astype(jnp.float32),
+        lax.psum(grad_lower_b.astype(jnp.bfloat16), DP).astype(jnp.float32),
+        lax.psum(grad_qkv_c.astype(jnp.bfloat16), DP).astype(jnp.float32),
+        lax.psum(grad_state_qkv.astype(jnp.bfloat16), DP).astype(jnp.float32),
+        lax.psum(grad_out_c.astype(jnp.bfloat16), DP).astype(jnp.float32),
+        lax.psum(grad_state_out.astype(jnp.bfloat16), DP).astype(jnp.float32),
+        lax.psum(grad_upper_d.astype(jnp.bfloat16), DP).astype(jnp.float32),
+        lax.psum(grad_lower_d.astype(jnp.bfloat16), DP).astype(jnp.float32),
+        lax.psum(initial_grad.astype(jnp.bfloat16), DP).astype(jnp.float32),
+    )
+    small_total = lax.psum(smalls, (DP, TENSOR))
     shares = (
         lax.psum_scatter(
-            totals[0].astype(jnp.bfloat16), "section", scatter_dimension=0, tiled=True
+            totals[0].astype(jnp.bfloat16), SECTION, scatter_dimension=0, tiled=True
         ).astype(jnp.float32),
         lax.psum_scatter(
-            totals[1].astype(jnp.bfloat16), "section", scatter_dimension=1, tiled=True
+            totals[1].astype(jnp.bfloat16), SECTION, scatter_dimension=1, tiled=True
         ).astype(jnp.float32),
         lax.psum_scatter(
-            totals[2].astype(jnp.bfloat16), "section", scatter_dimension=0, tiled=True
+            totals[2].astype(jnp.bfloat16), SECTION, scatter_dimension=0, tiled=True
         ).astype(jnp.float32),
         lax.psum_scatter(
-            totals[3].astype(jnp.bfloat16), "section", scatter_dimension=1, tiled=True
+            totals[3].astype(jnp.bfloat16), SECTION, scatter_dimension=1, tiled=True
         ).astype(jnp.float32),
         lax.psum_scatter(
-            totals[4].astype(jnp.bfloat16), "section", scatter_dimension=0, tiled=True
+            totals[4].astype(jnp.bfloat16), SECTION, scatter_dimension=0, tiled=True
         ).astype(jnp.float32),
         lax.psum_scatter(
-            totals[5].astype(jnp.bfloat16), "section", scatter_dimension=0, tiled=True
+            totals[5].astype(jnp.bfloat16), SECTION, scatter_dimension=0, tiled=True
         ).astype(jnp.float32),
         lax.psum_scatter(
-            totals[6].astype(jnp.bfloat16), "section", scatter_dimension=1, tiled=True
+            totals[6].astype(jnp.bfloat16), SECTION, scatter_dimension=1, tiled=True
         ).astype(jnp.float32),
         lax.psum_scatter(
-            totals[7].astype(jnp.bfloat16), "section", scatter_dimension=1, tiled=True
+            totals[7].astype(jnp.bfloat16), SECTION, scatter_dimension=1, tiled=True
         ).astype(jnp.float32),
         lax.psum_scatter(
-            totals[8].astype(jnp.bfloat16), "section", scatter_dimension=0, tiled=True
+            totals[8].astype(jnp.bfloat16), SECTION, scatter_dimension=0, tiled=True
         ).astype(jnp.float32),
         lax.psum_scatter(
-            totals[9].astype(jnp.bfloat16), "section", scatter_dimension=1, tiled=True
+            totals[9].astype(jnp.bfloat16), SECTION, scatter_dimension=1, tiled=True
         ).astype(jnp.float32),
         lax.psum_scatter(
-            totals[10].astype(jnp.bfloat16), "section", scatter_dimension=1, tiled=True
+            totals[10].astype(jnp.bfloat16), SECTION, scatter_dimension=1, tiled=True
         ).astype(jnp.float32),
         lax.psum_scatter(
-            small_total.astype(jnp.bfloat16), "section", scatter_dimension=1, tiled=True
+            small_total.astype(jnp.bfloat16), SECTION, scatter_dimension=1, tiled=True
         ).astype(jnp.float32),
     )
     small_share = shares[11]
@@ -789,50 +793,1308 @@
     )
 
 
+CHAIN = 4
+MESH = pl.DeviceIdType.MESH
+SCALE = 1.0 / math.sqrt(HEAD_DIM)
+LOG2_SCALE = SCALE * math.log2(math.e)
+ALL_AXES = (SECTION, DP, TENSOR)
+GROUP = (SECTION, TENSOR)
+VMEM_BYTES = 60 * 1024 * 1024
+CHUNK = 256
+
+
+def block_of(section, tensor):
+    high = section // 2
+    return 2 * (2 * high + (tensor + high) % 2) + section % 2
+
+
+DEVICE_OF_BLOCK = [0] * 8
+for _section in range(4):
+    for _tensor in range(2):
+        DEVICE_OF_BLOCK[block_of(_section, _tensor)] = 2 * _section + _tensor
+TO_NEXT = [(DEVICE_OF_BLOCK[b], DEVICE_OF_BLOCK[b + 1]) for b in range(7)]
+TO_PRIOR = [(there, here) for here, there in TO_NEXT]
+SWAP = [(0, 1), (1, 0)]
+
+
+def params(**extra):
+    return pltpu.CompilerParams(vmem_limit_bytes=VMEM_BYTES, **extra)
+
+
+def nt(a, b):
+    return lax.dot_general(a, b, (((1,), (1,)), ((), ())), preferred_element_type=jnp.float32)
+
+
+def nn(a, b):
+    return lax.dot_general(a, b, (((1,), (0,)), ((), ())), preferred_element_type=jnp.float32)
+
+
+def tn(a, b):
+    return lax.dot_general(a, b, (((0,), (0,)), ((), ())), preferred_element_type=jnp.float32)
+
+
+def bf(a):
+    return a.astype(jnp.bfloat16)
+
+
+def with_ones(values):
+    return jnp.concatenate([values, jnp.ones_like(values)], axis=1)
+
+
+def later_mask(rows):
+    return lax.broadcasted_iota(jnp.int32, (rows, rows), 1) > lax.broadcasted_iota(
+        jnp.int32, (rows, rows), 0
+    )
+
+
+def window_scores(query, k, pk, start, rows, bar):
+    stop = start + query.shape[0]
+    own = nt(query, k[:stop])
+    prior = nt(query, pk[start:]) + bar
+    later = later_mask(query.shape[0])
+    pieces = [jnp.where(later, prior[:, : stop - start], own[:, start:])]
+    if start:
+        pieces = [own[:, :start]] + pieces
+    if stop < rows:
+        pieces = pieces + [prior[:, stop - start :]]
+    return jnp.concatenate(pieces, axis=1) if len(pieces) > 1 else pieces[0]
+
+
+def window_parts(values, start):
+    size = values.shape[0]
+    later = later_mask(size)
+    middle = values[:, start : start + size]
+    zero = jnp.zeros_like(middle)
+    own, prior = jnp.where(later, zero, middle), jnp.where(later, middle, zero)
+    if start:
+        own = jnp.concatenate([values[:, :start], own], axis=1)
+    if start + size < values.shape[1]:
+        prior = jnp.concatenate([prior, values[:, start + size :]], axis=1)
+    return own, prior
+
+
+def attend_kernel(with_states, *refs):
+    if with_states:
+        open_ref, q, k, v, pk, pv, sk, sv, out, lse = refs
+    else:
+        open_ref, q, k, v, pk, pv, out, lse = refs
+    rows = q.shape[0]
+    bar = jnp.where(open_ref[0] > 0, NEGATIVE, 0.0)
+    keys, prior_keys = k[...], pk[...]
+    values, prior_values = with_ones(v[...]), with_ones(pv[...])
+    if with_states:
+        state_keys, state_values = sk[...], with_ones(sv[...])
+    for start in range(0, rows, CHUNK):
+        query = q[start : start + CHUNK]
+        scores = window_scores(query, keys, prior_keys, start, rows, bar)
+        top = jnp.max(scores, axis=-1, keepdims=True)
+        if with_states:
+            more = nt(query, state_keys)
+            top = jnp.maximum(top, jnp.max(more, axis=-1, keepdims=True))
+        own, prior = window_parts(bf(jnp.exp2((scores - top) * LOG2_SCALE)), start)
+        mixed = nn(own, values[: start + CHUNK]) + nn(prior, prior_values[start:])
+        if with_states:
+            mixed = mixed + nn(bf(jnp.exp2((more - top) * LOG2_SCALE)), state_values)
+        total = mixed[:, HEAD_DIM:]
+        out[start : start + CHUNK] = bf(mixed[:, :HEAD_DIM] / total)
+        lse[0, start : start + CHUNK] = top * LOG2_SCALE + jnp.log2(total[:, :1])
+
+
+def head_block(rows, offset):
+    return pl.BlockSpec((rows, HEAD_DIM), lambda h: (0, offset + h))
+
+
+def attend(opening, proj, prior, states=None):
+    rows, width = proj.shape[0], proj.shape[1] // 3
+    heads = width // HEAD_DIM
+    specs = [pl.BlockSpec(memory_space=pltpu.SMEM)]
+    specs += [head_block(rows, i * heads) for i in range(3)]
+    specs += [head_block(rows, i * heads) for i in range(2)]
+    args = [opening, proj, proj, proj, prior, prior]
+    keys = 2 * rows
+    if states is not None:
+        specs += [head_block(states.shape[0], i * heads) for i in (1, 2)]
+        args += [states, states]
+        keys += states.shape[0]
+    return pl.pallas_call(
+        functools.partial(attend_kernel, states is not None),
+        grid=(heads,),
+        in_specs=specs,
+        out_specs=[
+            head_block(rows, 0),
+            pl.BlockSpec((1, rows, 1), lambda h: (h, 0, 0)),
+        ],
+        out_shape=[
+            jax.ShapeDtypeStruct((rows, width), jnp.bfloat16),
+            jax.ShapeDtypeStruct((heads, rows, 1), jnp.float32),
+        ],
+        compiler_params=params(),
+        cost_estimate=pl.CostEstimate(
+            flops=4 * rows * keys * width,
+            bytes_accessed=2 * rows * width * 8,
+            transcendentals=rows * keys * heads // 2,
+        ),
+    )(*args)
+
+
+def attend_back_kernel(with_states, *refs):
+    if with_states:
+        (open_ref, q, k, v, pk, pv, sk, sv, gmix, mix, lse) = refs[:11]
+        (gq, gk, gv, gpk, gpv, gsk, gsv) = refs[11:18]
+    else:
+        (open_ref, q, k, v, pk, pv, gmix, mix, lse) = refs[:9]
+        (gq, gk, gv, gpk, gpv) = refs[9:14]
+    gpk_sum, gpv_sum = refs[-2:]
+    rows = q.shape[0]
+    bar = jnp.where(open_ref[0] > 0, NEGATIVE, 0.0)
+    keys, prior_keys, values, prior_values = k[...], pk[...], v[...], pv[...]
+    if with_states:
+        state_keys, state_values = sk[...], sv[...]
+    for start in range(0, rows, CHUNK):
+        stop = start + CHUNK
+        query, grad, log_total = q[start:stop], gmix[start:stop], lse[0, start:stop]
+        inner = jnp.sum(
+            grad.astype(jnp.float32) * mix[start:stop].astype(jnp.float32), axis=-1, keepdims=True
+        )
+        scores = window_scores(query, keys, prior_keys, start, rows, bar)
+        weights = jnp.exp2(scores * LOG2_SCALE - log_total)
+        grad_weights = window_scores(grad, values, prior_values, start, rows, 0.0)
+        own, prior = window_parts(bf(weights), start)
+        own_scores, prior_scores = window_parts(bf(weights * (grad_weights - inner)), start)
+        grad_query = nn(own_scores, keys[:stop]) + nn(prior_scores, prior_keys[start:])
+        add_own_v, add_own_k = tn(own, grad), tn(own_scores, query)
+        add_prior_v, add_prior_k = tn(prior, grad), tn(prior_scores, query)
+        if with_states:
+            more = jnp.exp2(nt(query, state_keys) * LOG2_SCALE - log_total)
+            from_states = bf(more * (nt(grad, state_values) - inner))
+            grad_query = grad_query + nn(from_states, state_keys)
+            add_sv, add_sk = tn(bf(more), grad), tn(from_states, query)
+        gq[start:stop] = bf(grad_query * SCALE)
+        if start == 0:
+            gv[:stop], gk[:stop] = add_own_v, add_own_k * SCALE
+            gpv_sum[...], gpk_sum[...] = add_prior_v, add_prior_k
+            if with_states:
+                gsv[...], gsk[...] = add_sv, add_sk * SCALE
+        else:
+            gv[:start] += add_own_v[:start]
+            gk[:start] += add_own_k[:start] * SCALE
+            gv[start:stop], gk[start:stop] = add_own_v[start:], add_own_k[start:] * SCALE
+            gpv_sum[start:] += add_prior_v
+            gpk_sum[start:] += add_prior_k
+            if with_states:
+                gsv[...] += add_sv
+                gsk[...] += add_sk * SCALE
+    gpv[...] = bf(gpv_sum[...])
+    gpk[...] = bf(gpk_sum[...] * SCALE)
+
+
+def attend_back(opening, proj, prior, grad_mixed, mixed, lse, states=None):
+    rows, width = proj.shape[0], proj.shape[1] // 3
+    heads = width // HEAD_DIM
+    specs = [pl.BlockSpec(memory_space=pltpu.SMEM)]
+    specs += [head_block(rows, i * heads) for i in range(3)]
+    specs += [head_block(rows, i * heads) for i in range(2)]
+    args = [opening, proj, proj, proj, prior, prior]
+    keys = 2 * rows
+    if states is not None:
+        specs += [head_block(states.shape[0], i * heads) for i in (1, 2)]
+        args += [states, states]
+        keys += states.shape[0]
+    specs += [head_block(rows, 0), head_block(rows, 0)]
+    specs += [pl.BlockSpec((1, rows, 1), lambda h: (h, 0, 0))]
+    args += [grad_mixed, mixed, lse]
+    kinds = [jnp.bfloat16, jnp.float32, jnp.float32, jnp.bfloat16, jnp.bfloat16]
+    if states is not None:
+        kinds += [jnp.float32, jnp.float32]
+    return pl.pallas_call(
+        functools.partial(attend_back_kernel, states is not None),
+        grid=(heads,),
+        in_specs=specs,
+        out_specs=[head_block(rows, 0) for _ in kinds],
+        out_shape=[jax.ShapeDtypeStruct((rows, width), kind) for kind in kinds],
+        scratch_shapes=[pltpu.VMEM((rows, HEAD_DIM), jnp.float32)] * 2,
+        compiler_params=params(),
+        cost_estimate=pl.CostEstimate(
+            flops=10 * rows * keys * width,
+            bytes_accessed=2 * rows * width * 24,
+            transcendentals=rows * keys * heads // 2,
+        ),
+    )(*args)
+
+
+KINDS = 9
+
+
+class Spread:
+    def __init__(self, sources, targets, send, recv):
+        section, tensor, group = (lax.axis_index(a) for a in (SECTION, TENSOR, DP))
+        self.sources, self.targets, self.send, self.recv = sources, targets, send, recv
+        self.core, self.high, self.near = section % 2, section // 2, group % 2
+        self.across = {TENSOR: 1 - tensor}
+        self.along = {SECTION: (section + 2) % 4}
+        self.beside = {DP: group + 1 - 2 * self.near}
+        self.other = {SECTION: section + 1 - 2 * self.core}
+
+    def partners(self):
+        return [self.across, self.along, self.beside, self.other]
+
+    def copy(self, kind, w):
+        size = self.targets[w].shape[0] // 8
+        y, z = self.high, self.near
+        high, near, first, rows, to = (
+            (y, z, 0, size, self.across),
+            (y, z, 0, size, self.along),
+            (y, z, 0, size, self.beside),
+            (y, 1 - z, 0, size // 2, self.along),
+            (1 - y, z, size // 2, size // 2, self.beside),
+            (y, z, 0, size, self.other),
+            (1 - y, z, 0, size, self.other),
+            (y, 1 - z, 0, size, self.other),
+            (1 - y, 1 - z, 0, size, self.other),
+        )[kind]
+        part = (near * 2 + high) * 2 + self.core
+        where = pl.ds(pl.multiple_of(part * size + first, rows), rows)
+        source = self.sources[w] if kind == 0 else self.targets[w]
+        return pltpu.make_async_remote_copy(
+            src_ref=source.at[where], dst_ref=self.targets[w].at[where],
+            send_sem=self.send.at[kind * len(self.targets) + w],
+            recv_sem=self.recv.at[kind * len(self.targets) + w],
+            device_id=to, device_id_type=MESH,
+        )
+
+    def begin(self, w):
+        self.copy(0, w).start()
+
+    def hop(self, w):
+        self.copy(0, w).wait_recv()
+        for kind in (1, 2, 5):
+            self.copy(kind, w).start()
+
+    def cross(self, w):
+        for kind in (1, 2):
+            self.copy(kind, w).wait_recv()
+        for kind in (3, 4, 6, 7):
+            self.copy(kind, w).start()
+
+    def close(self, w):
+        for kind in (3, 4):
+            self.copy(kind, w).wait_recv()
+        self.copy(8, w).start()
+
+    def end(self, w):
+        for kind in (5, 6, 7, 8):
+            self.copy(kind, w).wait_recv()
+        for kind in range(KINDS):
+            self.copy(kind, w).wait_send()
+
+
+class Join:
+    def __init__(self, source, theirs, mine, target, local, send, recv, i):
+        tensor = lax.axis_index(TENSOR)
+        rows = source.shape[-2]
+        where = pl.ds(pl.multiple_of(tensor * rows, rows), rows)
+
+        def of(index):
+            return source if index is None else source.at[0, index]
+
+        self.own = pltpu.make_async_copy(of(mine), target.at[where], local.at[i])
+        self.remote = pltpu.make_async_remote_copy(
+            src_ref=of(theirs), dst_ref=target.at[where], send_sem=send.at[i], recv_sem=recv.at[i],
+            device_id={TENSOR: 1 - tensor}, device_id_type=MESH,
+        )
+
+    def start(self):
+        self.remote.start()
+        self.own.start()
+
+    def wait(self):
+        self.remote.wait()
+        self.own.wait()
+
+
+def meet(partners):
+    barrier = pltpu.get_barrier_semaphore()
+    for partner in partners:
+        pl.semaphore_signal(barrier, inc=1, device_id=partner, device_id_type=MESH)
+    pl.semaphore_wait(barrier, len(partners))
+
+
+def gather_kernel(count, layer_input, init_states, *refs):
+    sources, refs = refs[:count], refs[count:]
+    tokens, before, initial = refs[:3]
+    targets = refs[3 : 3 + count]
+    send, recv, local, join_send, join_recv = refs[3 + count :]
+    spread = Spread(sources, targets, send, recv)
+    section, tensor = lax.axis_index(SECTION), lax.axis_index(TENSOR)
+    block, partner = block_of(section, tensor), block_of(section, 1 - tensor)
+    joins = [
+        Join(layer_input, partner, block, tokens, local, join_send, join_recv, 0),
+        Join(
+            layer_input, jnp.maximum(partner - 1, 0), jnp.maximum(block - 1, 0),
+            before, local, join_send, join_recv, 1,
+        ),
+        Join(init_states, None, None, initial, local, join_send, join_recv, 2),
+    ]
+    meet(spread.partners())
+    for w in range(2):
+        spread.begin(w)
+    for w in range(count + 3):
+        if w < count:
+            spread.hop(w)
+        if w + 2 < count:
+            spread.begin(w + 2)
+        elif w + 2 < count + 3:
+            joins[w + 2 - count].start()
+        if 0 <= w - 2 < count:
+            spread.cross(w - 2)
+        if 0 <= w - 3 < count:
+            spread.close(w - 3)
+    for w in range(count):
+        spread.end(w)
+    for join in joins:
+        join.wait()
+
+
+def gather(layer_input, init_states, weights):
+    count = len(weights)
+    rows, width = 2 * layer_input.shape[2], layer_input.shape[3]
+    dma = pltpu.SemaphoreType.DMA
+    anywhere = pl.BlockSpec(memory_space=pl.ANY)
+    shapes = [(rows, width)] * 2 + [(2 * init_states.shape[0], width)] + [w.shape for w in weights]
+    results = pl.pallas_call(
+        functools.partial(gather_kernel, count),
+        in_specs=[anywhere] * (2 + count),
+        out_specs=[anywhere] * (3 + count),
+        out_shape=[jax.ShapeDtypeStruct(s, jnp.bfloat16) for s in shapes],
+        scratch_shapes=[dma((KINDS * count,))] * 2 + [dma((3,))] * 3,
+        compiler_params=params(collective_id=4, has_side_effects=True),
+        cost_estimate=pl.CostEstimate(flops=0, bytes_accessed=200 * 1024 * 1024, transcendentals=0),
+    )(layer_input, init_states, *weights)
+    return results[:3], results[3:]
+
+
+def neighbours():
+    section, tensor = lax.axis_index(SECTION), lax.axis_index(TENSOR)
+    block = block_of(section, tensor)
+
+    return place_of((block + 7) % 8), place_of((block + 1) % 8)
+
+
+def place_of(block):
+    pair = block // 2
+    high = pair // 2
+    return {SECTION: 2 * high + block % 2, TENSOR: (pair + high) % 2}
+
+
+class Scatter:
+    def __init__(self, values, landed, send, recv, local):
+        section, tensor = lax.axis_index(SECTION), lax.axis_index(TENSOR)
+        block = block_of(section, tensor)
+        self.members = [place_of((block + i) % 8) for i in range(1, 8)]
+        rows, width = values[0].shape[0] // 2, values[0].shape[1] // 4
+
+        def piece(value, to):
+            high = pl.multiple_of(to[TENSOR] * rows, rows)
+            left = pl.multiple_of(to[SECTION] * width, width)
+            return value.at[pl.ds(high, rows), pl.ds(left, width)]
+
+        self.copies = [
+            pltpu.make_async_remote_copy(
+                src_ref=piece(value, to), dst_ref=landed.at[j, block],
+                send_sem=send.at[j * 7 + i], recv_sem=recv.at[j * 7 + i],
+                device_id=to, device_id_type=MESH,
+            )
+            for j, value in enumerate(values)
+            for i, to in enumerate(self.members)
+        ]
+        self.own = [
+            pltpu.make_async_copy(
+                piece(value, {SECTION: section, TENSOR: tensor}), landed.at[j, block], local.at[j]
+            )
+            for j, value in enumerate(values)
+        ]
+
+    def start(self):
+        for copy in self.copies + self.own:
+            copy.start()
+
+    def wait(self):
+        for copy in self.copies + self.own:
+            copy.wait()
+
+
+def pass_on(sent, landed, send_sem, recv_sem, slot, part, target):
+    rows = pl.ds(part * CHUNK, CHUNK)
+    return pltpu.make_async_remote_copy(
+        src_ref=sent.at[slot, rows],
+        dst_ref=landed.at[slot, rows],
+        send_sem=send_sem.at[slot, part],
+        recv_sem=recv_sem.at[slot, part],
+        device_id=target,
+        device_id_type=MESH,
+    )
+
+
+def chain_kernel(
+    initial, starts, gain, keep, own, other, sqkv0, sqkv1, sout0, sout1, output_grad,
+    state, hs, ps0, ps1, os0, os1, lse, update, fresh, cotangent,
+    sent, landed, send_sem, recv_sem, local, join_send, join_recv,
+):
+    prior, following = neighbours()
+    section, tensor = lax.axis_index(SECTION), lax.axis_index(TENSOR)
+    join = Join(
+        output_grad, block_of(section, 1 - tensor), block_of(section, tensor),
+        cotangent, local, join_send, join_recv, 0,
+    )
+    meet([prior, following, {TENSOR: 1 - tensor}])
+    join.start()
+    count, width = initial.shape
+    half = os0.shape[1]
+    parts = count // CHUNK
+    state[...] = initial[...]
+
+    def copy(slot, part):
+        return pass_on(sent, landed, send_sem, recv_sem, slot, part, following)
+
+    def one_round(turn, nothing):
+        for part in range(parts):
+            rows = slice(part * CHUNK, (part + 1) * CHUNK)
+
+            @pl.when(turn > 0)
+            def _():
+                slot = turn - 1
+                copy(slot, part).wait_recv()
+                state[rows] = jnp.where(
+                    starts[...] > 0.0, initial[rows], landed[slot, rows].astype(jnp.float32)
+                )
+
+            value = state[rows]
+            hidden = bf(value * inverse_rms(value) * gain[...])
+            hs[rows] = hidden
+            ps0[rows] = bf(nn(hidden, sqkv0[...]))
+            ps1[rows] = bf(nn(hidden, sqkv1[...]))
+
+        def one_head(h, carry):
+            at = [pl.ds(pl.multiple_of(i * half + h * HEAD_DIM, HEAD_DIM), HEAD_DIM) for i in range(3)]
+            for which, (tok, st, mixed) in enumerate(((own, ps0, os0), (other, ps1, os1))):
+                tok_key, tok_value = tok[:, at[1]], with_ones(tok[:, at[2]])
+                key, value = st[:, at[1]], with_ones(st[:, at[2]])
+                for part in range(parts):
+                    rows = slice(part * CHUNK, (part + 1) * CHUNK)
+                    query = st[rows, at[0]]
+                    score_tok, score = nt(query, tok_key), nt(query, key)
+                    top = jnp.maximum(
+                        jnp.max(score_tok, axis=-1, keepdims=True),
+                        jnp.max(score, axis=-1, keepdims=True),
+                    )
+                    mix = nn(bf(jnp.exp2((score_tok - top) * LOG2_SCALE)), tok_value) + nn(
+                        bf(jnp.exp2((score - top) * LOG2_SCALE)), value
+                    )
+                    total = mix[:, HEAD_DIM:]
+                    mixed[rows, at[0]] = bf(mix[:, :HEAD_DIM] / total)
+                    lse[which, h, rows] = top * LOG2_SCALE + jnp.log2(total[:, :1])
+            return carry
+
+        lax.fori_loop(0, half // HEAD_DIM, one_head, 0)
+        for part in range(parts):
+            rows = slice(part * CHUNK, (part + 1) * CHUNK)
+            term = nn(os0[rows], sout0[...]) + nn(os1[rows], sout1[...])
+            update[rows] = term
+            renewed_state = keep[...] * state[rows] + (1.0 - keep[...]) * term
+            fresh[rows] = renewed_state
+
+            @pl.when(turn < CHAIN - 1)
+            def _():
+                sent[turn, rows] = bf(renewed_state)
+                copy(turn, part).start()
+
+        return nothing
+
+    lax.fori_loop(0, CHAIN, one_round, 0)
+    for slot in range(CHAIN - 1):
+        for part in range(parts):
+            copy(slot, part).wait_send()
+    join.wait()
+
+
+def chain(initial, starts, gain, keep, own, other, sqkv0, sqkv1, sout0, sout1, output_grad):
+    count, width = initial.shape
+    half = sout0.shape[0]
+    heads = half // HEAD_DIM
+    bf16, f32 = jnp.bfloat16, jnp.float32
+    vmem, anywhere = pl.BlockSpec(memory_space=pltpu.VMEM), pl.BlockSpec(memory_space=pl.ANY)
+    dma = pltpu.SemaphoreType.DMA
+    parts = count // CHUNK
+    return pl.pallas_call(
+        chain_kernel,
+        in_specs=[vmem] * 10 + [anywhere],
+        out_specs=[vmem] * 9 + [anywhere],
+        out_shape=[
+            jax.ShapeDtypeStruct((count, width), f32),
+            jax.ShapeDtypeStruct((count, width), bf16),
+            jax.ShapeDtypeStruct((count, 3 * half), bf16),
+            jax.ShapeDtypeStruct((count, 3 * half), bf16),
+            jax.ShapeDtypeStruct((count, half), bf16),
+            jax.ShapeDtypeStruct((count, half), bf16),
+            jax.ShapeDtypeStruct((2, heads, count, 1), f32),
+            jax.ShapeDtypeStruct((count, width), f32),
+            jax.ShapeDtypeStruct((count, width), f32),
+            jax.ShapeDtypeStruct((2 * output_grad.shape[2], width), bf16),
+        ],
+        scratch_shapes=[
+            pltpu.VMEM((CHAIN - 1, count, width), bf16),
+            pltpu.VMEM((CHAIN - 1, count, width), bf16),
+            dma((CHAIN - 1, parts)), dma((CHAIN - 1, parts)),
+            dma((1,)), dma((1,)), dma((1,)),
+        ],
+        compiler_params=params(collective_id=1, has_side_effects=True),
+        cost_estimate=pl.CostEstimate(
+            flops=CHAIN * count * width * (8 * width + 8 * count),
+            bytes_accessed=25 * 1024 * 1024,
+            transcendentals=CHAIN * count * count * 4 * heads,
+        ),
+    )(initial, starts, gain, keep, own, other, sqkv0, sqkv1, sout0, sout1, output_grad)
+
+
+def chain_back_kernel(
+    ends, state, update, gain, keep, own, other, ps0, ps1, os0, os1, lse,
+    tok_k0, tok_v0, tok_k1, tok_v1, sqkv0, sqkv1, sout0, sout1, result, ending,
+    grad_state, gproj0, gproj1, gtok0, gtok1, gup, small, scattered,
+    weights, grad_os0, grad_os1, sent, landed, send_sem, recv_sem, piece_send, piece_recv, piece_sem,
+):
+    prior, following = neighbours()
+    scatter = Scatter((result, ending), scattered, piece_send, piece_recv, piece_sem)
+    meet([prior, following] + scatter.members)
+    scatter.start()
+    count, width = state.shape
+    half = os0.shape[1]
+    heads = half // HEAD_DIM
+    parts = count // CHUNK
+    sides = (
+        (own, ps0, os0, tok_k0, tok_v0, gproj0, gtok0, grad_os0),
+        (other, ps1, os1, tok_k1, tok_v1, gproj1, gtok1, grad_os1),
+    )
+
+    def lanes(h):
+        return [pl.ds(pl.multiple_of(i * half + h * HEAD_DIM, HEAD_DIM), HEAD_DIM) for i in range(3)]
+
+    def copy(slot, part):
+        return pass_on(sent, landed, send_sem, recv_sem, slot, part, prior)
+
+    def prepare(h, carry):
+        at = lanes(h)
+        for which, (tok, st, *_) in enumerate(sides):
+            tok_key, key = tok[:, at[1]], st[:, at[1]]
+            for part in range(parts):
+                rows = slice(part * CHUNK, (part + 1) * CHUNK)
+                query, log_total = st[rows, at[0]], lse[which, h, rows]
+                weights[which, h, rows, :count] = bf(
+                    jnp.exp2(nt(query, tok_key) * LOG2_SCALE - log_total)
+                )
+                weights[which, h, rows, count:] = bf(
+                    jnp.exp2(nt(query, key) * LOG2_SCALE - log_total)
+                )
+        return carry
+
+    lax.fori_loop(0, heads, prepare, 0)
+    grad_state[...] = jnp.zeros_like(grad_state)
+
+    def one_round(turn, nothing):
+        for part in range(parts):
+            rows = slice(part * CHUNK, (part + 1) * CHUNK)
+
+            @pl.when(turn > 0)
+            def _():
+                slot = turn - 1
+                copy(slot, part).wait_recv()
+                grad_state[rows] = jnp.where(
+                    ends[...] > 0.0, 0.0, landed[slot, rows].astype(jnp.float32)
+                )
+
+            out = bf((1.0 - keep[...]) * grad_state[rows])
+            gup[rows] = out
+            grad_os0[rows] = bf(nt(out, sout0[...]))
+            grad_os1[rows] = bf(nt(out, sout1[...]))
+
+        def one_head(h, carry):
+            at = lanes(h)
+            for which, (tok, st, mixed, given_k, given_v, gproj, gtok, grad_os) in enumerate(sides):
+                tok_key, tok_value = tok[:, at[1]], tok[:, at[2]]
+                key, value = st[:, at[1]], st[:, at[2]]
+                for part in range(parts):
+                    rows = slice(part * CHUNK, (part + 1) * CHUNK)
+                    query, grad = st[rows, at[0]], grad_os[rows, at[0]]
+                    inner = jnp.sum(
+                        grad.astype(jnp.float32) * mixed[rows, at[0]].astype(jnp.float32),
+                        axis=-1, keepdims=True,
+                    )
+                    p_tok, p = weights[which, h, rows, :count], weights[which, h, rows, count:]
+                    s_tok = bf(p_tok.astype(jnp.float32) * (nt(grad, tok_value) - inner))
+                    s = bf(p.astype(jnp.float32) * (nt(grad, value) - inner))
+                    gproj[rows, at[0]] = bf((nn(s_tok, tok_key) + nn(s, key)) * SCALE)
+                    gk, gv = tn(s, query) * SCALE, tn(p, grad)
+                    if part == 0:
+                        total_k, total_v = gk + given_k[:, at[0]], gv + given_v[:, at[0]]
+                    else:
+                        total_k, total_v = total_k + gk, total_v + gv
+
+                    @pl.when(turn == CHAIN - 1)
+                    def _():
+                        gtk, gtv = tn(s_tok, query) * SCALE, tn(p_tok, grad)
+                        if part == 0:
+                            gtok[:, at[0]], gtok[:, at[1]] = gtk, gtv
+                        else:
+                            gtok[:, at[0]] += gtk
+                            gtok[:, at[1]] += gtv
+
+                gproj[:, at[1]], gproj[:, at[2]] = bf(total_k), bf(total_v)
+            return carry
+
+        lax.fori_loop(0, heads, one_head, 0)
+        for part in range(parts):
+            rows = slice(part * CHUNK, (part + 1) * CHUNK)
+            back = nt(gproj0[rows], sqkv0[...]) + nt(gproj1[rows], sqkv1[...])
+            value, new = state[rows], grad_state[rows]
+            factor = inverse_rms(value)
+            scaled = value * factor
+            through = back * gain[...]
+            leaving = keep[...] * new + factor * (
+                through - scaled * jnp.mean(through * scaled, axis=-1, keepdims=True)
+            )
+
+            @pl.when(turn < CHAIN - 1)
+            def _():
+                sent[turn, rows] = bf(leaving)
+                copy(turn, part).start()
+
+            @pl.when(turn == CHAIN - 1)
+            def _():
+                gain_term = jnp.sum(back * scaled, axis=0, keepdims=True)
+                bias_term = jnp.sum(new * (value - update[rows]), axis=0, keepdims=True) * (
+                    keep[...] * (1.0 - keep[...])
+                )
+                if part == 0:
+                    small[0:1, :], small[1:2, :] = gain_term, bias_term
+                else:
+                    small[0:1, :] += gain_term
+                    small[1:2, :] += bias_term
+                grad_state[rows] = leaving
+
+        return nothing
+
+    lax.fori_loop(0, CHAIN, one_round, 0)
+    for slot in range(CHAIN - 1):
+        for part in range(parts):
+            copy(slot, part).wait_send()
+    scatter.wait()
+
+
+def chain_back(
+    ends, state, update, gain, keep, own, other, ps0, ps1, os0, os1, lse,
+    tok_k0, tok_v0, tok_k1, tok_v1, sqkv0, sqkv1, sout0, sout1, result, ending,
+):
+    count, width = state.shape
+    half = sout0.shape[0]
+    heads = half // HEAD_DIM
+    bf16, f32 = jnp.bfloat16, jnp.float32
+    vmem, anywhere = pl.BlockSpec(memory_space=pltpu.VMEM), pl.BlockSpec(memory_space=pl.ANY)
+    dma = pltpu.SemaphoreType.DMA
+    parts = count // CHUNK
+    rows = own.shape[0]
+    return pl.pallas_call(
+        chain_back_kernel,
+        in_specs=[vmem] * 20 + [anywhere] * 2,
+        out_specs=[vmem] * 7 + [anywhere],
+        out_shape=[
+            jax.ShapeDtypeStruct((count, width), f32),
+            jax.ShapeDtypeStruct((count, 3 * half), bf16),
+            jax.ShapeDtypeStruct((count, 3 * half), bf16),
+            jax.ShapeDtypeStruct((rows, 2 * half), f32),
+            jax.ShapeDtypeStruct((rows, 2 * half), f32),
+            jax.ShapeDtypeStruct((count, width), bf16),
+            jax.ShapeDtypeStruct((2, width), f32),
+            jax.ShapeDtypeStruct((2, 8, rows // 2, width // 4), bf16),
+        ],
+        scratch_shapes=[
+            pltpu.VMEM((2, heads, count, rows + count), bf16),
+            pltpu.VMEM((count, half), bf16),
+            pltpu.VMEM((count, half), bf16),
+            pltpu.VMEM((CHAIN - 1, count, width), bf16),
+            pltpu.VMEM((CHAIN - 1, count, width), bf16),
+            dma((CHAIN - 1, parts)), dma((CHAIN - 1, parts)), dma((14,)), dma((14,)), dma((2,)),
+        ],
+        compiler_params=params(collective_id=2, has_side_effects=True),
+        cost_estimate=pl.CostEstimate(
+            flops=CHAIN * count * width * (16 * width + 16 * count),
+            bytes_accessed=45 * 1024 * 1024,
+            transcendentals=count * count * 4 * heads,
+        ),
+    )(
+        ends, state, update, gain, keep, own, other, ps0, ps1, os0, os1, lse,
+        tok_k0, tok_v0, tok_k1, tok_v1, sqkv0, sqkv1, sout0, sout1, result, ending,
+    )
+
+
+RING = 8
+SHORT_RING = 4
+TILE = 256
+LAGS = (0, 1, 2, 4, 6, 7, 8, 9, 10)
+UP_D, DOWN_D, UP_B, DOWN_B, OUT_C, QKV_C, SOUT_C, SQKV_C, QKV_A, OUT_A = range(10)
+WEIGHTS = (
+    (UP_D, True, 8), (DOWN_D, False, 8), (UP_B, True, 8), (DOWN_B, False, 8), (OUT_C, False, 2),
+    (QKV_C, True, 6), (SOUT_C, False, 2), (SQKV_C, True, 6), (QKV_A, True, 6), (OUT_A, False, 2),
+)
+STARTS = [sum(w[2] for w in WEIGHTS[:i]) for i in range(len(WEIGHTS))]
+PLAIN = sum(w[2] for w in WEIGHTS)
+TILES = PLAIN + 2
+
+
+def grads_kernel(*refs):
+    count = len(WEIGHTS)
+    lefts, panels_own, panels_other = refs[:count], refs[count : 2 * count], refs[2 * count : 3 * count]
+    first, small, rows_out = refs[3 * count : 3 * count + 3]
+    refs = refs[3 * count + 3 :]
+    outs, last_out, landed = refs[:count], refs[count], refs[count + 1]
+    (
+        left, panel, pair, core_in, kept1, first_in, kept2, second_in, kept3, third_in, kept4, fourth_in, result,
+        left_sem, panel_sem, last_sem, core_send, core_recv, first_send, first_recv, second_send, second_recv,
+        send_sem, recv_sem, piece_send, piece_recv, piece_sem,
+    ) = refs[count + 2 :]
+    section, tensor, group = (lax.axis_index(a) for a in (SECTION, TENSOR, DP))
+    core, high = section % 2, section // 2
+    near, far = group % 2, group // 2
+    half, quarter = TILE // 2, TILE // 4
+    other_core = {SECTION: section + 1 - 2 * core}
+    near_group = {DP: group + 1 - 2 * near}
+    far_group = {DP: (group + 2) % 4}
+    scatter = Scatter((rows_out,), landed, piece_send, piece_recv, piece_sem)
+    meet(scatter.members + [near_group, far_group])
+    scatter.start()
+
+    def remote(source, target, sems, recvs, where, partner):
+        return pltpu.make_async_remote_copy(
+            src_ref=source, dst_ref=target, send_sem=sems.at[where], recv_sem=recvs.at[where],
+            device_id=partner, device_id_type=MESH,
+        )
+
+    def left_copy(w):
+        return pltpu.make_async_copy(lefts[w], left.at[w % 3], left_sem.at[w % 3])
+
+    left_copy(0).start()
+
+    def panel_copies(w, k):
+        slot = k % SHORT_RING
+        columns = pl.ds(pl.multiple_of((k - STARTS[w]) * TILE, TILE), TILE)
+        return [
+            pltpu.make_async_copy(source[w].at[:, columns], panel.at[slot, j], panel_sem.at[2 * slot + j])
+            for j, source in enumerate((panels_own, panels_other))
+        ]
+
+    def last_copies(which):
+        slot = (PLAIN + which) % SHORT_RING
+        for i in range(8):
+            s, t = i // 2, i % 2
+            columns = slice(s * TILE, (s + 1) * TILE)
+            source = small.at[:, columns] if which else first.at[t * TILE : (t + 1) * TILE, columns]
+            yield pltpu.make_async_copy(source, pair.at[slot, s % 2, s // 2, t], last_sem.at[i])
+
+    def core_copy(k):
+        slot = k % RING
+        return remote(
+            pair.at[k % SHORT_RING, 1 - core], core_in.at[slot], core_send, core_recv, slot, other_core
+        )
+
+    def order(k):
+        turn = k % 2
+        send = (
+            (1 - turn) * (1 - tensor) + turn * (2 - 2 * high),
+            (1 - turn) * (3 - tensor) + turn * (3 - 2 * high),
+        )
+        keep = (
+            (1 - turn) * tensor + turn * 2 * high,
+            (1 - turn) * (2 + tensor) + turn * (2 * high + 1),
+        )
+        return send, keep, (1 - turn) * high + turn * tensor
+
+    def partner_of(turn):
+        return {
+            SECTION: section * (1 - turn) + ((section + 2) % 4) * turn,
+            TENSOR: tensor + (1 - turn) * (1 - 2 * tensor),
+        }
+
+    def first_copy(k, i):
+        slot = k % RING
+        return remote(
+            kept1.at[k % SHORT_RING, order(k)[0][i]], first_in.at[slot, i], first_send, first_recv,
+            2 * slot + i, partner_of(k % 2),
+        )
+
+    def second_copy(k):
+        slot = k % RING
+        return remote(
+            kept2.at[slot, 1 - order(k)[2]], second_in.at[slot], second_send, second_recv,
+            slot, partner_of(1 - k % 2),
+        )
+
+    def third_copy(k):
+        slot = k % RING
+        return remote(
+            kept3.at[slot, pl.ds((1 - near) * half, half)], third_in.at[slot], send_sem, recv_sem,
+            slot, near_group,
+        )
+
+    def fourth_copy(k):
+        slot = k % RING
+        return remote(
+            kept4.at[slot, pl.ds((1 - far) * quarter, quarter)], fourth_in.at[slot], send_sem, recv_sem,
+            RING + slot, far_group,
+        )
+
+    def back_far(k):
+        rows = pl.ds(near * half + far * quarter, quarter)
+        return remote(
+            result.at[k, rows], result.at[k, rows], send_sem, recv_sem, 2 * RING + k % RING, far_group
+        )
+
+    def back_near(k):
+        rows = pl.ds(near * half, half)
+        return remote(
+            result.at[k, rows], result.at[k, rows], send_sem, recv_sem, 3 * RING + k % RING, near_group
+        )
+
+    def add(a, b):
+        return bf(a.astype(jnp.float32) + b.astype(jnp.float32))
+
+    def fetch(k):
+        for w in range(count):
+
+            @pl.when((k >= STARTS[w]) & (k < STARTS[w] + WEIGHTS[w][2]))
+            def _():
+                for copy in panel_copies(w, k):
+                    copy.start()
+
+            if w + 1 < count:
+
+                @pl.when(k == STARTS[w])
+                def _():
+                    left_copy(w + 1).start()
+
+    def multiply(k):
+        slot = k % SHORT_RING
+
+        @pl.when(k < PLAIN)
+        def _():
+            at = 0
+            for w in range(count):
+                if w:
+                    at = at + jnp.where(k >= STARTS[w], 1, 0)
+
+                @pl.when(k == STARTS[w])
+                def _():
+                    left_copy(w).wait()
+
+            for j, place in enumerate((tensor, 1 - tensor)):
+                pltpu.make_async_copy(
+                    panels_own[0].at[:, :TILE], panel.at[slot, j], panel_sem.at[2 * slot + j]
+                ).wait()
+                product = bf(tn(panel[slot, j], left[at % 3]))
+                for s in range(4):
+                    pair[slot, s % 2, s // 2, place] = product[:, s * TILE : (s + 1) * TILE]
+
+        for which in range(2):
+
+            @pl.when(k == PLAIN + which)
+            def _():
+                for copy in last_copies(which):
+                    copy.start()
+                for copy in last_copies(which):
+                    copy.wait()
+
+        core_copy(k).start()
+
+    def over_cores(k):
+        core_copy(k).wait()
+        for i in range(4):
+            kept1[k % SHORT_RING, i] = add(
+                pair[k % SHORT_RING, core, i // 2, i % 2], core_in[k % RING, i // 2, i % 2]
+            )
+        for i in range(2):
+            first_copy(k, i).start()
+
+    def over_first(k):
+        slot = k % RING
+        for i in range(2):
+            first_copy(k, i).wait()
+        for i in range(2):
+            kept2[slot, i] = add(kept1[k % SHORT_RING, order(k)[1][i]], first_in[slot, i])
+        second_copy(k).start()
+
+    def over_second(k):
+        slot = k % RING
+        second_copy(k).wait()
+        kept3[slot] = add(kept2[slot, order(k)[2]], second_in[slot])
+        third_copy(k).start()
+
+    def over_near(k):
+        slot = k % RING
+        third_copy(k).wait()
+        kept4[slot] = add(kept3[slot, pl.ds(near * half, half)], third_in[slot])
+        fourth_copy(k).start()
+
+    def over_far(k):
+        slot = k % RING
+        fourth_copy(k).wait()
+        result[k, pl.ds(near * half + far * quarter, quarter)] = add(
+            kept4[slot, pl.ds(far * quarter, quarter)], fourth_in[slot]
+        )
+        back_far(k).start()
+
+    def from_far(k):
+        back_far(k).wait()
+        back_near(k).start()
+
+    def from_near(k):
+        back_near(k).wait()
+        for w in range(count):
+
+            @pl.when((k >= STARTS[w]) & (k < STARTS[w] + WEIGHTS[w][2]))
+            def _():
+                at = pl.ds(pl.multiple_of((k - STARTS[w]) * TILE, TILE), TILE)
+                if WEIGHTS[w][1]:
+                    outs[w][:, at] = bf(result[k].astype(jnp.float32).T)
+                else:
+                    outs[w][at, :] = result[k]
+
+        @pl.when(k >= PLAIN)
+        def _():
+            last_out[k - PLAIN] = result[k]
+
+    stages = (
+        fetch, multiply, over_cores, over_first, over_second, over_near, over_far, from_far, from_near
+    )
+
+    def step(i, nothing):
+        for stage, lag in zip(stages, LAGS):
+            k = i - lag
+
+            @pl.when((k >= 0) & (k < TILES))
+            def _():
+                stage(k)
+
+        return nothing
+
+    lax.fori_loop(0, TILES + LAGS[-1], step, 0)
+    scatter.wait()
+
+
+def weight_grads(operands, first, small, rows_out):
+    bf16 = jnp.bfloat16
+    dma = pltpu.SemaphoreType.DMA
+    anywhere, vmem = pl.BlockSpec(memory_space=pl.ANY), pl.BlockSpec(memory_space=pltpu.VMEM)
+    count = len(WEIGHTS)
+    rows, width = operands[WEIGHTS[0][0]][0].shape
+    shapes = [(TILE, n * TILE) if by_rows else (n * TILE, TILE) for _, by_rows, n in WEIGHTS]
+    shapes += [(2, TILE, TILE)]
+    results = pl.pallas_call(
+        grads_kernel,
+        in_specs=[anywhere] * (3 * count + 3),
+        out_specs=[vmem] * (count + 1) + [anywhere],
+        out_shape=[jax.ShapeDtypeStruct(s, bf16) for s in shapes + [(1, 8, TILE, TILE)]],
+        scratch_shapes=[
+            pltpu.VMEM((3, rows, width), bf16),
+            pltpu.VMEM((SHORT_RING, 2, rows, TILE), bf16),
+            pltpu.VMEM((SHORT_RING, 2, 2, 2, TILE, TILE), bf16),
+            pltpu.VMEM((RING, 2, 2, TILE, TILE), bf16),
+            pltpu.VMEM((SHORT_RING, 4, TILE, TILE), bf16),
+            pltpu.VMEM((RING, 2, TILE, TILE), bf16),
+            pltpu.VMEM((RING, 2, TILE, TILE), bf16),
+            pltpu.VMEM((RING, TILE, TILE), bf16),
+            pltpu.VMEM((RING, TILE, TILE), bf16),
+            pltpu.VMEM((RING, TILE // 2, TILE), bf16),
+            pltpu.VMEM((RING, TILE // 2, TILE), bf16),
+            pltpu.VMEM((RING, TILE // 4, TILE), bf16),
+            pltpu.VMEM((TILES, TILE, TILE), bf16),
+            dma((3,)), dma((2 * SHORT_RING,)), dma((8,)),
+            dma((RING,)), dma((RING,)),
+            dma((2 * RING,)), dma((2 * RING,)), dma((RING,)), dma((RING,)),
+            dma((4 * RING,)), dma((4 * RING,)), dma((7,)), dma((7,)), dma((1,)),
+        ],
+        compiler_params=params(collective_id=3, has_side_effects=True),
+        cost_estimate=pl.CostEstimate(
+            flops=2 * 8 * TILES * TILE * TILE * rows,
+            bytes_accessed=40 * TILES * TILE * TILE,
+            transcendentals=0,
+        ),
+    )(*(operands[w[0]][i] for i in range(3) for w in WEIGHTS), first, small, rows_out)
+    shares = {w[0]: r for w, r in zip(WEIGHTS, results)}
+    return shares, results[count], results[count + 1]
+
+
+def gelu_back(values, grad):
+    return jax.vjp(smooth, values)[1](grad)[0]
+
+
+def block_body(
+    layer_input, output_grad, seg_blocks, seg_group, gain_a, wqkv_a, wout_a, gain_b, up_b, down_b,
+    gain_c, gain_s, wqkv_c, sqkv_c, wout_c, sout_c, gate_bias, init_states, gain_d, up_d, down_d,
+):
+    sections, tensors = lax.axis_size(SECTION), lax.axis_size(TENSOR)
+    block_count, shard_rows, width = layer_input.shape[1:]
+    rows = shard_rows * tensors
+    section, tensor = lax.axis_index(SECTION), lax.axis_index(TENSOR)
+    block = block_of(section, tensor)
+    begins, closes, lively, numbers = layout(
+        seg_blocks, seg_group, lax.axis_index(DP), block_count
+    )
+    alive = lively[block]
+    starts = begins[block] | jnp.logical_not(alive)
+    ends = closes[block] | jnp.logical_not(alive)
+    opening = starts.astype(jnp.int32)[None]
+    f32 = jnp.float32
+    ga, gb, gc, gd = (v.astype(f32) for v in (gain_a, gain_b, gain_c, gain_d))
+
+    def in_order(own, other):
+        low = jnp.where(tensor == 0, own, other)
+        high = jnp.where(tensor == 0, other, own)
+        return low, high
+
+    def other_half(weight):
+        size = weight.shape[0] // sections
+        piece = lax.dynamic_slice_in_dim(weight, section * size, size, 0)
+        landed = lax.ppermute(piece, TENSOR, SWAP)
+        return lax.all_gather(landed, SECTION, axis=0, tiled=True)
+
+    def flat(weight):
+        return jnp.concatenate([weight[:, i] for i in range(3)], axis=1)
+
+    wqkv_a0, wqkv_c0, sqkv_c0 = flat(wqkv_a), flat(wqkv_c), flat(sqkv_c)
+    (tokens, before, initial), others = gather(
+        layer_input, init_states,
+        (wqkv_a0, wout_a, up_b, down_b, wqkv_c0, sqkv_c0, sout_c, wout_c),
+    )
+    wqkv_a1, wout_a1, up_b1, down_b1, wqkv_c1, sqkv_c1, sout_c1, wout_c1 = others
+    tokens, late_up, late_down = lax.optimization_barrier((tokens, up_d, down_d))
+    up_d1, down_d1 = other_half(late_up), other_half(late_down)
+    initial = initial.astype(f32)
+
+    def normed(values, gain):
+        return bf(values * inverse_rms(values) * gain)
+
+    def dot(a, b):
+        return jnp.dot(a, b, preferred_element_type=f32)
+
+    def dot_t(a, b):
+        return lax.dot_general(a, b, (((1,), (1,)), ((), ())), preferred_element_type=f32)
+
+    half = wout_a.shape[0]
+    r0 = tokens.astype(f32)
+    h0 = normed(r0, ga)
+    h_before = normed(before.astype(f32), ga)
+    pa0, pa1 = bf(dot(h0, wqkv_a0)), bf(dot(h0, wqkv_a1))
+    prior_a0 = bf(dot(h_before, wqkv_a0[:, half:]))
+    prior_a1 = bf(dot(h_before, wqkv_a1[:, half:]))
+    oa0, lse_a0 = attend(opening, pa0, prior_a0)
+    oa1, lse_a1 = attend(opening, pa1, prior_a1)
+    r1 = r0 + (dot(oa0, wout_a) + dot(oa1, wout_a1))
+
+    h1 = normed(r1, gb)
+    ub0, ub1 = dot(h1, up_b), dot(h1, up_b1)
+    ab0, ab1 = bf(smooth(ub0)), bf(smooth(ub1))
+    r2 = r1 + (dot(ab0, down_b) + dot(ab1, down_b1))
+
+    h2 = normed(r2, gc)
+    pc0, pc1 = bf(dot(h2, wqkv_c0)), bf(dot(h2, wqkv_c1))
+    halo = lax.ppermute(jnp.stack(in_order(pc0[:, half:], pc1[:, half:])), GROUP, TO_NEXT)
+    prior_c0, prior_c1 = in_order(halo[0], halo[1])
+
+    retain = jax.nn.sigmoid(gate_bias.astype(f32))[None, :]
+    state_gain = gain_s.astype(f32)[None, :]
+
+    def flag(value):
+        return jnp.broadcast_to(value.astype(f32), (1, width))
+
+    (
+        state_in, hs, ps0, ps1, os0, os1, lse_s, update, state_new, cotangent
+    ) = chain(
+        initial, flag(starts), state_gain, retain, pc0, pc1,
+        sqkv_c0, sqkv_c1, sout_c, sout_c1, output_grad,
+    )
+    oc0, lse_c0 = attend(opening, pc0, prior_c0, ps0)
+    oc1, lse_c1 = attend(opening, pc1, prior_c1, ps1)
+    r3 = r2 + (dot(oc0, wout_c) + dot(oc1, wout_c1))
+
+    h3 = normed(r3, gd)
+    ud0, ud1 = dot(h3, up_d), dot(h3, up_d1)
+    ad0, ad1 = bf(smooth(ud0)), bf(smooth(ud1))
+    r4 = r3 + (dot(ad0, down_d) + dot(ad1, down_d1))
+    result = bf(jnp.where(alive, r4, 0.0))
+
+    def feed_back(up_name, down_name, grad, values, h, gain, u0, u1, a0, a1, up0, up1, down0, down1):
+        gy = bf(grad)
+        g0 = bf(gelu_back(u0, dot_t(gy, down0)))
+        g1 = bf(gelu_back(u1, dot_t(gy, down1)))
+        operands[down_name] = (gy, a0, a1)
+        operands[up_name] = (h, g0, g1)
+        through = dot_t(g0, up0) + dot_t(g1, up1)
+        back, gain_grad = norm_back(values, gain, through)
+        return grad + back, gain_grad
+
+    operands = {}
+    grad4 = jnp.where(alive, cotangent.astype(f32), 0.0)
+    grad3, gain_d_grad = feed_back(
+        UP_D, DOWN_D, grad4, r3, h3, gd, ud0, ud1, ad0, ad1, up_d, up_d1, down_d, down_d1
+    )
+    gy3 = bf(grad3)
+    tok0 = attend_back(opening, pc0, prior_c0, bf(dot_t(gy3, wout_c)), oc0, lse_c0, ps0)
+    tok1 = attend_back(opening, pc1, prior_c1, bf(dot_t(gy3, wout_c1)), oc1, lse_c1, ps1)
+
+    def halo_back(one, two):
+        pair = in_order(
+            jnp.concatenate([one[3], one[4]], axis=1), jnp.concatenate([two[3], two[4]], axis=1)
+        )
+        back = lax.ppermute(jnp.stack(pair), GROUP, TO_PRIOR).astype(f32)
+        return in_order(back[0], back[1])
+
+    halo_c0, halo_c1 = halo_back(tok0, tok1)
+    grad_state, gs0, gs1, gtok0, gtok1, gup, small, landed = chain_back(
+        flag(ends), state_in, update, state_gain, retain, pc0, pc1, ps0, ps1, os0, os1, lse_s,
+        tok0[5], tok0[6], tok1[5], tok1[6], sqkv_c0, sqkv_c1, sout_c, sout_c1, result, bf(state_new),
+    )
+
+    def projected_back(parts, halo_part, extra=None):
+        pair = jnp.concatenate([parts[1], parts[2]], axis=1) + halo_part
+        if extra is not None:
+            pair = pair + extra
+        return jnp.concatenate([parts[0], bf(pair)], axis=1)
+
+    gc0 = projected_back(tok0, halo_c0, gtok0)
+    gc1 = projected_back(tok1, halo_c1, gtok1)
+    operands[QKV_C] = (h2, gc0, gc1)
+    operands[SQKV_C] = (hs, gs0, gs1)
+    operands[OUT_C] = (gy3, oc0, oc1)
+    operands[SOUT_C] = (gup, os0, os1)
+    first_grad = bf(jnp.where(begins[block], grad_state, 0.0))
+    def through_qkv(g, w):
+        return dot_t(g, w)
+
+    back_c, gain_c_grad = norm_back(
+        r2, gc, through_qkv(gc0, wqkv_c0) + through_qkv(gc1, wqkv_c1)
+    )
+    grad2 = grad3 + back_c
+
+    grad1, gain_b_grad = feed_back(
+        UP_B, DOWN_B, grad2, r1, h1, gb, ub0, ub1, ab0, ab1, up_b, up_b1, down_b, down_b1
+    )
+
+    gy1 = bf(grad1)
+    att0 = attend_back(opening, pa0, prior_a0, bf(dot_t(gy1, wout_a)), oa0, lse_a0)
+    att1 = attend_back(opening, pa1, prior_a1, bf(dot_t(gy1, wout_a1)), oa1, lse_a1)
+    halo_a0, halo_a1 = halo_back(att0, att1)
+    ga0, ga1 = projected_back(att0, halo_a0), projected_back(att1, halo_a1)
+    operands[QKV_A] = (h0, ga0, ga1)
+    operands[OUT_A] = (gy1, oa0, oa1)
+    back_a, gain_a_grad = norm_back(
+        r0, ga, through_qkv(ga0, wqkv_a0) + through_qkv(ga1, wqkv_a1)
+    )
+    smalls = jnp.stack(
+        [gain_a_grad, gain_b_grad, gain_c_grad, small[0], gain_d_grad, small[1]]
+    )
+    shares, last_share, landed_input = weight_grads(
+        operands, first_grad, jnp.pad(bf(smalls), ((0, TILE - 6), (0, 0))), bf(grad1 + back_a)
+    )
+    small_share = last_share[1].astype(f32)
+    chosen = (
+        (numbers[:, None] == jnp.arange(SLOTS, dtype=jnp.int32)[None, :])
+        & (closes & lively)[:, None]
+    )
+    state_tiles = landed[1].astype(f32)
+    final_share = jnp.stack(
+        [
+            jnp.sum(jnp.where(chosen[:, i, None, None], state_tiles, 0.0), axis=0)
+            for i in range(SLOTS)
+        ],
+        axis=1,
+    )
+
+    def share(name):
+        value = shares[name].astype(f32)
+        return value.reshape(value.shape[0], 3, -1) if name in (QKV_A, QKV_C, SQKV_C) else value
+
+    return (
+        landed[0][None],
+        final_share[None],
+        landed_input.astype(f32),
+        small_share[0],
+        share(QKV_A),
+        share(OUT_A),
+        small_share[1],
+        share(UP_B),
+        share(DOWN_B),
+        small_share[2],
+        small_share[3],
+        share(QKV_C),
+        share(SQKV_C),
+        share(OUT_C),
+        share(SOUT_C),
+        small_share[5],
+        last_share[0].astype(f32),
+        small_share[4],
+        share(UP_D),
+        share(DOWN_D),
+    )
+
+
+def chosen(*arrays):
+    devices = (lax.axis_size(SECTION), lax.axis_size(TENSOR), lax.axis_size(DP))
+    if devices == (4, 2, 4) and arrays[0].shape[1] == 8:
+        return block_body(*arrays)
+    return relay_body(*arrays)
+
+
 def solution(mesh):
     in_specs = (
-        P("dp", None, "tensor", None),
-        P("dp", None, "tensor", None),
+        P(DP, None, TENSOR, None),
+        P(DP, None, TENSOR, None),
         P(),
         P(),
         P(),
-        P(None, None, "tensor"),
-        P("tensor", None),
+        P(None, None, TENSOR),
+        P(TENSOR, None),
         P(),
-        P(None, "tensor"),
-        P("tensor", None),
+        P(None, TENSOR),
+        P(TENSOR, None),
         P(),
         P(),
-        P(None, None, "tensor"),
-        P(None, None, "tensor"),
-        P("tensor", None),
-        P("tensor", None),
+        P(None, None, TENSOR),
+        P(None, None, TENSOR),
+        P(TENSOR, None),
+        P(TENSOR, None),
         P(),
-        P("tensor", None),
+        P(TENSOR, None),
         P(),
-        P(None, "tensor"),
-        P("tensor", None),
+        P(None, TENSOR),
+        P(TENSOR, None),
     )
     out_specs = (
-        P("dp", None, "tensor", "section"),
-        P("dp", "tensor", None, "section"),
-        P("dp", None, "tensor", "section"),
-        P("section"),
-        P("section", None, "tensor"),
-        P("tensor", "section"),
-        P("section"),
-        P("section", "tensor"),
-        P("tensor", "section"),
-        P("section"),
-        P("section"),
-        P("section", None, "tensor"),
-        P("section", None, "tensor"),
-        P("tensor", "section"),
-        P("tensor", "section"),
-        P("section"),
-        P("tensor", "section"),
-        P("section"),
-        P("section", "tensor"),
-        P("tensor", "section"),
-    )
-    return jax.shard_map(body, mesh=mesh, in_specs=in_specs, out_specs=out_specs, check_vma=False)
+        P(DP, None, TENSOR, SECTION),
+        P(DP, TENSOR, None, SECTION),
+        P(DP, None, TENSOR, SECTION),
+        P(SECTION),
+        P(SECTION, None, TENSOR),
+        P(TENSOR, SECTION),
+        P(SECTION),
+        P(SECTION, TENSOR),
+        P(TENSOR, SECTION),
+        P(SECTION),
+        P(SECTION),
+        P(SECTION, None, TENSOR),
+        P(SECTION, None, TENSOR),
+        P(TENSOR, SECTION),
+        P(TENSOR, SECTION),
+        P(SECTION),
+        P(TENSOR, SECTION),
+        P(SECTION),
+        P(SECTION, TENSOR),
+        P(TENSOR, SECTION),
+    )
+    return jax.shard_map(chosen, mesh=mesh, in_specs=in_specs, out_specs=out_specs, check_vma=False)

time: 5730 us -> 975 us (0.17)
  waiting for transfers between devices: 2680 us -> 6.36 us
  local copies, waits for them, and re-layouts: 1150 us -> 43.1 us
  other arithmetic: 863 us -> 57.8 us
  Pallas kernels: 0 us -> 724 us
  matrix products: 620 us -> 110 us
  loops' own time: 290 us -> 0 us
    reduce_scatter x59 -> x0, waiting for transfers between devices: 1640 us -> none  [the longest x11 699 us: backward_tick(): lax.psum_scatter(grad_normed_tok.astype(jnp.bfloat16), 'tensor', scatter_...]
    all_gather x44 -> x2, waiting for transfers between devices: 771 us -> 0.01 us  [other_half(): return lax.all_gather(landed, SECTION, axis=0, tiled=True)]
    pallas_call x0 -> x12, Pallas kernels: none -> 724 us  [the longest x1 315 us: weight_grads(): pl.pallas_call(grads_kernel, in_specs=[anywhere] * (3 * count + 3), out_s...]
    dot_general x143 -> x34, matrix products: 620 us -> 110 us  [the longest x18 58.8 us: dot(): return jnp.dot(a, b, preferred_element_type=f32)]
    another operation x112 -> x5, local copies, waits for them, and re-layouts: 384 us -> 0.07 us  [block_body(): jnp.stack([gain_a_grad, gain_b_grad, gain_c_grad, small[0], gain_d_grad,...]
    dynamic_slice x199 -> x5, local copies, waits for them, and re-layouts: 305 us -> 6.43 us  [the longest x2 4.66 us: other_half(): piece = lax.dynamic_slice_in_dim(weight, section * size, size, 0)]
    another operation x24 -> x0, loops' own time: 290 us -> none  [the longest x11 195 us: backward_tick(): lax.switch(section_index, backward_branches, grad_tok, grad_st, tok_norme...]
    psum x1 -> x0, waiting for transfers between devices: 265 us -> none  [body(): lax.psum(grad_qkv_a.astype(jnp.bfloat16), 'dp').astype(jnp.float32)]
  transfers between devices with their start and end apart: 126 -> 7, of which waited for: 100 -> 1; matrix products, arithmetic and copies ran while one was open for 18% -> 9% of each run, Pallas kernels for 0% -> 25%
where the time goes in v2:
time: 975 us; the launch traced here: 966 us
  Pallas kernels  724 us (74%)
  matrix products  110 us (11%)
  other arithmetic  57.8 us (6%)
  local copies, waits for them, and re-layouts  43.1 us (4%)
  between operations  18.2 us (2%)
    pallas_call x1, Pallas kernels, weight_grads(): pl.pallas_call(grads_kernel, in_specs=[anywhere] * (3 * count + 3), out_s...  315 us
    pallas_call x1, Pallas kernels, gather(): pl.pallas_call(functools.partial(gather_kernel, count), in_specs=[anywher...  125 us
    pallas_call x1, Pallas kernels, chain_back(): pl.pallas_call(chain_back_kernel, in_specs=[vmem] * 20 + [anywhere] * 2,...  120 us
    pallas_call x1, Pallas kernels, chain(): pl.pallas_call(chain_kernel, in_specs=[vmem] * 10 + [anywhere], out_specs...  97.8 us
    dot_general x18, matrix products, dot(): return jnp.dot(a, b, preferred_element_type=f32)  58.8 us
    dot_general x16, matrix products, dot_t(): lax.dot_general(a, b, (((1,), (1,)), ((), ())), preferred_element_type=f32)  50.8 us
    pallas_call x4, Pallas kernels, attend_back(): pl.pallas_call(functools.partial(attend_back_kernel, states is not None),...  39.3 us
    unnamed x299, local copies, waits for them, and re-layouts  29.5 us
  transfers between devices with their start and end apart: 7, of which 1 were waited for; matrix products, arithmetic and copies ran while one was open for 9% of the time, Pallas kernels for 25%

profile of v2, /device:TPU:0, one launch (start us, length us, event | category | flops | bytes accessed | tf_op | source)
XLA Modules:
  0.0 966.3 jit_solution(13010238822739513919)
XLA Ops:
  18.6 124.6 %shard_map.356 = (bf16[512,1024]{1,0:T(8,128)(2,1)}, bf16[512,1024]{1,0:T(8,128)(2,1)}, bf16[512,1024]{1,0:T(8,128)(2,1)}, bf16[1024,1536]{1,0:T(8,128)(2,1)}, b...) custom-call(bf16[1,8,256,1024]{3,2,1,0:T(8,128)(2,1)} %layer_input.1, ...), custom_call_target="tpu_custom_call" | custom-call | bytes 209715200 | tf_op jit(solution)/shard_map/pallas_call | solution.py:1164
  155.2 2.9 convolution_convert_fusion.3.refs_1_.refs_2_.refs_3_
  160.8 6.2 shard_map.357
  167.0 4.0 fusion.59.refs_4_.refs_5_
  171.0 2.9 convolution_convert_fusion.2.refs_1_.refs_2_.refs_3_
  174.0 6.1 shard_map.358
  185.2 5.1 multiply_convert_fusion.3
  193.3 5.1 multiply_convert_fusion.2
  215.8 97.8 %shard_map.359 = (f32[512,1024]{1,0:T(8,128)}, bf16[512,1024]{1,0:T(8,128)(2,1)}, bf16[512,1536]{1,0:T(8,128)(2,1)}, bf16[512,1536]{1,0:T(8,128)(2,1)}, bf16[512...) custom-call(f32[512,1024]{1,0:T(8,128)} %convert_element_type.197.in, ...), custom_call_target="tpu_custom_call" | custom-call | flops 25769803776 | bytes 26214400 | tf_op jit(solution)/shard_map/pallas_call | solution.py:1328
  318.6 4.4 fusion.88
  324.5 7.5 shard_map.360
  332.1 7.7 shard_map.361
  345.2 5.3 multiply_convert_fusion.1
  350.5 3.7 fusion.89
  355.0 3.7 fusion.91
  358.7 6.9 fusion.90
  365.6 10.2 %multiply_convert_fusion = (bf16[512,2048]{1,0:T(8,128)(2,1)}, bf16[512,2048]{1,0:T(8,128)(2,1)S(1)}) fusion(f32[512,2048]{1,0:T(8,128)} %fusion.90, bf16[512,1024]{1,0:T(8,128)(2,1)} %copy-done.64, bf16[1024,2048]{1,0:T(8,128)(2,1)} %all-gather.5.cloned.1.call-done), kind=kOutput, calls=%fused_computation.36 | convolution fusion | flops 2170552320 | bytes 13631488 | tf_op jit(solution)/shard_map/dot_general | solution.py:1884
  375.8 3.0 multiply_reduce_fusion
  384.0 11.4 %shard_map.362 = (bf16[512,512]{1,0:T(8,128)(2,1)}, f32[512,512]{1,0:T(8,128)}, f32[512,512]{1,0:T(8,128)}, bf16[512,512]{1,0:T(8,128)(2,1)}, bf16[512,512]{1,0:...) custom-call(s32[1]{0:T(128)} %bitcast.16.refs_0_, bf16[512,1536]{1,0:T(8,128)(2,1)} %copy-done, ...), custom_call_target="tpu_custom_call" | custom-call | flops 4026531840 | bytes 12582912 | tf_op jit(solution)/shard_map/pallas_call | solution.py:1009
  395.4 11.4 %shard_map.363 = (bf16[512,512]{1,0:T(8,128)(2,1)}, f32[512,512]{1,0:T(8,128)}, f32[512,512]{1,0:T(8,128)}, bf16[512,512]{1,0:T(8,128)(2,1)}, bf16[512,512]{1,0:...) custom-call(s32[1]{0:T(128)} %bitcast.16.refs_0_, bf16[512,1536]{1,0:T(8,128)(2,1)} %copy-done.1, ...), custom_call_target="tpu_custom_call" | custom-call | flops 4026531840 | bytes 12582912 | tf_op jit(solution)/shard_map/pallas_call | solution.py:1009
  412.0 4.1 select_convert_fusion.1.result
  416.7 120.1 %shard_map.364 = (f32[512,1024]{1,0:T(8,128)}, bf16[512,1536]{1,0:T(8,128)(2,1)}, bf16[512,1536]{1,0:T(8,128)(2,1)}, f32[512,1024]{1,0:T(8,128)}, f32[512,1024]{...) custom-call(f32[1,1024]{1,0:T(1,128)} %broadcast_in_dim.107.ends, ...), custom_call_target="tpu_custom_call" | custom-call | flops 51539607552 | bytes 47185920 | tf_op jit(solution)/shard_map/pallas_call | solution.py:1504
  540.2 3.2 fusion.51
  543.5 4.5 fusion.79
  554.1 4.7 fusion.6.refs_12_
  563.1 4.9 fusion.13.refs_22_
  575.2 8.2 shard_map.366
  583.4 8.3 shard_map.365
  603.4 6.3 collective-permute-done.4
  618.1 3.4 fusion.37
  622.4 3.1 fusion.41.refs_32_
  625.5 315.0 %shard_map.367 = (bf16[256,2048]{1,0:T(8,128)(2,1)}, bf16[2048,256]{1,0:T(8,128)(2,1)}, bf16[256,2048]{1,0:T(8,128)(2,1)}, bf16[2048,256]{1,0:T(8,128)(2,1)}, bf...) custom-call(bf16[512,1024]{1,0:T(8,128)(2,1)} %copy-done.64, ...), custom_call_target="tpu_custom_call" | custom-call | flops 31138512896 | bytes 152043520 | tf_op jit(solution)/shard_map/pallas_call | solution.py:1798
  (419 shorter events, 132.3 us)
Async XLA Ops:
  7.2 351.5 %all-gather.3.cloned.1.call-start = ((), (), s32[]{:S(2)}) async-start(), calls=%async_computation | async-start | bytes 5242880 | tf_op jit(solution)/shard_map/all_gather | solution.py:1865
  10.1 144.5 %copy-start.24 = (bf16[1024,512]{1,0:T(8,128)(2,1)}, bf16[1024,512]{1,0:T(8,128)(2,1)S(1)}, u32[]{:S(2)}) copy-start(bf16[1024,512]{1,0:T(8,128)(2,1)S(1)} %get-tuple-element.268) | copy-start | bytes 3145732
  10.1 148.4 %copy-start.26 = (bf16[1024,512]{1,0:T(8,128)(2,1)}, bf16[1024,512]{1,0:T(8,128)(2,1)S(1)}, u32[]{:S(2)}) copy-start(bf16[1024,512]{1,0:T(8,128)(2,1)S(1)} %get-tuple-element.269) | copy-start | bytes 3145732
  143.2 6.9 copy-start.120
  143.2 10.7 %copy-start.113 = (bf16[1024]{0:T(1024)(128)(2,1)S(1)}, bf16[1024]{0:T(1024)(128)(2,1)}, u32[]{:S(2)}) copy-start(bf16[1024]{0:T(1024)(128)(2,1)} %param.25) | copy-start | bytes 6148
  143.2 10.7 %copy-start.7 = (bf16[512,1024]{1,0:T(8,128)(2,1)S(1)}, bf16[512,1024]{1,0:T(8,128)(2,1)}, u32[]{:S(2)}) copy-start(bf16[512,1024]{1,0:T(8,128)(2,1)} %get-tuple-element.98) | copy-start | bytes 3145732
  145.6 34.5 %collective-permute-start.1 = (bf16[512,1024]{1,0:T(8,128)(2,1)}, bf16[512,1024]{1,0:T(8,128)(2,1)}, u32[]{:S(2)}, u32[]{:S(2)}) collective-permute-start(bf16[512,1024]{1,0:T(8,128)(2,1)} %constant_dynamic-slice_fusion.1), channel_id=1, source_target_pairs={{0,1},{1,0},{2,3},{3,2},{4,5},{5,4},{6,7},{7,6},{8,9},{9,8},{10,11... | collective-permute-start | bytes 3145736 | tf_op jit(solution)/shard_map/ppermute | solution.py:1864
  149.0 66.1 %collective-permute-start.2 = (bf16[256,2048]{1,0:T(8,128)(2,1)}, bf16[256,2048]{1,0:T(8,128)(2,1)}, u32[]{:S(2)}, u32[]{:S(2)}) collective-permute-start(bf16[256,2048]{1,0:T(8,128)(2,1)} %constant_dynamic-slice_fusion), channel_id=1, source_target_pairs={{0,1},{1,0},{2,3},{3,2},{4,5},{5,4},{6,7},{7,6},{8,9},{9,8},{10,11... | collective-permute-start | bytes 3145736 | tf_op jit(solution)/shard_map/ppermute | solution.py:1864
  149.9 8.2 copy-start.106
  150.3 7.8 copy-start.109
  150.8 7.3 copy-start.111
  150.9 162.6 %copy-start.123 = (pred[8]{0:T(512)(128)(4,1)}, pred[8]{0:T(512)(128)(4,1)S(1)}, u32[]{:S(2)}) copy-start(pred[8]{0:T(512)(128)(4,1)S(1)} %get-tuple-element.245) | copy-start | bytes 28
  154.0 13.0 %copy-start.96 = (f32[1024]{0:T(1024)}, f32[1024]{0:T(1024)S(1)}, u32[]{:S(2)}) copy-start(f32[1024]{0:T(1024)S(1)} %convert_element_type.201) | copy-start | bytes 12292
  160.8 22.5 %copy-start.98 = (f32[1024]{0:T(1024)}, f32[1024]{0:T(1024)S(1)}, u32[]{:S(2)}) copy-start(f32[1024]{0:T(1024)S(1)} %convert_element_type.209) | copy-start | bytes 12292
  160.8 40.2 %copy-start.94 = (f32[1024]{0:T(1024)}, f32[1024]{0:T(1024)S(1)}, u32[]{:S(2)}) copy-start(f32[1024]{0:T(1024)S(1)} %convert_element_type.213) | copy-start | bytes 12292
  180.1 185.4 %all-gather.5.cloned.1.call-start = ((), (), s32[]{:S(2)}) async-start(), calls=%async_computation.1 | async-start | bytes 5242880 | tf_op jit(solution)/shard_map/all_gather | solution.py:1865
  183.2 15.2 %copy-start.5 = (f32[512,1024]{1,0:T(8,128)}, f32[512,1024]{1,0:T(8,128)S(1)}, u32[]{:S(2)}) copy-start(f32[512,1024]{1,0:T(8,128)S(1)} %get-tuple-element.294) | copy-start | bytes 6291460
  183.2 7.1 copy-start.104
  185.2 7.5 copy-start.62
  210.8 112.2 %collective-permute-start = (bf16[2,512,1024]{2,1,0:T(8,128)(2,1)}, bf16[2,512,1024]{2,1,0:T(8,128)(2,1)S(1)}, u32[]{:S(2)}, u32[]{:S(2)}) collective-permute-start(bf16[2,512,1024]{2,1,0:T(8,128)(2,1)} %pad_maximum_fusion.3), channel_id=1, source_target_pairs={{0,8},{8,1},{1,9},{9,17},{17,25},{25,16},{16,24},{2,10},{10,3},{3,... | collective-permute-start | bytes 6291464 | tf_op jit(solution)/shard_map/ppermute | solution.py:1907
  215.8 99.0 %copy-start.118 = (bf16[1024]{0:T(1024)(128)(2,1)S(1)}, bf16[1024]{0:T(1024)(128)(2,1)}, u32[]{:S(2)}) copy-start(bf16[1024]{0:T(1024)(128)(2,1)} %param.39) | copy-start | bytes 6148
  332.0 7.7 copy-start.16
  332.1 7.7 copy-start.76
  365.6 10.2 %copy-start.131 = (bf16[1024,2048]{1,0:T(8,128)(2,1)S(1)}, bf16[1024,2048]{1,0:T(8,128)(2,1)}, u32[]{:S(2)}) copy-start(bf16[1024,2048]{1,0:T(8,128)(2,1)} %all-gather.5.cloned.1.call-done) | copy-start | bytes 12582916
  365.6 10.2 %copy-start.138 = (f32[512,1024]{1,0:T(8,128)S(1)}, f32[512,1024]{1,0:T(8,128)}, u32[]{:S(2)}) copy-start(f32[512,1024]{1,0:T(8,128)} %fusion.89) | copy-start | bytes 6291460
  395.4 11.4 %copy-start.78 = (bf16[512,512]{1,0:T(8,128)(2,1)S(1)}, bf16[512,512]{1,0:T(8,128)(2,1)}, u32[]{:S(2)}) copy-start(bf16[512,512]{1,0:T(8,128)(2,1)} %get-tuple-element.133) | copy-start | bytes 1572868
  410.4 126.4 %collective-permute-start.3 = (bf16[2,512,1024]{2,1,0:T(8,128)(2,1)}, bf16[2,512,1024]{2,1,0:T(8,128)(2,1)}, u32[]{:S(2)}, u32[]{:S(2)}) collective-permute-start(bf16[2,512,1024]{2,1,0:T(8,128)(2,1)} %pad_maximum_fusion.4), channel_id=1, source_target_pairs={{8,0},{1,8},{9,1},{17,9},{25,17},{16,25},{24,16},{10,2},{3,10},{11... | collective-permute-start | bytes 6291464 | tf_op jit(solution)/shard_map/ppermute | solution.py:1955
  552.5 8.7 copy-start.52
  583.4 8.3 copy-start.79
  583.4 8.3 copy-start.80
  593.8 16.0 %collective-permute-start.4 = (bf16[2,512,1024]{2,1,0:T(8,128)(2,1)S(1)}, bf16[2,512,1024]{2,1,0:T(8,128)(2,1)S(1)}, u32[]{:S(2)}, u32[]{:S(2)}) collective-permute-start(bf16[2,512,1024]{2,1,0:T(8,128)(2,1)S(1)} %pad_maximum_fusion.5), channel_id=1, source_target_pairs={{8,0},{1,8},{9,1},{17,9},{25,17},{16,25},{24,16},{10,2},{3,10},{11... | collective-permute-start | bytes 6291464 | tf_op jit(solution)/shard_map/ppermute | solution.py:1955
  603.4 6.8 copy-start.71
  (123 other events, 385.3 us)
Sparse Core Ops, SparseCore 0:
  180.3 36.1 all-gather.2
  218.0 42.2 all-gather.4

commit v3 on v2

--- a/solution.py
+++ b/solution.py
@@ -1023,6 +1023,7 @@
 
 
 KINDS = 9
+FLIGHT = 4
 
 
 class Spread:
@@ -1136,15 +1137,18 @@
         Join(init_states, None, None, initial, local, join_send, join_recv, 2),
     ]
     meet(spread.partners())
-    for w in range(2):
-        spread.begin(w)
+    def begin(i):
+        if i < count:
+            spread.begin(i)
+        elif i < count + len(joins):
+            joins[i - count].start()
+
+    for i in range(FLIGHT):
+        begin(i)
     for w in range(count + 3):
         if w < count:
             spread.hop(w)
-        if w + 2 < count:
-            spread.begin(w + 2)
-        elif w + 2 < count + 3:
-            joins[w + 2 - count].start()
+        begin(w + FLIGHT)
         if 0 <= w - 2 < count:
             spread.cross(w - 2)
         if 0 <= w - 3 < count:
@@ -1256,7 +1260,7 @@
     def copy(slot, part):
         return pass_on(sent, landed, send_sem, recv_sem, slot, part, following)
 
-    def one_round(turn, nothing):
+    def work(turn):
         for part in range(parts):
             rows = slice(part * CHUNK, (part + 1) * CHUNK)
 
@@ -1295,7 +1299,7 @@
                     lse[which, h, rows] = top * LOG2_SCALE + jnp.log2(total[:, :1])
             return carry
 
-        lax.fori_loop(0, half // HEAD_DIM, one_head, 0)
+        lax.fori_loop(0, half // HEAD_DIM, one_head, 0, unroll=True)
         for part in range(parts):
             rows = slice(part * CHUNK, (part + 1) * CHUNK)
             term = nn(os0[rows], sout0[...]) + nn(os1[rows], sout1[...])
@@ -1308,12 +1312,20 @@
                 sent[turn, rows] = bf(renewed_state)
                 copy(turn, part).start()
 
+    parity = block_of(section, tensor) % 2
+
+    def one_round(turn, nothing):
+        pl.when(parity == turn % 2)(lambda: work(turn))
         return nothing
 
     lax.fori_loop(0, CHAIN, one_round, 0)
     for slot in range(CHAIN - 1):
-        for part in range(parts):
-            copy(slot, part).wait_send()
+
+        @pl.when(parity == slot % 2)
+        def _():
+            for part in range(parts):
+                copy(slot, part).wait_send()
+
     join.wait()
 
 
@@ -1356,12 +1368,25 @@
     )(initial, starts, gain, keep, own, other, sqkv0, sqkv1, sout0, sout1, output_grad)
 
 
+LATE = 10
+
+
 def chain_back_kernel(
-    ends, state, update, gain, keep, own, other, ps0, ps1, os0, os1, lse,
-    tok_k0, tok_v0, tok_k1, tok_v1, sqkv0, sqkv1, sout0, sout1, result, ending,
-    grad_state, gproj0, gproj1, gtok0, gtok1, gup, small, scattered,
-    weights, grad_os0, grad_os1, sent, landed, send_sem, recv_sem, piece_send, piece_recv, piece_sem,
+    ends, gain, keep, own, other, ps0, ps1, os0, os1, lse, *refs,
 ):
+    distant, refs = refs[:LATE], refs[LATE:]
+    result, ending, grad_state, gproj0, gproj1, gtok0, gtok1, gup, small, scattered = refs[:10]
+    fetched, refs = refs[10 : 10 + LATE], refs[10 + LATE :]
+    state, update, tok_k0, tok_v0, tok_k1, tok_v1, sqkv0, sqkv1, sout0, sout1 = fetched
+    (
+        weights, grad_os0, grad_os1, sent, landed, send_sem, recv_sem, piece_send, piece_recv, piece_sem, late_sem
+    ) = refs
+    fetches = [
+        pltpu.make_async_copy(source, target, late_sem.at[i])
+        for i, (source, target) in enumerate(zip(distant, fetched))
+    ]
+    for fetch in fetches:
+        fetch.start()
     prior, following = neighbours()
     scatter = Scatter((result, ending), scattered, piece_send, piece_recv, piece_sem)
     meet([prior, following] + scatter.members)
@@ -1397,9 +1422,11 @@
         return carry
 
     lax.fori_loop(0, heads, prepare, 0)
+    for fetch in fetches:
+        fetch.wait()
     grad_state[...] = jnp.zeros_like(grad_state)
 
-    def one_round(turn, nothing):
+    def work(turn):
         for part in range(parts):
             rows = slice(part * CHUNK, (part + 1) * CHUNK)
 
@@ -1438,7 +1465,7 @@
                     else:
                         total_k, total_v = total_k + gk, total_v + gv
 
-                    @pl.when(turn == CHAIN - 1)
+                    @pl.when(turn >= CHAIN - 2)
                     def _():
                         gtk, gtv = tn(s_tok, query) * SCALE, tn(p_tok, grad)
                         if part == 0:
@@ -1450,7 +1477,7 @@
                 gproj[:, at[1]], gproj[:, at[2]] = bf(total_k), bf(total_v)
             return carry
 
-        lax.fori_loop(0, heads, one_head, 0)
+        lax.fori_loop(0, heads, one_head, 0, unroll=True)
         for part in range(parts):
             rows = slice(part * CHUNK, (part + 1) * CHUNK)
             back = nt(gproj0[rows], sqkv0[...]) + nt(gproj1[rows], sqkv1[...])
@@ -1467,7 +1494,7 @@
                 sent[turn, rows] = bf(leaving)
                 copy(turn, part).start()
 
-            @pl.when(turn == CHAIN - 1)
+            @pl.when(turn >= CHAIN - 2)
             def _():
                 gain_term = jnp.sum(back * scaled, axis=0, keepdims=True)
                 bias_term = jnp.sum(new * (value - update[rows]), axis=0, keepdims=True) * (
@@ -1480,12 +1507,20 @@
                     small[1:2, :] += bias_term
                 grad_state[rows] = leaving
 
+    parity = 1 - block_of(lax.axis_index(SECTION), lax.axis_index(TENSOR)) % 2
+
+    def one_round(turn, nothing):
+        pl.when(parity == turn % 2)(lambda: work(turn))
         return nothing
 
     lax.fori_loop(0, CHAIN, one_round, 0)
     for slot in range(CHAIN - 1):
-        for part in range(parts):
-            copy(slot, part).wait_send()
+
+        @pl.when(parity == slot % 2)
+        def _():
+            for part in range(parts):
+                copy(slot, part).wait_send()
+
     scatter.wait()
 
 
@@ -1501,9 +1536,10 @@
     dma = pltpu.SemaphoreType.DMA
     parts = count // CHUNK
     rows = own.shape[0]
+    distant = (state, update, tok_k0, tok_v0, tok_k1, tok_v1, sqkv0, sqkv1, sout0, sout1)
     return pl.pallas_call(
         chain_back_kernel,
-        in_specs=[vmem] * 20 + [anywhere] * 2,
+        in_specs=[vmem] * 10 + [anywhere] * (LATE + 2),
         out_specs=[vmem] * 7 + [anywhere],
         out_shape=[
             jax.ShapeDtypeStruct((count, width), f32),
@@ -1515,13 +1551,14 @@
             jax.ShapeDtypeStruct((2, width), f32),
             jax.ShapeDtypeStruct((2, 8, rows // 2, width // 4), bf16),
         ],
-        scratch_shapes=[
+        scratch_shapes=[pltpu.VMEM(late.shape, late.dtype) for late in distant]
+        + [
             pltpu.VMEM((2, heads, count, rows + count), bf16),
             pltpu.VMEM((count, half), bf16),
             pltpu.VMEM((count, half), bf16),
             pltpu.VMEM((CHAIN - 1, count, width), bf16),
             pltpu.VMEM((CHAIN - 1, count, width), bf16),
-            dma((CHAIN - 1, parts)), dma((CHAIN - 1, parts)), dma((14,)), dma((14,)), dma((2,)),
+            dma((CHAIN - 1, parts)), dma((CHAIN - 1, parts)), dma((14,)), dma((14,)), dma((2,)), dma((LATE,)),
         ],
         compiler_params=params(collective_id=2, has_side_effects=True),
         cost_estimate=pl.CostEstimate(
@@ -1529,10 +1566,7 @@
             bytes_accessed=45 * 1024 * 1024,
             transcendentals=count * count * 4 * heads,
         ),
-    )(
-        ends, state, update, gain, keep, own, other, ps0, ps1, os0, os1, lse,
-        tok_k0, tok_v0, tok_k1, tok_v1, sqkv0, sqkv1, sout0, sout1, result, ending,
-    )
+    )(ends, gain, keep, own, other, ps0, ps1, os0, os1, lse, *distant, result, ending)
 
 
 RING = 8

time: 975 us -> 909 us (0.932)
  Pallas kernels: 724 us -> 663 us
    pallas_call x1, Pallas kernels: 97.8 us -> 61.1 us  [chain(): pl.pallas_call(chain_kernel, in_specs=[vmem] * 10 + [anywhere], out_specs...]
    pallas_call x1, Pallas kernels: 125 us -> 108 us  [gather(): pl.pallas_call(functools.partial(gather_kernel, count), in_specs=[anywher...]
    pallas_call x1, Pallas kernels: 315 us -> 304 us  [weight_grads(): pl.pallas_call(grads_kernel, in_specs=[anywhere] * (3 * count + 3), out_s...]
  transfers between devices with their start and end apart: 7 -> 7, of which waited for: 1 -> 0; matrix products, arithmetic and copies ran while one was open for 9% -> 10% of each run, Pallas kernels for 25% -> 24%
where the time goes in v3:
time: 909 us; the launch traced here: 900 us
  Pallas kernels  663 us (73%)
  matrix products  110 us (12%)
  other arithmetic  57.8 us (6%)
  local copies, waits for them, and re-layouts  44.8 us (5%)
  between operations  18 us (2%)
    pallas_call x1, Pallas kernels, weight_grads(): pl.pallas_call(grads_kernel, in_specs=[anywhere] * (3 * count + 3), out_s...  304 us
    pallas_call x1, Pallas kernels, chain_back(): pl.pallas_call(chain_back_kernel, in_specs=[vmem] * 10 + [anywhere] * (LA...  124 us
    pallas_call x1, Pallas kernels, gather(): pl.pallas_call(functools.partial(gather_kernel, count), in_specs=[anywher...  108 us
    pallas_call x1, Pallas kernels, chain(): pl.pallas_call(chain_kernel, in_specs=[vmem] * 10 + [anywhere], out_specs...  61.1 us
    dot_general x18, matrix products, dot(): return jnp.dot(a, b, preferred_element_type=f32)  58.6 us
    dot_general x16, matrix products, dot_t(): lax.dot_general(a, b, (((1,), (1,)), ((), ())), preferred_element_type=f32)  51 us
    pallas_call x4, Pallas kernels, attend_back(): pl.pallas_call(functools.partial(attend_back_kernel, states is not None),...  39.3 us
    unnamed x299, local copies, waits for them, and re-layouts  31.1 us
  transfers between devices with their start and end apart: 7, of which 0 were waited for; matrix products, arithmetic and copies ran while one was open for 10% of the time, Pallas kernels for 24%

profile of v3, /device:TPU:0, one launch (start us, length us, event | category | flops | bytes accessed | tf_op | source)
XLA Modules:
  0.0 900.3 jit_solution(10948171410316457289)
XLA Ops:
  18.6 107.7 %shard_map.356 = (bf16[512,1024]{1,0:T(8,128)(2,1)}, bf16[512,1024]{1,0:T(8,128)(2,1)}, bf16[512,1024]{1,0:T(8,128)(2,1)}, bf16[1024,1536]{1,0:T(8,128)(2,1)}, b...) custom-call(bf16[1,8,256,1024]{3,2,1,0:T(8,128)(2,1)} %layer_input.1, ...), custom_call_target="tpu_custom_call" | custom-call | bytes 209715200 | tf_op jit(solution)/shard_map/pallas_call | solution.py:1168
  138.3 2.9 convolution_convert_fusion.3.refs_1_.refs_2_.refs_3_
  144.0 6.2 shard_map.357
  150.1 4.0 fusion.59.refs_4_.refs_5_
  154.2 2.9 convolution_convert_fusion.2.refs_1_.refs_2_.refs_3_
  157.1 6.1 shard_map.358
  168.4 5.1 multiply_convert_fusion.3
  176.5 5.1 multiply_convert_fusion.2
  199.3 61.1 %shard_map.359 = (f32[512,1024]{1,0:T(8,128)}, bf16[512,1024]{1,0:T(8,128)(2,1)}, bf16[512,1536]{1,0:T(8,128)(2,1)}, bf16[512,1536]{1,0:T(8,128)(2,1)}, bf16[512...) custom-call(f32[512,1024]{1,0:T(8,128)} %convert_element_type.215.in, ...), custom_call_target="tpu_custom_call" | custom-call | flops 25769803776 | bytes 26214400 | tf_op jit(solution)/shard_map/pallas_call | solution.py:1340
  261.6 2.9 convert_element_type.229.refs_11_
  265.4 4.4 fusion.88
  271.3 7.7 shard_map.360
  279.0 7.7 shard_map.361
  292.1 5.1 multiply_convert_fusion.1
  297.3 3.7 fusion.89
  301.8 3.7 fusion.91
  305.5 6.9 fusion.90
  312.4 10.2 %multiply_convert_fusion = (bf16[512,2048]{1,0:T(8,128)(2,1)}, bf16[512,2048]{1,0:T(8,128)(2,1)S(1)}) fusion(f32[512,2048]{1,0:T(8,128)} %fusion.90, bf16[512,1024]{1,0:T(8,128)(2,1)} %copy-done.64, bf16[1024,2048]{1,0:T(8,128)(2,1)} %all-gather.5.cloned.1.call-done), kind=kOutput, calls=%fused_computation.36 | convolution fusion | flops 2170552320 | bytes 13631488 | tf_op jit(solution)/shard_map/dot_general | solution.py:1918
  322.6 3.2 multiply_reduce_fusion
  331.0 11.4 %shard_map.362 = (bf16[512,512]{1,0:T(8,128)(2,1)}, f32[512,512]{1,0:T(8,128)}, f32[512,512]{1,0:T(8,128)}, bf16[512,512]{1,0:T(8,128)(2,1)}, bf16[512,512]{1,0:...) custom-call(s32[1]{0:T(128)} %bitcast.16.refs_0_, bf16[512,1536]{1,0:T(8,128)(2,1)} %copy-done, ...), custom_call_target="tpu_custom_call" | custom-call | flops 4026531840 | bytes 12582912 | tf_op jit(solution)/shard_map/pallas_call | solution.py:1009
  342.4 11.4 %shard_map.363 = (bf16[512,512]{1,0:T(8,128)(2,1)}, f32[512,512]{1,0:T(8,128)}, f32[512,512]{1,0:T(8,128)}, bf16[512,512]{1,0:T(8,128)(2,1)}, bf16[512,512]{1,0:...) custom-call(s32[1]{0:T(128)} %bitcast.16.refs_0_, bf16[512,1536]{1,0:T(8,128)(2,1)} %copy-done.1, ...), custom_call_target="tpu_custom_call" | custom-call | flops 4026531840 | bytes 12582912 | tf_op jit(solution)/shard_map/pallas_call | solution.py:1009
  359.0 4.1 select_convert_fusion.1.refs_10_
  363.6 123.5 %shard_map.364 = (f32[512,1024]{1,0:T(8,128)}, bf16[512,1536]{1,0:T(8,128)(2,1)}, bf16[512,1536]{1,0:T(8,128)(2,1)}, f32[512,1024]{1,0:T(8,128)}, f32[512,1024]{...) custom-call(f32[1,1024]{1,0:T(1,128)} %broadcast_in_dim.107.ends, ...), custom_call_target="tpu_custom_call" | custom-call | flops 51539607552 | bytes 47185920 | tf_op jit(solution)/shard_map/pallas_call | solution.py:1540
  490.6 3.2 fusion.51
  493.9 4.5 fusion.79
  504.5 4.7 fusion.6.refs_12_
  513.5 4.9 fusion.13.refs_22_
  525.6 8.2 shard_map.366
  533.8 8.3 shard_map.365
  563.8 3.4 fusion.37
  568.1 3.1 fusion.41.refs_32_
  571.2 303.5 %shard_map.367 = (bf16[256,2048]{1,0:T(8,128)(2,1)}, bf16[2048,256]{1,0:T(8,128)(2,1)}, bf16[256,2048]{1,0:T(8,128)(2,1)}, bf16[2048,256]{1,0:T(8,128)(2,1)}, bf...) custom-call(bf16[512,1024]{1,0:T(8,128)(2,1)} %copy-done.64, ...), custom_call_target="tpu_custom_call" | custom-call | flops 31138512896 | bytes 152043520 | tf_op jit(solution)/shard_map/pallas_call | solution.py:1832
  (419 shorter events, 131.4 us)
Async XLA Ops:
  7.2 298.3 %all-gather.3.cloned.1.call-start = ((), (), s32[]{:S(2)}) async-start(), calls=%async_computation | async-start | bytes 5242880 | tf_op jit(solution)/shard_map/all_gather | solution.py:1899
  10.1 127.7 %copy-start.24 = (bf16[1024,512]{1,0:T(8,128)(2,1)}, bf16[1024,512]{1,0:T(8,128)(2,1)S(1)}, u32[]{:S(2)}) copy-start(bf16[1024,512]{1,0:T(8,128)(2,1)S(1)} %get-tuple-element.268) | copy-start | bytes 3145732
  10.1 131.5 %copy-start.26 = (bf16[1024,512]{1,0:T(8,128)(2,1)}, bf16[1024,512]{1,0:T(8,128)(2,1)S(1)}, u32[]{:S(2)}) copy-start(bf16[1024,512]{1,0:T(8,128)(2,1)S(1)} %get-tuple-element.269) | copy-start | bytes 3145732
  126.3 6.8 copy-start.125
  126.3 6.9 copy-start.120
  126.4 10.7 %copy-start.113 = (bf16[1024]{0:T(1024)(128)(2,1)S(1)}, bf16[1024]{0:T(1024)(128)(2,1)}, u32[]{:S(2)}) copy-start(bf16[1024]{0:T(1024)(128)(2,1)} %param.25) | copy-start | bytes 6148
  126.4 10.8 %copy-start.7 = (bf16[512,1024]{1,0:T(8,128)(2,1)S(1)}, bf16[512,1024]{1,0:T(8,128)(2,1)}, u32[]{:S(2)}) copy-start(bf16[512,1024]{1,0:T(8,128)(2,1)} %get-tuple-element.97) | copy-start | bytes 3145732
  128.7 34.5 %collective-permute-start.1 = (bf16[512,1024]{1,0:T(8,128)(2,1)}, bf16[512,1024]{1,0:T(8,128)(2,1)}, u32[]{:S(2)}, u32[]{:S(2)}) collective-permute-start(bf16[512,1024]{1,0:T(8,128)(2,1)} %constant_dynamic-slice_fusion.1), channel_id=1, source_target_pairs={{0,1},{1,0},{2,3},{3,2},{4,5},{5,4},{6,7},{7,6},{8,9},{9,8},{10,11... | collective-permute-start | bytes 3145736 | tf_op jit(solution)/shard_map/ppermute | solution.py:1898
  131.6 67.0 %collective-permute-start.2 = (bf16[256,2048]{1,0:T(8,128)(2,1)}, bf16[256,2048]{1,0:T(8,128)(2,1)}, u32[]{:S(2)}, u32[]{:S(2)}) collective-permute-start(bf16[256,2048]{1,0:T(8,128)(2,1)} %constant_dynamic-slice_fusion), channel_id=1, source_target_pairs={{0,1},{1,0},{2,3},{3,2},{4,5},{5,4},{6,7},{7,6},{8,9},{9,8},{10,11... | collective-permute-start | bytes 3145736 | tf_op jit(solution)/shard_map/ppermute | solution.py:1898
  133.1 8.2 copy-start.106
  133.5 7.8 copy-start.109
  134.0 7.3 copy-start.111
  134.1 126.3 %copy-start.123 = (pred[8]{0:T(512)(128)(4,1)}, pred[8]{0:T(512)(128)(4,1)S(1)}, u32[]{:S(2)}) copy-start(pred[8]{0:T(512)(128)(4,1)S(1)} %get-tuple-element.245) | copy-start | bytes 28
  137.1 13.0 %copy-start.96 = (f32[1024]{0:T(1024)}, f32[1024]{0:T(1024)S(1)}, u32[]{:S(2)}) copy-start(f32[1024]{0:T(1024)S(1)} %convert_element_type.199) | copy-start | bytes 12292
  143.9 22.5 %copy-start.98 = (f32[1024]{0:T(1024)}, f32[1024]{0:T(1024)S(1)}, u32[]{:S(2)}) copy-start(f32[1024]{0:T(1024)S(1)} %convert_element_type.207) | copy-start | bytes 12292
  143.9 40.2 %copy-start.94 = (f32[1024]{0:T(1024)}, f32[1024]{0:T(1024)S(1)}, u32[]{:S(2)}) copy-start(f32[1024]{0:T(1024)S(1)} %convert_element_type.211) | copy-start | bytes 12292
  163.3 149.1 %all-gather.5.cloned.1.call-start = ((), (), s32[]{:S(2)}) async-start(), calls=%async_computation.1 | async-start | bytes 5242880 | tf_op jit(solution)/shard_map/all_gather | solution.py:1899
  166.4 15.2 %copy-start.5 = (f32[512,1024]{1,0:T(8,128)}, f32[512,1024]{1,0:T(8,128)S(1)}, u32[]{:S(2)}) copy-start(f32[512,1024]{1,0:T(8,128)S(1)} %get-tuple-element.294) | copy-start | bytes 6291460
  166.4 7.1 copy-start.104
  168.4 7.5 copy-start.62
  193.9 75.9 %collective-permute-start = (bf16[2,512,1024]{2,1,0:T(8,128)(2,1)}, bf16[2,512,1024]{2,1,0:T(8,128)(2,1)S(1)}, u32[]{:S(2)}, u32[]{:S(2)}) collective-permute-start(bf16[2,512,1024]{2,1,0:T(8,128)(2,1)} %pad_maximum_fusion.3), channel_id=1, source_target_pairs={{0,8},{8,1},{1,9},{9,17},{17,25},{25,16},{16,24},{2,10},{10,3},{3,... | collective-permute-start | bytes 6291464 | tf_op jit(solution)/shard_map/ppermute | solution.py:1941
  199.3 62.3 %copy-start.118 = (bf16[1024]{0:T(1024)(128)(2,1)S(1)}, bf16[1024]{0:T(1024)(128)(2,1)}, u32[]{:S(2)}) copy-start(bf16[1024]{0:T(1024)(128)(2,1)} %param.39) | copy-start | bytes 6148
  279.0 7.7 copy-start.16
  279.0 7.7 copy-start.76
  312.4 10.2 %copy-start.131 = (bf16[1024,2048]{1,0:T(8,128)(2,1)S(1)}, bf16[1024,2048]{1,0:T(8,128)(2,1)}, u32[]{:S(2)}) copy-start(bf16[1024,2048]{1,0:T(8,128)(2,1)} %all-gather.5.cloned.1.call-done) | copy-start | bytes 12582916
  312.4 10.2 %copy-start.138 = (f32[512,1024]{1,0:T(8,128)S(1)}, f32[512,1024]{1,0:T(8,128)}, u32[]{:S(2)}) copy-start(f32[512,1024]{1,0:T(8,128)} %fusion.89) | copy-start | bytes 6291460
  342.4 11.4 %copy-start.78 = (bf16[512,512]{1,0:T(8,128)(2,1)S(1)}, bf16[512,512]{1,0:T(8,128)(2,1)}, u32[]{:S(2)}) copy-start(bf16[512,512]{1,0:T(8,128)(2,1)} %get-tuple-element.133) | copy-start | bytes 1572868
  357.4 129.8 %collective-permute-start.3 = (bf16[2,512,1024]{2,1,0:T(8,128)(2,1)}, bf16[2,512,1024]{2,1,0:T(8,128)(2,1)}, u32[]{:S(2)}, u32[]{:S(2)}) collective-permute-start(bf16[2,512,1024]{2,1,0:T(8,128)(2,1)} %pad_maximum_fusion.4), channel_id=1, source_target_pairs={{8,0},{1,8},{9,1},{17,9},{25,17},{16,25},{24,16},{10,2},{3,10},{11... | collective-permute-start | bytes 6291464 | tf_op jit(solution)/shard_map/ppermute | solution.py:1989
  503.0 8.7 copy-start.52
  533.8 8.3 copy-start.79
  533.8 8.3 copy-start.80
  544.1 9.6 %collective-permute-start.4 = (bf16[2,512,1024]{2,1,0:T(8,128)(2,1)S(1)}, bf16[2,512,1024]{2,1,0:T(8,128)(2,1)S(1)}, u32[]{:S(2)}, u32[]{:S(2)}) collective-permute-start(bf16[2,512,1024]{2,1,0:T(8,128)(2,1)S(1)} %pad_maximum_fusion.5), channel_id=1, source_target_pairs={{8,0},{1,8},{9,1},{17,9},{25,17},{16,25},{24,16},{10,2},{3,10},{11... | collective-permute-start | bytes 6291464 | tf_op jit(solution)/shard_map/ppermute | solution.py:1989
  (123 other events, 366.2 us)
Sparse Core Ops, SparseCore 0:
  163.4 36.4 all-gather.2
  201.5 37.1 all-gather.4

commit v4 on v3

--- a/solution.py
+++ b/solution.py
@@ -900,41 +900,59 @@
         lse[0, start : start + CHUNK] = top * LOG2_SCALE + jnp.log2(total[:, :1])
 
 
-def head_block(rows, offset):
-    return pl.BlockSpec((rows, HEAD_DIM), lambda h: (0, offset + h))
-
-
-def attend(opening, proj, prior, states=None):
-    rows, width = proj.shape[0], proj.shape[1] // 3
+def side_blocks(rows, offset, heads):
+    return (
+        pl.BlockSpec((rows, HEAD_DIM), lambda h: (0, offset + jnp.minimum(h, heads - 1))),
+        pl.BlockSpec((rows, HEAD_DIM), lambda h: (0, offset + jnp.maximum(h - heads, 0))),
+    )
+
+
+def lse_blocks(rows, heads):
+    return (
+        pl.BlockSpec((1, rows, 1), lambda h: (jnp.minimum(h, heads - 1), 0, 0)),
+        pl.BlockSpec((1, rows, 1), lambda h: (jnp.maximum(h - heads, 0), 0, 0)),
+    )
+
+
+def both_sides(kernel, inputs, outputs, open_ref, *refs):
+    ins, outs, scratch = refs[: 2 * inputs], refs[2 * inputs : 2 * (inputs + outputs)], refs[2 * (inputs + outputs) :]
+    own = pl.program_id(0) < pl.num_programs(0) // 2
+    pl.when(own)(lambda: kernel(open_ref, *ins[:inputs], *outs[:outputs], *scratch))
+    pl.when(jnp.logical_not(own))(lambda: kernel(open_ref, *ins[inputs:], *outs[outputs:], *scratch))
+
+
+def attend(opening, projs, priors, states=None):
+    rows, width = projs[0].shape[0], projs[0].shape[1] // 3
     heads = width // HEAD_DIM
-    specs = [pl.BlockSpec(memory_space=pltpu.SMEM)]
-    specs += [head_block(rows, i * heads) for i in range(3)]
-    specs += [head_block(rows, i * heads) for i in range(2)]
-    args = [opening, proj, proj, proj, prior, prior]
+    columns = [side_blocks(rows, i * heads, heads) for i in (0, 1, 2, 0, 1)]
+    arrays = [projs, projs, projs, priors, priors]
     keys = 2 * rows
     if states is not None:
-        specs += [head_block(states.shape[0], i * heads) for i in (1, 2)]
-        args += [states, states]
-        keys += states.shape[0]
-    return pl.pallas_call(
-        functools.partial(attend_kernel, states is not None),
-        grid=(heads,),
-        in_specs=specs,
-        out_specs=[
-            head_block(rows, 0),
-            pl.BlockSpec((1, rows, 1), lambda h: (h, 0, 0)),
-        ],
+        columns += [side_blocks(states[0].shape[0], i * heads, heads) for i in (1, 2)]
+        arrays += [states, states]
+        keys += states[0].shape[0]
+    outs = [side_blocks(rows, 0, heads), lse_blocks(rows, heads)]
+    mixed0, lse0, mixed1, lse1 = pl.pallas_call(
+        functools.partial(
+            both_sides, functools.partial(attend_kernel, states is not None), len(arrays), 2
+        ),
+        grid=(2 * heads,),
+        in_specs=[pl.BlockSpec(memory_space=pltpu.SMEM)]
+        + [pair[side] for side in range(2) for pair in columns],
+        out_specs=[pair[side] for side in range(2) for pair in outs],
         out_shape=[
             jax.ShapeDtypeStruct((rows, width), jnp.bfloat16),
             jax.ShapeDtypeStruct((heads, rows, 1), jnp.float32),
-        ],
+        ]
+        * 2,
         compiler_params=params(),
         cost_estimate=pl.CostEstimate(
-            flops=4 * rows * keys * width,
-            bytes_accessed=2 * rows * width * 8,
-            transcendentals=rows * keys * heads // 2,
+            flops=8 * rows * keys * width,
+            bytes_accessed=4 * rows * width * 8,
+            transcendentals=rows * keys * heads,
         ),
-    )(*args)
+    )(opening, *(pair[side] for side in range(2) for pair in arrays))
+    return mixed0, lse0, mixed1, lse1
 
 
 def attend_back_kernel(with_states, *refs):
@@ -988,38 +1006,38 @@
     gpk[...] = bf(gpk_sum[...] * SCALE)
 
 
-def attend_back(opening, proj, prior, grad_mixed, mixed, lse, states=None):
-    rows, width = proj.shape[0], proj.shape[1] // 3
+def attend_back(opening, projs, priors, grads, mixed, lse, states=None):
+    rows, width = projs[0].shape[0], projs[0].shape[1] // 3
     heads = width // HEAD_DIM
-    specs = [pl.BlockSpec(memory_space=pltpu.SMEM)]
-    specs += [head_block(rows, i * heads) for i in range(3)]
-    specs += [head_block(rows, i * heads) for i in range(2)]
-    args = [opening, proj, proj, proj, prior, prior]
+    columns = [side_blocks(rows, i * heads, heads) for i in (0, 1, 2, 0, 1)]
+    arrays = [projs, projs, projs, priors, priors]
+    kinds = [jnp.bfloat16, jnp.float32, jnp.float32, jnp.bfloat16, jnp.bfloat16]
     keys = 2 * rows
     if states is not None:
-        specs += [head_block(states.shape[0], i * heads) for i in (1, 2)]
-        args += [states, states]
-        keys += states.shape[0]
-    specs += [head_block(rows, 0), head_block(rows, 0)]
-    specs += [pl.BlockSpec((1, rows, 1), lambda h: (h, 0, 0))]
-    args += [grad_mixed, mixed, lse]
-    kinds = [jnp.bfloat16, jnp.float32, jnp.float32, jnp.bfloat16, jnp.bfloat16]
-    if states is not None:
+        columns += [side_blocks(states[0].shape[0], i * heads, heads) for i in (1, 2)]
+        arrays += [states, states]
         kinds += [jnp.float32, jnp.float32]
-    return pl.pallas_call(
-        functools.partial(attend_back_kernel, states is not None),
-        grid=(heads,),
-        in_specs=specs,
-        out_specs=[head_block(rows, 0) for _ in kinds],
-        out_shape=[jax.ShapeDtypeStruct((rows, width), kind) for kind in kinds],
+        keys += states[0].shape[0]
+    columns += [side_blocks(rows, 0, heads)] * 2 + [lse_blocks(rows, heads)]
+    arrays += [grads, mixed, lse]
+    results = pl.pallas_call(
+        functools.partial(
+            both_sides, functools.partial(attend_back_kernel, states is not None), len(arrays), len(kinds)
+        ),
+        grid=(2 * heads,),
+        in_specs=[pl.BlockSpec(memory_space=pltpu.SMEM)]
+        + [pair[side] for side in range(2) for pair in columns],
+        out_specs=[side_blocks(rows, 0, heads)[side] for side in range(2) for _ in kinds],
+        out_shape=[jax.ShapeDtypeStruct((rows, width), kind) for kind in kinds] * 2,
         scratch_shapes=[pltpu.VMEM((rows, HEAD_DIM), jnp.float32)] * 2,
         compiler_params=params(),
         cost_estimate=pl.CostEstimate(
-            flops=10 * rows * keys * width,
-            bytes_accessed=2 * rows * width * 24,
-            transcendentals=rows * keys * heads // 2,
+            flops=20 * rows * keys * width,
+            bytes_accessed=4 * rows * width * 24,
+            transcendentals=rows * keys * heads,
         ),
-    )(*args)
+    )(opening, *(pair[side] for side in range(2) for pair in arrays))
+    return results[: len(kinds)], results[len(kinds) :]
 
 
 KINDS = 9
@@ -1145,14 +1163,14 @@
 
     for i in range(FLIGHT):
         begin(i)
-    for w in range(count + 3):
+    for w in range(count + 2):
         if w < count:
             spread.hop(w)
         begin(w + FLIGHT)
+        if 0 <= w - 1 < count:
+            spread.cross(w - 1)
         if 0 <= w - 2 < count:
-            spread.cross(w - 2)
-        if 0 <= w - 3 < count:
-            spread.close(w - 3)
+            spread.close(w - 2)
     for w in range(count):
         spread.end(w)
     for join in joins:
@@ -1304,12 +1322,12 @@
             rows = slice(part * CHUNK, (part + 1) * CHUNK)
             term = nn(os0[rows], sout0[...]) + nn(os1[rows], sout1[...])
             update[rows] = term
-            renewed_state = keep[...] * state[rows] + (1.0 - keep[...]) * term
+            renewed_state = bf(keep[...] * state[rows] + (1.0 - keep[...]) * term)
             fresh[rows] = renewed_state
 
             @pl.when(turn < CHAIN - 1)
             def _():
-                sent[turn, rows] = bf(renewed_state)
+                sent[turn, rows] = renewed_state
                 copy(turn, part).start()
 
     parity = block_of(section, tensor) % 2
@@ -1350,7 +1368,7 @@
             jax.ShapeDtypeStruct((count, half), bf16),
             jax.ShapeDtypeStruct((2, heads, count, 1), f32),
             jax.ShapeDtypeStruct((count, width), f32),
-            jax.ShapeDtypeStruct((count, width), f32),
+            jax.ShapeDtypeStruct((count, width), bf16),
             jax.ShapeDtypeStruct((2 * output_grad.shape[2], width), bf16),
         ],
         scratch_shapes=[
@@ -1372,14 +1390,14 @@
 
 
 def chain_back_kernel(
-    ends, gain, keep, own, other, ps0, ps1, os0, os1, lse, *refs,
+    starts, ends, gain, keep, own, other, ps0, ps1, os0, os1, lse, *refs,
 ):
     distant, refs = refs[:LATE], refs[LATE:]
-    result, ending, grad_state, gproj0, gproj1, gtok0, gtok1, gup, small, scattered = refs[:10]
+    result, ending, first_grad, gproj0, gproj1, gtok0, gtok1, gup, small, scattered = refs[:10]
     fetched, refs = refs[10 : 10 + LATE], refs[10 + LATE :]
     state, update, tok_k0, tok_v0, tok_k1, tok_v1, sqkv0, sqkv1, sout0, sout1 = fetched
     (
-        weights, grad_os0, grad_os1, sent, landed, send_sem, recv_sem, piece_send, piece_recv, piece_sem, late_sem
+        grad_state, weights, grad_os0, grad_os1, sent, landed, send_sem, recv_sem, piece_send, piece_recv, piece_sem, late_sem
     ) = refs
     fetches = [
         pltpu.make_async_copy(source, target, late_sem.at[i])
@@ -1505,7 +1523,7 @@
                 else:
                     small[0:1, :] += gain_term
                     small[1:2, :] += bias_term
-                grad_state[rows] = leaving
+                first_grad[rows] = bf(jnp.where(starts[...] > 0.0, leaving, 0.0))
 
     parity = 1 - block_of(lax.axis_index(SECTION), lax.axis_index(TENSOR)) % 2
 
@@ -1525,7 +1543,7 @@
 
 
 def chain_back(
-    ends, state, update, gain, keep, own, other, ps0, ps1, os0, os1, lse,
+    starts, ends, state, update, gain, keep, own, other, ps0, ps1, os0, os1, lse,
     tok_k0, tok_v0, tok_k1, tok_v1, sqkv0, sqkv1, sout0, sout1, result, ending,
 ):
     count, width = state.shape
@@ -1539,10 +1557,10 @@
     distant = (state, update, tok_k0, tok_v0, tok_k1, tok_v1, sqkv0, sqkv1, sout0, sout1)
     return pl.pallas_call(
         chain_back_kernel,
-        in_specs=[vmem] * 10 + [anywhere] * (LATE + 2),
+        in_specs=[vmem] * 11 + [anywhere] * (LATE + 2),
         out_specs=[vmem] * 7 + [anywhere],
         out_shape=[
-            jax.ShapeDtypeStruct((count, width), f32),
+            jax.ShapeDtypeStruct((count, width), bf16),
             jax.ShapeDtypeStruct((count, 3 * half), bf16),
             jax.ShapeDtypeStruct((count, 3 * half), bf16),
             jax.ShapeDtypeStruct((rows, 2 * half), f32),
@@ -1553,6 +1571,7 @@
         ],
         scratch_shapes=[pltpu.VMEM(late.shape, late.dtype) for late in distant]
         + [
+            pltpu.VMEM((count, width), f32),
             pltpu.VMEM((2, heads, count, rows + count), bf16),
             pltpu.VMEM((count, half), bf16),
             pltpu.VMEM((count, half), bf16),
@@ -1566,12 +1585,13 @@
             bytes_accessed=45 * 1024 * 1024,
             transcendentals=count * count * 4 * heads,
         ),
-    )(ends, gain, keep, own, other, ps0, ps1, os0, os1, lse, *distant, result, ending)
+    )(starts, ends, gain, keep, own, other, ps0, ps1, os0, os1, lse, *distant, result, ending)
 
 
 RING = 8
 SHORT_RING = 4
 TILE = 256
+TAIL = 12
 LAGS = (0, 1, 2, 4, 6, 7, 8, 9, 10)
 UP_D, DOWN_D, UP_B, DOWN_B, OUT_C, QKV_C, SOUT_C, SQKV_C, QKV_A, OUT_A = range(10)
 WEIGHTS = (
@@ -1580,20 +1600,28 @@
 )
 STARTS = [sum(w[2] for w in WEIGHTS[:i]) for i in range(len(WEIGHTS))]
 PLAIN = sum(w[2] for w in WEIGHTS)
+TAIL_WEIGHT = [w[0] for w in WEIGHTS].index(QKV_A)
+TAIL_INPUTS = 10
 TILES = PLAIN + 2
 
 
 def grads_kernel(*refs):
     count = len(WEIGHTS)
-    lefts, panels_own, panels_other = refs[:count], refs[count : 2 * count], refs[2 * count : 3 * count]
-    first, small, rows_out = refs[3 * count : 3 * count + 3]
-    refs = refs[3 * count + 3 :]
+    lefts, refs = refs[:count], refs[count:]
+    panels_own, panels_other, refs = list(refs[: count - 1]), list(refs[count - 1 : 2 * count - 2]), refs[2 * count - 2 :]
+    first, small, leaving_keys, refs = refs[0], refs[1], refs[2:6], refs[6:]
+    distant, gain, refs = refs[:TAIL_INPUTS], refs[TAIL_INPUTS], refs[TAIL_INPUTS + 1 :]
     outs, last_out, landed = refs[:count], refs[count], refs[count + 1]
+    refs = refs[count + 2 :]
     (
         left, panel, pair, core_in, kept1, first_in, kept2, second_in, kept3, third_in, kept4, fourth_in, result,
         left_sem, panel_sem, last_sem, core_send, core_recv, first_send, first_recv, second_send, second_recv,
         send_sem, recv_sem, piece_send, piece_recv, piece_sem,
-    ) = refs[count + 2 :]
+        halo, ga0, ga1, rows_out, small_rows, gain_sum, tail_sem, halo_send, halo_recv,
+    ) = refs[:-TAIL_INPUTS]
+    fetched = refs[-TAIL_INPUTS:]
+    panels_own.insert(TAIL_WEIGHT, ga0)
+    panels_other.insert(TAIL_WEIGHT, ga1)
     section, tensor, group = (lax.axis_index(a) for a in (SECTION, TENSOR, DP))
     core, high = section % 2, section // 2
     near, far = group % 2, group // 2
@@ -1602,8 +1630,24 @@
     near_group = {DP: group + 1 - 2 * near}
     far_group = {DP: (group + 2) % 4}
     scatter = Scatter((rows_out,), landed, piece_send, piece_recv, piece_sem)
+    tail_fetches = [
+        pltpu.make_async_copy(source, target, tail_sem.at[i])
+        for i, (source, target) in enumerate(zip(distant + (small,), fetched + (small_rows,)))
+    ]
+    for fetch in tail_fetches:
+        fetch.start()
+    prior, _ = neighbours()
     meet(scatter.members + [near_group, far_group])
-    scatter.start()
+
+    def halo_copy(i):
+        to = 2 * ((tensor + prior[TENSOR] + i // 2) % 2) + i % 2
+        return pltpu.make_async_remote_copy(
+            src_ref=leaving_keys[i], dst_ref=halo.at[to], send_sem=halo_send.at[i],
+            recv_sem=halo_recv.at[to], device_id=prior, device_id_type=MESH,
+        )
+
+    for i in range(4):
+        halo_copy(i).start()
 
     def remote(source, target, sems, recvs, where, partner):
         return pltpu.make_async_remote_copy(
@@ -1629,13 +1673,13 @@
         for i in range(8):
             s, t = i // 2, i % 2
             columns = slice(s * TILE, (s + 1) * TILE)
-            source = small.at[:, columns] if which else first.at[t * TILE : (t + 1) * TILE, columns]
+            source = small_rows.at[:, columns] if which else first.at[t * TILE : (t + 1) * TILE, columns]
             yield pltpu.make_async_copy(source, pair.at[slot, s % 2, s // 2, t], last_sem.at[i])
 
     def core_copy(k):
-        slot = k % RING
+        slot = k % SHORT_RING
         return remote(
-            pair.at[k % SHORT_RING, 1 - core], core_in.at[slot], core_send, core_recv, slot, other_core
+            pair.at[slot, 1 - core], core_in.at[slot], core_send, core_recv, slot, other_core
         )
 
     def order(k):
@@ -1750,7 +1794,7 @@
         core_copy(k).wait()
         for i in range(4):
             kept1[k % SHORT_RING, i] = add(
-                pair[k % SHORT_RING, core, i // 2, i % 2], core_in[k % RING, i // 2, i % 2]
+                pair[k % SHORT_RING, core, i // 2, i % 2], core_in[k % SHORT_RING, i // 2, i % 2]
             )
         for i in range(2):
             first_copy(k, i).start()
@@ -1803,11 +1847,52 @@
         def _():
             last_out[k - PLAIN] = result[k]
 
+    gq0, gk0, gv0, gq1, gk1, gv1, w0, w1, tokens, grad = fetched
+    wide = gq0.shape[1]
+
+    def tail_begin():
+        for copy in tail_fetches:
+            copy.wait()
+        for i in range(4):
+            halo_copy(i).wait_send()
+            pltpu.make_async_remote_copy(
+                src_ref=leaving_keys[i], dst_ref=halo.at[i], send_sem=halo_send.at[i],
+                recv_sem=halo_recv.at[i], device_id=prior, device_id_type=MESH,
+            ).wait_recv()
+        gain_sum[...] = jnp.zeros_like(gain_sum)
+
+    def tail_rows(start):
+        rows = slice(start, start + CHUNK)
+        for side, (to, q, k, v) in enumerate(((ga0, gq0, gk0, gv0), (ga1, gq1, gk1, gv1))):
+            to[rows, :wide] = q[rows]
+            to[rows, wide : 2 * wide] = bf(k[rows] + halo[2 * side, rows].astype(jnp.float32))
+            to[rows, 2 * wide :] = bf(v[rows] + halo[2 * side + 1, rows].astype(jnp.float32))
+        back = nt(ga0[rows], w0[...]) + nt(ga1[rows], w1[...])
+        value = tokens[rows].astype(jnp.float32)
+        factor = inverse_rms(value)
+        scaled = value * factor
+        through = back * gain[...]
+        rows_out[rows] = bf(
+            grad[rows]
+            + factor * (through - scaled * jnp.mean(through * scaled, axis=-1, keepdims=True))
+        )
+        gain_sum[0:1] += jnp.sum(back * scaled, axis=0, keepdims=True)
+
+    def tail_end():
+        top = small_rows[:16].astype(jnp.float32)
+        row = lax.broadcasted_iota(jnp.int32, top.shape, 0)
+        small_rows[:16] = bf(jnp.where(row == 0, gain_sum[0:1], top))
+        scatter.start()
+
     stages = (
         fetch, multiply, over_cores, over_first, over_second, over_near, over_far, from_far, from_near
     )
 
     def step(i, nothing):
+        pl.when(i == TAIL)(tail_begin)
+        for part in range(grad.shape[0] // CHUNK):
+            pl.when(i == TAIL + 2 + 2 * part)(functools.partial(tail_rows, part * CHUNK))
+        pl.when(i == TAIL + 3 + 2 * (grad.shape[0] // CHUNK))(tail_end)
         for stage, lag in zip(stages, LAGS):
             k = i - lag
 
@@ -1821,7 +1906,7 @@
     scatter.wait()
 
 
-def weight_grads(operands, first, small, rows_out):
+def weight_grads(operands, first, small, leaving_keys, tail, gain):
     bf16 = jnp.bfloat16
     dma = pltpu.SemaphoreType.DMA
     anywhere, vmem = pl.BlockSpec(memory_space=pl.ANY), pl.BlockSpec(memory_space=pltpu.VMEM)
@@ -1831,14 +1916,14 @@
     shapes += [(2, TILE, TILE)]
     results = pl.pallas_call(
         grads_kernel,
-        in_specs=[anywhere] * (3 * count + 3),
+        in_specs=[anywhere] * (3 * count + 4 + TAIL_INPUTS) + [vmem],
         out_specs=[vmem] * (count + 1) + [anywhere],
         out_shape=[jax.ShapeDtypeStruct(s, bf16) for s in shapes + [(1, 8, TILE, TILE)]],
         scratch_shapes=[
             pltpu.VMEM((3, rows, width), bf16),
             pltpu.VMEM((SHORT_RING, 2, rows, TILE), bf16),
             pltpu.VMEM((SHORT_RING, 2, 2, 2, TILE, TILE), bf16),
-            pltpu.VMEM((RING, 2, 2, TILE, TILE), bf16),
+            pltpu.VMEM((SHORT_RING, 2, 2, TILE, TILE), bf16),
             pltpu.VMEM((SHORT_RING, 4, TILE, TILE), bf16),
             pltpu.VMEM((RING, 2, TILE, TILE), bf16),
             pltpu.VMEM((RING, 2, TILE, TILE), bf16),
@@ -1849,19 +1934,99 @@
             pltpu.VMEM((RING, TILE // 4, TILE), bf16),
             pltpu.VMEM((TILES, TILE, TILE), bf16),
             dma((3,)), dma((2 * SHORT_RING,)), dma((8,)),
-            dma((RING,)), dma((RING,)),
+            dma((SHORT_RING,)), dma((SHORT_RING,)),
             dma((2 * RING,)), dma((2 * RING,)), dma((RING,)), dma((RING,)),
             dma((4 * RING,)), dma((4 * RING,)), dma((7,)), dma((7,)), dma((1,)),
-        ],
+            pltpu.VMEM((4, rows, width // 2), bf16),
+            pltpu.VMEM((rows, 3 * width // 2), bf16),
+            pltpu.VMEM((rows, 3 * width // 2), bf16),
+            pltpu.VMEM((rows, width), bf16),
+            pltpu.VMEM((TILE, width), bf16),
+            pltpu.VMEM((8, width), jnp.float32),
+            dma((TAIL_INPUTS + 1,)), dma((4,)), dma((4,)),
+        ]
+        + [pltpu.VMEM(value.shape, value.dtype) for value in tail],
         compiler_params=params(collective_id=3, has_side_effects=True),
         cost_estimate=pl.CostEstimate(
             flops=2 * 8 * TILES * TILE * TILE * rows,
             bytes_accessed=40 * TILES * TILE * TILE,
             transcendentals=0,
         ),
-    )(*(operands[w[0]][i] for i in range(3) for w in WEIGHTS), first, small, rows_out)
+    )(
+        *(operands[w[0]][0] for w in WEIGHTS),
+        *(operands[w[0]][i] for i in (1, 2) for w in WEIGHTS if w[0] != QKV_A),
+        first, small, *leaving_keys, *tail, gain,
+    )
     shares = {w[0]: r for w, r in zip(WEIGHTS, results)}
     return shares, results[count], results[count + 1]
+
+
+def last_layer_kernel(
+    alive, h, gy, r, up0, up1, down0, down1, a0, a1, g0, g1, result, through, total, back
+):
+    step, steps = pl.program_id(0), pl.num_programs(0)
+
+    @pl.when(step == 0)
+    def _():
+        total[...] = jnp.zeros_like(total)
+        back[...] = jnp.zeros_like(back)
+
+    def chunk(up, down, a_out, g_out):
+        u = nn(h[...], up[...])
+        square = u * u
+        slope = math.sqrt(2.0 / math.pi)
+        t = jnp.tanh(slope * (u + 0.044715 * (square * u)))
+        a = bf(0.5 * u * (1.0 + t))
+        a_out[...] = a
+        total[...] += nn(a, down[...])
+        rise = 0.5 * (1.0 + t) + 0.5 * u * (1.0 - t * t) * (slope + (3.0 * 0.044715 * slope) * square)
+        g = bf(nt(gy[...], down[...]) * rise)
+        g_out[...] = g
+        back[...] += nt(g, up[...])
+
+    pl.when(step < steps // 2)(lambda: chunk(up0, down0, a0, g0))
+    pl.when(step >= steps // 2)(lambda: chunk(up1, down1, a1, g1))
+
+    @pl.when(step == steps - 1)
+    def _():
+        result[...] = bf(jnp.where(alive[0] > 0, r[...] + total[...], 0.0))
+        through[...] = back[...]
+
+
+def last_layer(alive, h, gy, r, up0, up1, down0, down1):
+    rows, width = h.shape
+    hidden = up0.shape[1]
+    wide = 512
+    half = hidden // wide
+
+    def first(i):
+        return jnp.minimum(i, half - 1)
+
+    def second(i):
+        return jnp.maximum(i - half, 0)
+
+    ups = [pl.BlockSpec((width, wide), lambda i, of=of: (0, of(i))) for of in (first, second)]
+    downs = [pl.BlockSpec((wide, width), lambda i, of=of: (of(i), 0)) for of in (first, second)]
+    hiddens = [pl.BlockSpec((rows, wide), lambda i, of=of: (0, of(i))) for of in (first, second)]
+    kept = pl.BlockSpec((rows, width), lambda i: (0, 0))
+    return pl.pallas_call(
+        last_layer_kernel,
+        grid=(2 * half,),
+        in_specs=[pl.BlockSpec(memory_space=pltpu.SMEM), kept, kept, kept] + ups + downs,
+        out_specs=hiddens + hiddens + [kept, kept],
+        out_shape=[jax.ShapeDtypeStruct((rows, hidden), jnp.bfloat16)] * 4
+        + [
+            jax.ShapeDtypeStruct((rows, width), jnp.bfloat16),
+            jax.ShapeDtypeStruct((rows, width), jnp.float32),
+        ],
+        scratch_shapes=[pltpu.VMEM((rows, width), jnp.float32)] * 2,
+        compiler_params=params(),
+        cost_estimate=pl.CostEstimate(
+            flops=16 * rows * width * hidden,
+            bytes_accessed=8 * width * hidden + 16 * rows * hidden,
+            transcendentals=2 * rows * hidden,
+        ),
+    )(alive, h, gy, r, up0, up1, down0, down1)
 
 
 def gelu_back(values, grad):
@@ -1892,11 +2057,10 @@
         high = jnp.where(tensor == 0, other, own)
         return low, high
 
-    def other_half(weight):
+    def crossed(weight):
         size = weight.shape[0] // sections
         piece = lax.dynamic_slice_in_dim(weight, section * size, size, 0)
-        landed = lax.ppermute(piece, TENSOR, SWAP)
-        return lax.all_gather(landed, SECTION, axis=0, tiled=True)
+        return lax.ppermute(piece, TENSOR, SWAP)
 
     def flat(weight):
         return jnp.concatenate([weight[:, i] for i in range(3)], axis=1)
@@ -1904,11 +2068,11 @@
     wqkv_a0, wqkv_c0, sqkv_c0 = flat(wqkv_a), flat(wqkv_c), flat(sqkv_c)
     (tokens, before, initial), others = gather(
         layer_input, init_states,
-        (wqkv_a0, wout_a, up_b, down_b, wqkv_c0, sqkv_c0, sout_c, wout_c),
-    )
-    wqkv_a1, wout_a1, up_b1, down_b1, wqkv_c1, sqkv_c1, sout_c1, wout_c1 = others
+        (wout_a, sout_c, wout_c, wqkv_a0, wqkv_c0, sqkv_c0, up_b, down_b),
+    )
+    wout_a1, sout_c1, wout_c1, wqkv_a1, wqkv_c1, sqkv_c1, up_b1, down_b1 = others
     tokens, late_up, late_down = lax.optimization_barrier((tokens, up_d, down_d))
-    up_d1, down_d1 = other_half(late_up), other_half(late_down)
+    pieces = crossed(late_up), crossed(late_down)
     initial = initial.astype(f32)
 
     def normed(values, gain):
@@ -1927,13 +2091,14 @@
     pa0, pa1 = bf(dot(h0, wqkv_a0)), bf(dot(h0, wqkv_a1))
     prior_a0 = bf(dot(h_before, wqkv_a0[:, half:]))
     prior_a1 = bf(dot(h_before, wqkv_a1[:, half:]))
-    oa0, lse_a0 = attend(opening, pa0, prior_a0)
-    oa1, lse_a1 = attend(opening, pa1, prior_a1)
+    oa0, lse_a0, oa1, lse_a1 = attend(opening, (pa0, pa1), (prior_a0, prior_a1))
     r1 = r0 + (dot(oa0, wout_a) + dot(oa1, wout_a1))
 
     h1 = normed(r1, gb)
     ub0, ub1 = dot(h1, up_b), dot(h1, up_b1)
     ab0, ab1 = bf(smooth(ub0)), bf(smooth(ub1))
+    ab0, *pieces = lax.optimization_barrier((ab0, *pieces))
+    up_d1, down_d1 = (lax.all_gather(piece, SECTION, axis=0, tiled=True) for piece in pieces)
     r2 = r1 + (dot(ab0, down_b) + dot(ab1, down_b1))
 
     h2 = normed(r2, gc)
@@ -1953,16 +2118,10 @@
         initial, flag(starts), state_gain, retain, pc0, pc1,
         sqkv_c0, sqkv_c1, sout_c, sout_c1, output_grad,
     )
-    oc0, lse_c0 = attend(opening, pc0, prior_c0, ps0)
-    oc1, lse_c1 = attend(opening, pc1, prior_c1, ps1)
+    oc0, lse_c0, oc1, lse_c1 = attend(opening, (pc0, pc1), (prior_c0, prior_c1), (ps0, ps1))
     r3 = r2 + (dot(oc0, wout_c) + dot(oc1, wout_c1))
 
     h3 = normed(r3, gd)
-    ud0, ud1 = dot(h3, up_d), dot(h3, up_d1)
-    ad0, ad1 = bf(smooth(ud0)), bf(smooth(ud1))
-    r4 = r3 + (dot(ad0, down_d) + dot(ad1, down_d1))
-    result = bf(jnp.where(alive, r4, 0.0))
-
     def feed_back(up_name, down_name, grad, values, h, gain, u0, u1, a0, a1, up0, up1, down0, down1):
         gy = bf(grad)
         g0 = bf(gelu_back(u0, dot_t(gy, down0)))
@@ -1975,12 +2134,20 @@
 
     operands = {}
     grad4 = jnp.where(alive, cotangent.astype(f32), 0.0)
-    grad3, gain_d_grad = feed_back(
-        UP_D, DOWN_D, grad4, r3, h3, gd, ud0, ud1, ad0, ad1, up_d, up_d1, down_d, down_d1
-    )
+    gy4 = bf(grad4)
+    ad0, ad1, gd0, gd1, result, through_d = last_layer(
+        alive.astype(jnp.int32)[None], h3, gy4, r3, up_d, up_d1, down_d, down_d1
+    )
+    operands[DOWN_D] = (gy4, ad0, ad1)
+    operands[UP_D] = (h3, gd0, gd1)
+    back_d, gain_d_grad = norm_back(r3, gd, through_d)
+    grad3 = grad4 + back_d
+
     gy3 = bf(grad3)
-    tok0 = attend_back(opening, pc0, prior_c0, bf(dot_t(gy3, wout_c)), oc0, lse_c0, ps0)
-    tok1 = attend_back(opening, pc1, prior_c1, bf(dot_t(gy3, wout_c1)), oc1, lse_c1, ps1)
+    tok0, tok1 = attend_back(
+        opening, (pc0, pc1), (prior_c0, prior_c1), (bf(dot_t(gy3, wout_c)), bf(dot_t(gy3, wout_c1))),
+        (oc0, oc1), (lse_c0, lse_c1), (ps0, ps1),
+    )
 
     def halo_back(one, two):
         pair = in_order(
@@ -1990,9 +2157,9 @@
         return in_order(back[0], back[1])
 
     halo_c0, halo_c1 = halo_back(tok0, tok1)
-    grad_state, gs0, gs1, gtok0, gtok1, gup, small, landed = chain_back(
-        flag(ends), state_in, update, state_gain, retain, pc0, pc1, ps0, ps1, os0, os1, lse_s,
-        tok0[5], tok0[6], tok1[5], tok1[6], sqkv_c0, sqkv_c1, sout_c, sout_c1, result, bf(state_new),
+    first_grad, gs0, gs1, gtok0, gtok1, gup, small, landed = chain_back(
+        flag(starts), flag(ends), state_in, update, state_gain, retain, pc0, pc1, ps0, ps1, os0, os1, lse_s,
+        tok0[5], tok0[6], tok1[5], tok1[6], sqkv_c0, sqkv_c1, sout_c, sout_c1, result, state_new,
     )
 
     def projected_back(parts, halo_part, extra=None):
@@ -2007,7 +2174,6 @@
     operands[SQKV_C] = (hs, gs0, gs1)
     operands[OUT_C] = (gy3, oc0, oc1)
     operands[SOUT_C] = (gup, os0, os1)
-    first_grad = bf(jnp.where(begins[block], grad_state, 0.0))
     def through_qkv(g, w):
         return dot_t(g, w)
 
@@ -2021,20 +2187,18 @@
     )
 
     gy1 = bf(grad1)
-    att0 = attend_back(opening, pa0, prior_a0, bf(dot_t(gy1, wout_a)), oa0, lse_a0)
-    att1 = attend_back(opening, pa1, prior_a1, bf(dot_t(gy1, wout_a1)), oa1, lse_a1)
-    halo_a0, halo_a1 = halo_back(att0, att1)
-    ga0, ga1 = projected_back(att0, halo_a0), projected_back(att1, halo_a1)
-    operands[QKV_A] = (h0, ga0, ga1)
+    att0, att1 = attend_back(
+        opening, (pa0, pa1), (prior_a0, prior_a1), (bf(dot_t(gy1, wout_a)), bf(dot_t(gy1, wout_a1))),
+        (oa0, oa1), (lse_a0, lse_a1),
+    )
+    operands[QKV_A] = (h0,)
     operands[OUT_A] = (gy1, oa0, oa1)
-    back_a, gain_a_grad = norm_back(
-        r0, ga, through_qkv(ga0, wqkv_a0) + through_qkv(ga1, wqkv_a1)
-    )
     smalls = jnp.stack(
-        [gain_a_grad, gain_b_grad, gain_c_grad, small[0], gain_d_grad, small[1]]
+        [jnp.zeros_like(gain_b_grad), gain_b_grad, gain_c_grad, small[0], gain_d_grad, small[1]]
     )
     shares, last_share, landed_input = weight_grads(
-        operands, first_grad, jnp.pad(bf(smalls), ((0, TILE - 6), (0, 0))), bf(grad1 + back_a)
+        operands, first_grad, jnp.pad(bf(smalls), ((0, TILE - 6), (0, 0))), (*att0[3:5], *att1[3:5]),
+        (*att0[:3], *att1[:3], wqkv_a0, wqkv_a1, tokens, grad1), ga[None, :],
     )
     small_share = last_share[1].astype(f32)
     chosen = (

time: 909 us -> 888 us (0.977)
  matrix products: 110 us -> 64.8 us
  Pallas kernels: 663 us -> 696 us
    pallas_call x10 -> x7, Pallas kernels: 494 us -> 533 us  [the longest x1 316 us: weight_grads(): pl.pallas_call(grads_kernel, in_specs=[anywhere] * (3 * count + 4 + TAIL_...]
    dot_general x16 -> x10, matrix products: 51 us -> 26.8 us  [dot_t(): lax.dot_general(a, b, (((1,), (1,)), ((), ())), preferred_element_type=f32)]
    dot_general x18 -> x14, matrix products: 58.6 us -> 38 us  [dot(): return jnp.dot(a, b, preferred_element_type=f32)]
    unnamed x299 -> x197, local copies, waits for them, and re-layouts: 31.1 us -> 23.6 us
    convert_element_type x13 -> x9, other arithmetic: 18.4 us -> 12.5 us  [bf(): return a.astype(jnp.bfloat16)]
  transfers between devices with their start and end apart: 7 -> 6, of which waited for: 0 -> 1; matrix products, arithmetic and copies ran while one was open for 10% -> 7% of each run, Pallas kernels for 24% -> 24%
where the time goes in v4:
time: 888 us; the launch traced here: 881 us
  Pallas kernels  696 us (78%)
  matrix products  64.8 us (7%)
  other arithmetic  50.3 us (6%)
  local copies, waits for them, and re-layouts  39.1 us (4%)
  between operations  18.2 us (2%)
    pallas_call x1, Pallas kernels, weight_grads(): pl.pallas_call(grads_kernel, in_specs=[anywhere] * (3 * count + 4 + TAIL_...  316 us
    pallas_call x1, Pallas kernels, chain_back(): pl.pallas_call(chain_back_kernel, in_specs=[vmem] * 11 + [anywhere] * (LA...  124 us
    pallas_call x1, Pallas kernels, gather(): pl.pallas_call(functools.partial(gather_kernel, count), in_specs=[anywher...  100 us
    pallas_call x1, Pallas kernels, chain(): pl.pallas_call(chain_kernel, in_specs=[vmem] * 10 + [anywhere], out_specs...  63.5 us
    pallas_call x2, Pallas kernels, attend_back(): pl.pallas_call(functools.partial(both_sides, functools.partial(attend_bac...  38.7 us
    dot_general x14, matrix products, dot(): return jnp.dot(a, b, preferred_element_type=f32)  38 us
    pallas_call x1, Pallas kernels, last_layer(): pl.pallas_call(last_layer_kernel, grid=(2 * half,), in_specs=[pl.BlockSpe...  28 us
    dot_general x10, matrix products, dot_t(): lax.dot_general(a, b, (((1,), (1,)), ((), ())), preferred_element_type=f32)  26.8 us
  transfers between devices with their start and end apart: 6, of which 1 were waited for; matrix products, arithmetic and copies ran while one was open for 7% of the time, Pallas kernels for 24%

profile of v4, /device:TPU:0, one launch (start us, length us, event | category | flops | bytes accessed | tf_op | source)
XLA Modules:
  0.0 880.6 jit_solution(18414852211464830254)
XLA Ops:
  10.3 2.4 copy-done.35
  15.3 2.9 pad_maximum_fusion
  18.2 100.1 %shard_map.356 = (bf16[512,1024]{1,0:T(8,128)(2,1)}, bf16[512,1024]{1,0:T(8,128)(2,1)}, bf16[512,1024]{1,0:T(8,128)(2,1)}, bf16[512,1024]{1,0:T(8,128)(2,1)}, bf...) custom-call(bf16[1,8,256,1024]{3,2,1,0:T(8,128)(2,1)} %layer_input.1, ...), custom_call_target="tpu_custom_call" | custom-call | bytes 209715200 | tf_op jit(solution)/shard_map/pallas_call | solution.py:1186
  118.3 2.4 constant_dynamic-slice_fusion.1
  121.3 2.3 constant_dynamic-slice_fusion
  126.6 2.9 convolution_convert_fusion.3.refs_0_.refs_1_.refs_2_
  129.8 2.3 fusion.37.refs_3_.refs_4_
  132.1 2.9 convolution_convert_fusion.2.refs_5_.refs_6_.refs_7_.refs_8_.refs_9_.refs_10_
  135.0 2.3 fusion.34.refs_8_.refs_9_.refs_11_.refs_12_
  140.3 11.2 %shard_map.357 = (bf16[512,512]{1,0:T(8,128)(2,1)}, f32[4,512,1]{2,1,0:T(8,128)}, bf16[512,512]{1,0:T(8,128)(2,1)}, f32[4,512,1]{2,1,0:T(8,128)}) custom-call(s32[1]{0:T(128)} %bitcast.16.open_ref, bf16[512,1536]{1,0:T(8,128)(2,1)} %convolution_convert_fusion.3.refs_0_.refs_1_.refs_2_, bf16[512,1536]{1,0:T(8,128)(2,1)} %convolution_convert_fusion.3.refs_0_.refs_1_.refs_2_, ...), custom_call_target="tpu_custom_call" | custom-call | flops 2147483648 | bytes 8388608 | tf_op jit(solution)/shard_map/pallas_call | solution.py:935
  156.4 5.8 multiply_convert_fusion.1
  162.2 6.8 collective-permute-done.1
  174.3 7.8 multiply_convert_fusion
  182.1 2.3 fusion.60
  186.4 2.5 multiply_reduce_fusion.7
  200.4 63.5 %shard_map.358 = (f32[512,1024]{1,0:T(8,128)}, bf16[512,1024]{1,0:T(8,128)(2,1)}, bf16[512,1536]{1,0:T(8,128)(2,1)}, bf16[512,1536]{1,0:T(8,128)(2,1)}, bf16[512...) custom-call(f32[512,1024]{1,0:T(8,128)} %convert_element_type.185.in, ...), custom_call_target="tpu_custom_call" | custom-call | flops 25769803776 | bytes 26214400 | tf_op jit(solution)/shard_map/pallas_call | solution.py:1358
  264.0 3.1 fusion.31.gy.refs_1_
  268.5 14.4 %shard_map.359 = (bf16[512,512]{1,0:T(8,128)(2,1)}, f32[4,512,1]{2,1,0:T(8,128)}, bf16[512,512]{1,0:T(8,128)(2,1)}, f32[4,512,1]{2,1,0:T(8,128)}) custom-call(s32[1]{0:T(128)} %bitcast.16.open_ref, bf16[512,1536]{1,0:T(8,128)(2,1)} %copy-done.3, bf16[512,1536]{1,0:T(8,128)(2,1)} %copy-done.3, bf16[512,1536]{1,0:T(8,128)(2,1)} %copy-done.3, ...), custom_call_target="tpu_custom_call" | custom-call | flops 3221225472 | bytes 8388608 | tf_op jit(solution)/shard_map/pallas_call | solution.py:935
  287.6 28.0 %shard_map.360 = (bf16[512,2048]{1,0:T(8,128)(2,1)}, bf16[512,2048]{1,0:T(8,128)(2,1)}, bf16[512,2048]{1,0:T(8,128)(2,1)}, bf16[512,2048]{1,0:T(8,128)(2,1)}, bf...) custom-call(s32[1]{0:T(128)S(6)} %broadcast_in_dim.117.alive, bf16[512,1024]{1,0:T(8,128)(2,1)} %multiply_convert_fusion.2.h.refs_0_, ...), custom_call_target="tpu_custom_call" | custom-call | flops 17179869184 | bytes 33554432 | tf_op jit(solution)/shard_map/pallas_call | solution.py:2012
  315.6 3.0 multiply_reduce_fusion
  323.7 22.9 %shard_map.361 = (bf16[512,512]{1,0:T(8,128)(2,1)}, f32[512,512]{1,0:T(8,128)}, f32[512,512]{1,0:T(8,128)}, bf16[512,512]{1,0:T(8,128)(2,1)}, bf16[512,512]{1,0:...) custom-call(s32[1]{0:T(128)} %bitcast.16.open_ref, ...), custom_call_target="tpu_custom_call" | custom-call | flops 8053063680 | bytes 25165824 | tf_op jit(solution)/shard_map/pallas_call | solution.py:1023
  352.0 124.4 %shard_map.362 = (bf16[512,1024]{1,0:T(8,128)(2,1)}, bf16[512,1536]{1,0:T(8,128)(2,1)}, bf16[512,1536]{1,0:T(8,128)(2,1)}, f32[512,1024]{1,0:T(8,128)}, f32[512,...) custom-call(f32[1,1024]{1,0:T(1,128)} %broadcast_in_dim.109.starts, ...), custom_call_target="tpu_custom_call" | custom-call | flops 51539607552 | bytes 47185920 | tf_op jit(solution)/shard_map/pallas_call | solution.py:1558
  476.5 2.4 slice.117
  486.4 3.7 fusion.53
  496.2 2.2 fusion.56
  500.1 4.7 fusion.6.refs_12_
  504.8 2.4 fusion.62
  509.0 4.9 fusion.13.refs_21_
  514.0 2.8 multiply_reduce_fusion.2
  522.8 15.8 %shard_map.363 = (bf16[512,512]{1,0:T(8,128)(2,1)}, f32[512,512]{1,0:T(8,128)}, f32[512,512]{1,0:T(8,128)}, bf16[512,512]{1,0:T(8,128)(2,1)}, bf16[512,512]{1,0:...) custom-call(s32[1]{0:T(128)} %bitcast.16.open_ref, ...), custom_call_target="tpu_custom_call" | custom-call | flops 5368709120 | bytes 25165824 | tf_op jit(solution)/shard_map/pallas_call | solution.py:1023
  538.6 316.2 %shard_map.364 = (bf16[256,2048]{1,0:T(8,128)(2,1)}, bf16[2048,256]{1,0:T(8,128)(2,1)}, bf16[256,2048]{1,0:T(8,128)(2,1)}, bf16[2048,256]{1,0:T(8,128)(2,1)}, bf...) custom-call(bf16[512,1024]{1,0:T(8,128)(2,1)} %multiply_convert_fusi, ...), custom_call_target="tpu_custom_call" | custom-call | flops 31138512896 | bytes 152043520 | tf_op jit(solution)/shard_map/pallas_call | solution.py:1917
  854.8 2.8 convert_element_type.205
  (293 shorter events, 88.3 us)
Async XLA Ops:
  7.2 280.2 %all-gather.3.cloned.1.call-start = ((), (), s32[]{:S(2)}) async-start(), calls=%async_computation | async-start | bytes 5242880 | tf_op jit(solution)/shard_map/all_gather | solution.py:2101
  10.1 5.0 copy-start.30
  10.1 5.0 copy-start.32
  12.7 181.0 %copy-start.22 = (bf16[1024,512]{1,0:T(8,128)(2,1)}, bf16[1024,512]{1,0:T(8,128)(2,1)S(1)}, u32[]{:S(2)}) copy-start(bf16[1024,512]{1,0:T(8,128)(2,1)S(1)} %get-tuple-element.275) | copy-start | bytes 3145732
  118.3 6.7 copy-start.75
  118.3 6.7 copy-start.13
  120.7 41.5 %collective-permute-start = (bf16[256,2048]{1,0:T(8,128)(2,1)}, bf16[256,2048]{1,0:T(8,128)(2,1)}, u32[]{:S(2)}, u32[]{:S(2)}) collective-permute-start(bf16[256,2048]{1,0:T(8,128)(2,1)} %constant_dynamic-slice_fusion.1), channel_id=1, source_target_pairs={{0,1},{1,0},{2,3},{3,2},{4,5},{5,4},{6,7},{7,6},{8,9},{9,8},{10,11... | collective-permute-start | bytes 3145736 | tf_op jit(solution)/shard_map/ppermute | solution.py:2063
  123.5 45.4 %collective-permute-start.1 = (bf16[512,1024]{1,0:T(8,128)(2,1)}, bf16[512,1024]{1,0:T(8,128)(2,1)}, u32[]{:S(2)}, u32[]{:S(2)}) collective-permute-start(bf16[512,1024]{1,0:T(8,128)(2,1)} %constant_dynamic-slice_fusion), channel_id=1, source_target_pairs={{0,1},{1,0},{2,3},{3,2},{4,5},{5,4},{6,7},{7,6},{8,9},{9,8},{10,11... | collective-permute-start | bytes 3145736 | tf_op jit(solution)/shard_map/ppermute | solution.py:2063
  125.0 10.0 %copy-start.74 = (f32[1024]{0:T(1024)}, f32[1024]{0:T(1024)S(1)}, u32[]{:S(2)}) copy-start(f32[1024]{0:T(1024)S(1)} %convert_element_type.169) | copy-start | bytes 12292
  126.6 5.5 copy-start.54
  140.3 11.2 %copy-start.20 = (bf16[512,1024]{1,0:T(8,128)(2,1)S(1)}, bf16[512,1024]{1,0:T(8,128)(2,1)}, u32[]{:S(2)}) copy-start(bf16[512,1024]{1,0:T(8,128)(2,1)} %refs_0_.1) | copy-start | bytes 3145732
  156.4 18.0 %copy-start.55 = (bf16[512,1024]{1,0:T(8,128)(2,1)}, bf16[512,1024]{1,0:T(8,128)(2,1)S(1)}, u32[]{:S(2)}) copy-start(bf16[512,1024]{1,0:T(8,128)(2,1)S(1)} %multiply_convert_fusion.4.refs_2_) | copy-start | bytes 3145732
  156.4 14.6 %copy-start.77 = (bf16[1024]{0:T(1024)(128)(2,1)S(1)}, bf16[1024]{0:T(1024)(128)(2,1)}, u32[]{:S(2)}) copy-start(bf16[1024]{0:T(1024)(128)(2,1)} %param.32) | copy-start | bytes 6148
  156.4 15.2 %copy-start.78 = (bf16[1024]{0:T(1024)(128)(2,1)S(1)}, bf16[1024]{0:T(1024)(128)(2,1)}, u32[]{:S(2)}) copy-start(bf16[1024]{0:T(1024)(128)(2,1)} %param.31) | copy-start | bytes 6148
  156.4 15.2 %copy-start.44 = (bf16[512,1024]{1,0:T(8,128)(2,1)S(1)}, bf16[512,1024]{1,0:T(8,128)(2,1)}, u32[]{:S(2)}) copy-start(bf16[512,1024]{1,0:T(8,128)(2,1)} %get-tuple-element.118) | copy-start | bytes 3145732
  168.9 4.2 copy-start.79
  168.9 4.8 copy-start.80
  169.0 118.4 %all-gather.5.cloned.1.call-start = ((), (), s32[]{:S(2)}) async-start(), calls=%async_computation.1 | async-start | bytes 5242880 | tf_op jit(solution)/shard_map/all_gather | solution.py:2101
  174.3 7.8 copy-start.87
  182.1 4.2 copy-start.92
  198.3 68.8 %collective-permute-start.2 = (bf16[2,512,1024]{2,1,0:T(8,128)(2,1)}, bf16[2,512,1024]{2,1,0:T(8,128)(2,1)S(1)}, u32[]{:S(2)}, u32[]{:S(2)}) collective-permute-start(bf16[2,512,1024]{2,1,0:T(8,128)(2,1)} %pad_maximum_fusion.3), channel_id=1, source_target_pairs={{0,8},{8,1},{1,9},{9,17},{17,25},{25,16},{16,24},{2,10},{10,3},{3,... | collective-permute-start | bytes 6291464 | tf_op jit(solution)/shard_map/ppermute | solution.py:2106
  268.5 14.5 %copy-start.18 = (bf16[512,1024]{1,0:T(8,128)(2,1)S(1)}, bf16[512,1024]{1,0:T(8,128)(2,1)}, u32[]{:S(2)}) copy-start(bf16[512,1024]{1,0:T(8,128)(2,1)} %refs_2_.1) | copy-start | bytes 3145732
  287.6 31.0 %copy-start.12 = (bf16[512,1024]{1,0:T(8,128)(2,1)S(1)}, bf16[512,1024]{1,0:T(8,128)(2,1)}, u32[]{:S(2)}) copy-start(bf16[512,1024]{1,0:T(8,128)(2,1)} %get-tuple-element.128) | copy-start | bytes 3145732
  350.2 131.1 %collective-permute-start.3 = (bf16[2,512,1024]{2,1,0:T(8,128)(2,1)}, bf16[2,512,1024]{2,1,0:T(8,128)(2,1)}, u32[]{:S(2)}, u32[]{:S(2)}) collective-permute-start(bf16[2,512,1024]{2,1,0:T(8,128)(2,1)} %pad_maximum_fusion.4), channel_id=1, source_target_pairs={{8,0},{1,8},{9,1},{17,9},{25,17},{16,25},{24,16},{10,2},{3,10},{11... | collective-permute-start | bytes 6291464 | tf_op jit(solution)/shard_map/ppermute | solution.py:2156
  498.5 8.7 copy-start.45
  500.1 4.7 copy-start.17
  504.8 4.2 copy-start.94
  509.0 5.0 copy-start.11
  509.0 5.0 copy-start.71
  509.0 5.0 copy-start.73
  509.0 5.0 copy-start.86
  854.8 4.2 copy-start.61
  (71 other events, 168.2 us)
Sparse Core Ops, SparseCore 0:
  169.1 34.7 all-gather.2
  205.5 37.6 all-gather.4

commit v5 on v4

--- a/solution.py
+++ b/solution.py
@@ -1273,7 +1273,7 @@
     count, width = initial.shape
     half = os0.shape[1]
     parts = count // CHUNK
-    state[...] = initial[...]
+    state[...] = initial[...].astype(jnp.float32)
 
     def copy(slot, part):
         return pass_on(sent, landed, send_sem, recv_sem, slot, part, following)
@@ -1287,7 +1287,7 @@
                 slot = turn - 1
                 copy(slot, part).wait_recv()
                 state[rows] = jnp.where(
-                    starts[...] > 0.0, initial[rows], landed[slot, rows].astype(jnp.float32)
+                    starts[...] > 0.0, initial[rows].astype(jnp.float32), landed[slot, rows].astype(jnp.float32)
                 )
 
             value = state[rows]
@@ -2073,7 +2073,6 @@
     wout_a1, sout_c1, wout_c1, wqkv_a1, wqkv_c1, sqkv_c1, up_b1, down_b1 = others
     tokens, late_up, late_down = lax.optimization_barrier((tokens, up_d, down_d))
     pieces = crossed(late_up), crossed(late_down)
-    initial = initial.astype(f32)
 
     def normed(values, gain):
         return bf(values * inverse_rms(values) * gain)
@@ -2153,7 +2152,7 @@
         pair = in_order(
             jnp.concatenate([one[3], one[4]], axis=1), jnp.concatenate([two[3], two[4]], axis=1)
         )
-        back = lax.ppermute(jnp.stack(pair), GROUP, TO_PRIOR).astype(f32)
+        back = lax.ppermute(jnp.stack(pair), GROUP, TO_PRIOR)
         return in_order(back[0], back[1])
 
     halo_c0, halo_c1 = halo_back(tok0, tok1)
@@ -2163,7 +2162,7 @@
     )
 
     def projected_back(parts, halo_part, extra=None):
-        pair = jnp.concatenate([parts[1], parts[2]], axis=1) + halo_part
+        pair = jnp.concatenate([parts[1], parts[2]], axis=1) + halo_part.astype(f32)
         if extra is not None:
             pair = pair + extra
         return jnp.concatenate([parts[0], bf(pair)], axis=1)

time: 888 us -> 885 us (level)
    unnamed x197 -> x189, local copies, waits for them, and re-layouts: 23.6 us -> 22 us
where the time goes in v5:
time: 885 us; the launch traced here: 877 us
  Pallas kernels  697 us (79%)
  matrix products  62.8 us (7%)
  other arithmetic  48.7 us (6%)
  local copies, waits for them, and re-layouts  38.7 us (4%)
  between operations  18 us (2%)
    pallas_call x1, Pallas kernels, weight_grads(): pl.pallas_call(grads_kernel, in_specs=[anywhere] * (3 * count + 4 + TAIL_...  317 us
    pallas_call x1, Pallas kernels, chain_back(): pl.pallas_call(chain_back_kernel, in_specs=[vmem] * 11 + [anywhere] * (LA...  123 us
    pallas_call x1, Pallas kernels, gather(): pl.pallas_call(functools.partial(gather_kernel, count), in_specs=[anywher...  100 us
    pallas_call x1, Pallas kernels, chain(): pl.pallas_call(chain_kernel, in_specs=[vmem] * 10 + [anywhere], out_specs...  64.8 us
    pallas_call x2, Pallas kernels, attend_back(): pl.pallas_call(functools.partial(both_sides, functools.partial(attend_bac...  39 us
    dot_general x14, matrix products, dot(): return jnp.dot(a, b, preferred_element_type=f32)  37.9 us
    pallas_call x1, Pallas kernels, last_layer(): pl.pallas_call(last_layer_kernel, grid=(2 * half,), in_specs=[pl.BlockSpe...  28 us
    pallas_call x2, Pallas kernels, attend(): pl.pallas_call(functools.partial(both_sides, functools.partial(attend_ker...  25.6 us
  transfers between devices with their start and end apart: 6, of which 1 were waited for; matrix products, arithmetic and copies ran while one was open for 7% of the time, Pallas kernels for 24%

profile of v5, /device:TPU:0, one launch (start us, length us, event | category | flops | bytes accessed | tf_op | source)
XLA Modules:
  0.0 877.2 jit_solution(2395212909837508924)
XLA Ops:
  7.3 2.2 slice_bitcast_fusion.5
  10.3 2.8 copy-done.35
  15.5 2.9 pad_maximum_fusion
  18.3 100.1 %shard_map.356 = (bf16[512,1024]{1,0:T(8,128)(2,1)}, bf16[512,1024]{1,0:T(8,128)(2,1)}, bf16[512,1024]{1,0:T(8,128)(2,1)}, bf16[512,1024]{1,0:T(8,128)(2,1)}, bf...) custom-call(bf16[1,8,256,1024]{3,2,1,0:T(8,128)(2,1)} %layer_input.1, ...), custom_call_target="tpu_custom_call" | custom-call | bytes 209715200 | tf_op jit(solution)/shard_map/pallas_call | solution.py:1186
  118.4 2.4 constant_dynamic-slice_fusion.1
  121.4 2.3 constant_dynamic-slice_fusion
  126.7 2.9 convolution_convert_fusion.3.refs_0_.refs_1_.refs_2_
  129.6 2.9 convolution_convert_fusion.2.refs_5_.refs_6_.refs_7_.refs_8_.refs_9_.refs_10_
  132.8 2.3 fusion.34.refs_8_.refs_9_.refs_11_.refs_12_
  135.2 2.3 fusion.37.refs_3_.refs_4_
  140.4 11.2 %shard_map.357 = (bf16[512,512]{1,0:T(8,128)(2,1)}, f32[4,512,1]{2,1,0:T(8,128)}, bf16[512,512]{1,0:T(8,128)(2,1)}, f32[4,512,1]{2,1,0:T(8,128)}) custom-call(s32[1]{0:T(128)} %bitcast.16.open_ref, bf16[512,1536]{1,0:T(8,128)(2,1)} %convolution_convert_fusion.3.refs_0_.refs_1_.refs_2_, bf16[512,1536]{1,0:T(8,128)(2,1)} %convolution_convert_fusion.3.refs_0_.refs_1_.refs_2_, ...), custom_call_target="tpu_custom_call" | custom-call | flops 2147483648 | bytes 8388608 | tf_op jit(solution)/shard_map/pallas_call | solution.py:935
  156.5 5.8 multiply_convert_fusion.1
  162.3 6.7 collective-permute-done.1
  172.9 7.7 multiply_convert_fusion
  180.6 2.3 fusion.60
  184.8 2.5 multiply_reduce_fusion.7
  199.1 64.8 %shard_map.358 = (f32[512,1024]{1,0:T(8,128)}, bf16[512,1024]{1,0:T(8,128)(2,1)}, bf16[512,1536]{1,0:T(8,128)(2,1)}, bf16[512,1536]{1,0:T(8,128)(2,1)}, bf16[512...) custom-call(bf16[512,1024]{1,0:T(8,128)(2,1)} %get-tuple-element.118, ...), custom_call_target="tpu_custom_call" | custom-call | flops 25769803776 | bytes 26214400 | tf_op jit(solution)/shard_map/pallas_call | solution.py:1358
  263.9 3.1 fusion.31.gy.refs_1_
  268.5 14.4 %shard_map.359 = (bf16[512,512]{1,0:T(8,128)(2,1)}, f32[4,512,1]{2,1,0:T(8,128)}, bf16[512,512]{1,0:T(8,128)(2,1)}, f32[4,512,1]{2,1,0:T(8,128)}) custom-call(s32[1]{0:T(128)} %bitcast.16.open_ref, bf16[512,1536]{1,0:T(8,128)(2,1)} %copy-done.3, bf16[512,1536]{1,0:T(8,128)(2,1)} %copy-done.3, bf16[512,1536]{1,0:T(8,128)(2,1)} %copy-done.3, ...), custom_call_target="tpu_custom_call" | custom-call | flops 3221225472 | bytes 8388608 | tf_op jit(solution)/shard_map/pallas_call | solution.py:935
  287.6 28.0 %shard_map.360 = (bf16[512,2048]{1,0:T(8,128)(2,1)}, bf16[512,2048]{1,0:T(8,128)(2,1)}, bf16[512,2048]{1,0:T(8,128)(2,1)}, bf16[512,2048]{1,0:T(8,128)(2,1)}, bf...) custom-call(s32[1]{0:T(128)S(6)} %broadcast_in_dim.117.alive, bf16[512,1024]{1,0:T(8,128)(2,1)} %multiply_convert_fusion.2.h.refs_0_, ...), custom_call_target="tpu_custom_call" | custom-call | flops 17179869184 | bytes 33554432 | tf_op jit(solution)/shard_map/pallas_call | solution.py:2012
  315.6 3.0 multiply_reduce_fusion
  323.7 23.2 %shard_map.361 = (bf16[512,512]{1,0:T(8,128)(2,1)}, f32[512,512]{1,0:T(8,128)}, f32[512,512]{1,0:T(8,128)}, bf16[512,512]{1,0:T(8,128)(2,1)}, bf16[512,512]{1,0:...) custom-call(s32[1]{0:T(128)} %bitcast.16.open_ref, ...), custom_call_target="tpu_custom_call" | custom-call | flops 8053063680 | bytes 25165824 | tf_op jit(solution)/shard_map/pallas_call | solution.py:1023
  352.3 122.8 %shard_map.362 = (bf16[512,1024]{1,0:T(8,128)(2,1)}, bf16[512,1536]{1,0:T(8,128)(2,1)}, bf16[512,1536]{1,0:T(8,128)(2,1)}, f32[512,1024]{1,0:T(8,128)}, f32[512,...) custom-call(f32[1,1024]{1,0:T(1,128)} %broadcast_in_dim.109.starts, ...), custom_call_target="tpu_custom_call" | custom-call | flops 51539607552 | bytes 47185920 | tf_op jit(solution)/shard_map/pallas_call | solution.py:1558
  476.0 2.4 slice.117
  481.5 3.9 fusion.30
  490.3 2.3 fusion.56
  494.1 4.7 fusion.13.refs_21_
  498.8 4.9 fusion.6.refs_12_
  505.0 2.4 fusion.62
  507.9 2.8 multiply_reduce_fusion.2
  519.2 15.8 %shard_map.363 = (bf16[512,512]{1,0:T(8,128)(2,1)}, f32[512,512]{1,0:T(8,128)}, f32[512,512]{1,0:T(8,128)}, bf16[512,512]{1,0:T(8,128)(2,1)}, bf16[512,512]{1,0:...) custom-call(s32[1]{0:T(128)} %bitcast.16.open_ref, ...), custom_call_target="tpu_custom_call" | custom-call | flops 5368709120 | bytes 25165824 | tf_op jit(solution)/shard_map/pallas_call | solution.py:1023
  535.0 316.8 %shard_map.364 = (bf16[256,2048]{1,0:T(8,128)(2,1)}, bf16[2048,256]{1,0:T(8,128)(2,1)}, bf16[256,2048]{1,0:T(8,128)(2,1)}, bf16[2048,256]{1,0:T(8,128)(2,1)}, bf...) custom-call(bf16[512,1024]{1,0:T(8,128)(2,1)} %multiply_convert_fusi, ...), custom_call_target="tpu_custom_call" | custom-call | flops 31138512896 | bytes 152043520 | tf_op jit(solution)/shard_map/pallas_call | solution.py:1917
  (283 shorter events, 84.8 us)
Async XLA Ops:
  7.2 280.2 %all-gather.3.cloned.1.call-start = ((), (), s32[]{:S(2)}) async-start(), calls=%async_computation | async-start | bytes 5242880 | tf_op jit(solution)/shard_map/all_gather | solution.py:2100
  10.1 5.2 copy-start.24
  10.1 5.2 copy-start.27
  10.1 182.1 %copy-start.22 = (bf16[1024,512]{1,0:T(8,128)(2,1)}, bf16[1024,512]{1,0:T(8,128)(2,1)S(1)}, u32[]{:S(2)}) copy-start(bf16[1024,512]{1,0:T(8,128)(2,1)S(1)} %get-tuple-element.273) | copy-start | bytes 3145732
  118.4 6.7 copy-start.13
  120.8 4.6 copy-start.70
  120.8 41.5 %collective-permute-start = (bf16[256,2048]{1,0:T(8,128)(2,1)}, bf16[256,2048]{1,0:T(8,128)(2,1)}, u32[]{:S(2)}, u32[]{:S(2)}) collective-permute-start(bf16[256,2048]{1,0:T(8,128)(2,1)} %constant_dynamic-slice_fusion.1), channel_id=1, source_target_pairs={{0,1},{1,0},{2,3},{3,2},{4,5},{5,4},{6,7},{7,6},{8,9},{9,8},{10,11... | collective-permute-start | bytes 3145736 | tf_op jit(solution)/shard_map/ppermute | solution.py:2063
  123.6 45.4 %collective-permute-start.1 = (bf16[512,1024]{1,0:T(8,128)(2,1)}, bf16[512,1024]{1,0:T(8,128)(2,1)}, u32[]{:S(2)}, u32[]{:S(2)}) collective-permute-start(bf16[512,1024]{1,0:T(8,128)(2,1)} %constant_dynamic-slice_fusion), channel_id=1, source_target_pairs={{0,1},{1,0},{2,3},{3,2},{4,5},{5,4},{6,7},{7,6},{8,9},{9,8},{10,11... | collective-permute-start | bytes 3145736 | tf_op jit(solution)/shard_map/ppermute | solution.py:2063
  125.4 9.7 %copy-start.69 = (f32[1024]{0:T(1024)}, f32[1024]{0:T(1024)S(1)}, u32[]{:S(2)}) copy-start(f32[1024]{0:T(1024)S(1)} %convert_element_type.175) | copy-start | bytes 12292
  140.4 11.2 %copy-start.20 = (bf16[512,1024]{1,0:T(8,128)(2,1)S(1)}, bf16[512,1024]{1,0:T(8,128)(2,1)}, u32[]{:S(2)}) copy-start(bf16[512,1024]{1,0:T(8,128)(2,1)} %refs_0_.1) | copy-start | bytes 3145732
  156.5 16.4 %copy-start.51 = (bf16[512,1024]{1,0:T(8,128)(2,1)}, bf16[512,1024]{1,0:T(8,128)(2,1)S(1)}, u32[]{:S(2)}) copy-start(bf16[512,1024]{1,0:T(8,128)(2,1)S(1)} %multiply_convert_fusion.4.refs_2_) | copy-start | bytes 3145732
  156.5 13.9 %copy-start.72 = (bf16[1024]{0:T(1024)(128)(2,1)S(1)}, bf16[1024]{0:T(1024)(128)(2,1)}, u32[]{:S(2)}) copy-start(bf16[1024]{0:T(1024)(128)(2,1)} %param.31) | copy-start | bytes 6148
  156.5 13.9 %copy-start.73 = (bf16[1024]{0:T(1024)(128)(2,1)S(1)}, bf16[1024]{0:T(1024)(128)(2,1)}, u32[]{:S(2)}) copy-start(bf16[1024]{0:T(1024)(128)(2,1)} %param.32) | copy-start | bytes 6148
  156.5 14.5 %copy-start.74 = (bf16[1024]{0:T(1024)(128)(2,1)S(1)}, bf16[1024]{0:T(1024)(128)(2,1)}, u32[]{:S(2)}) copy-start(bf16[1024]{0:T(1024)(128)(2,1)} %param.39) | copy-start | bytes 6148
  156.5 15.8 %copy-start.75 = (bf16[1024]{0:T(1024)(128)(2,1)S(1)}, bf16[1024]{0:T(1024)(128)(2,1)}, u32[]{:S(2)}) copy-start(bf16[1024]{0:T(1024)(128)(2,1)} %param.37) | copy-start | bytes 6148
  169.1 118.3 %all-gather.5.cloned.1.call-start = ((), (), s32[]{:S(2)}) async-start(), calls=%async_computation.1 | async-start | bytes 5242880 | tf_op jit(solution)/shard_map/all_gather | solution.py:2100
  172.9 7.7 copy-start.82
  180.6 4.2 copy-start.88
  196.7 70.3 %collective-permute-start.2 = (bf16[2,512,1024]{2,1,0:T(8,128)(2,1)}, bf16[2,512,1024]{2,1,0:T(8,128)(2,1)S(1)}, u32[]{:S(2)}, u32[]{:S(2)}) collective-permute-start(bf16[2,512,1024]{2,1,0:T(8,128)(2,1)} %pad_maximum_fusion.3), channel_id=1, source_target_pairs={{0,8},{8,1},{1,9},{9,17},{17,25},{25,16},{16,24},{2,10},{10,3},{3,... | collective-permute-start | bytes 6291464 | tf_op jit(solution)/shard_map/ppermute | solution.py:2105
  268.5 14.5 %copy-start.18 = (bf16[512,1024]{1,0:T(8,128)(2,1)S(1)}, bf16[512,1024]{1,0:T(8,128)(2,1)}, u32[]{:S(2)}) copy-start(bf16[512,1024]{1,0:T(8,128)(2,1)} %refs_2_.1) | copy-start | bytes 3145732
  287.6 31.0 %copy-start.12 = (bf16[512,1024]{1,0:T(8,128)(2,1)S(1)}, bf16[512,1024]{1,0:T(8,128)(2,1)}, u32[]{:S(2)}) copy-start(bf16[512,1024]{1,0:T(8,128)(2,1)} %get-tuple-element.128) | copy-start | bytes 3145732
  350.5 131.0 %collective-permute-start.3 = (bf16[2,512,1024]{2,1,0:T(8,128)(2,1)}, bf16[2,512,1024]{2,1,0:T(8,128)(2,1)}, u32[]{:S(2)}, u32[]{:S(2)}) collective-permute-start(bf16[2,512,1024]{2,1,0:T(8,128)(2,1)} %pad_maximum_fusion.4), channel_id=1, source_target_pairs={{8,0},{1,8},{9,1},{17,9},{25,17},{16,25},{24,16},{10,2},{3,10},{11... | collective-permute-start | bytes 6291464 | tf_op jit(solution)/shard_map/ppermute | solution.py:2155
  476.0 5.5 copy-start.37
  481.5 3.9 copy-start.23
  481.5 3.9 copy-start.26
  481.5 3.9 copy-start.29
  492.6 6.1 copy-start.43
  494.1 4.7 copy-start.15
  494.1 4.7 copy-start.89
  498.8 8.7 copy-start.87
  498.8 6.2 copy-start.17
  864.8 4.5 copy-start.61
  (67 other events, 153.1 us)
Sparse Core Ops, SparseCore 0:
  169.2 33.7 all-gather.2
  204.5 39.2 all-gather.4

commit v6 on v5

--- a/solution.py
+++ b/solution.py
@@ -2096,7 +2096,7 @@
     h1 = normed(r1, gb)
     ub0, ub1 = dot(h1, up_b), dot(h1, up_b1)
     ab0, ab1 = bf(smooth(ub0)), bf(smooth(ub1))
-    ab0, *pieces = lax.optimization_barrier((ab0, *pieces))
+    ab1, *pieces = lax.optimization_barrier((ab1, *pieces))
     up_d1, down_d1 = (lax.all_gather(piece, SECTION, axis=0, tiled=True) for piece in pieces)
     r2 = r1 + (dot(ab0, down_b) + dot(ab1, down_b1))
 

time: 885 us -> 885 us (level)
  no operation moved by 1% of the time
where the time goes in v6:
time: 885 us; the launch traced here: 877 us
  Pallas kernels  697 us (79%)
  matrix products  62.9 us (7%)
  other arithmetic  48.6 us (5%)
  local copies, waits for them, and re-layouts  38.1 us (4%)
  between operations  18 us (2%)
    pallas_call x1, Pallas kernels, weight_grads(): pl.pallas_call(grads_kernel, in_specs=[anywhere] * (3 * count + 4 + TAIL_...  317 us
    pallas_call x1, Pallas kernels, chain_back(): pl.pallas_call(chain_back_kernel, in_specs=[vmem] * 11 + [anywhere] * (LA...  123 us
    pallas_call x1, Pallas kernels, gather(): pl.pallas_call(functools.partial(gather_kernel, count), in_specs=[anywher...  100 us
    pallas_call x1, Pallas kernels, chain(): pl.pallas_call(chain_kernel, in_specs=[vmem] * 10 + [anywhere], out_specs...  64.8 us
    pallas_call x2, Pallas kernels, attend_back(): pl.pallas_call(functools.partial(both_sides, functools.partial(attend_bac...  39 us
    dot_general x14, matrix products, dot(): return jnp.dot(a, b, preferred_element_type=f32)  38 us
    pallas_call x1, Pallas kernels, last_layer(): pl.pallas_call(last_layer_kernel, grid=(2 * half,), in_specs=[pl.BlockSpe...  28 us
    pallas_call x2, Pallas kernels, attend(): pl.pallas_call(functools.partial(both_sides, functools.partial(attend_ker...  25.6 us
  transfers between devices with their start and end apart: 6, of which 1 were waited for; matrix products, arithmetic and copies ran while one was open for 7% of the time, Pallas kernels for 24%

profile of v6, /device:TPU:0, one launch (start us, length us, event | category | flops | bytes accessed | tf_op | source)
XLA Modules:
  0.0 876.8 jit_solution(6923664223352175604)
XLA Ops:
  7.3 2.2 slice_bitcast_fusion.5
  10.3 2.8 copy-done.34
  15.5 2.9 pad_maximum_fusion
  18.3 100.1 %shard_map.356 = (bf16[512,1024]{1,0:T(8,128)(2,1)}, bf16[512,1024]{1,0:T(8,128)(2,1)}, bf16[512,1024]{1,0:T(8,128)(2,1)}, bf16[512,1024]{1,0:T(8,128)(2,1)}, bf...) custom-call(bf16[1,8,256,1024]{3,2,1,0:T(8,128)(2,1)} %layer_input.1, ...), custom_call_target="tpu_custom_call" | custom-call | bytes 209715200 | tf_op jit(solution)/shard_map/pallas_call | solution.py:1186
  118.4 2.4 constant_dynamic-slice_fusion.1
  121.4 2.3 constant_dynamic-slice_fusion
  126.7 2.9 convolution_convert_fusion.3.refs_0_.refs_1_.refs_2_
  129.6 2.9 convolution_convert_fusion.2.refs_5_.refs_6_.refs_7_.refs_8_.refs_9_.refs_10_
  132.8 2.3 fusion.34.refs_8_.refs_9_.refs_11_.refs_12_
  135.2 2.3 fusion.37.refs_3_.refs_4_
  140.4 11.2 %shard_map.357 = (bf16[512,512]{1,0:T(8,128)(2,1)}, f32[4,512,1]{2,1,0:T(8,128)}, bf16[512,512]{1,0:T(8,128)(2,1)}, f32[4,512,1]{2,1,0:T(8,128)}) custom-call(s32[1]{0:T(128)} %bitcast.16.open_ref, bf16[512,1536]{1,0:T(8,128)(2,1)} %convolution_convert_fusion.3.refs_0_.refs_1_.refs_2_, bf16[512,1536]{1,0:T(8,128)(2,1)} %convolution_convert_fusion.3.refs_0_.refs_1_.refs_2_, ...), custom_call_target="tpu_custom_call" | custom-call | flops 2147483648 | bytes 8388608 | tf_op jit(solution)/shard_map/pallas_call | solution.py:935
  156.5 5.8 multiply_convert_fusion
  162.3 6.7 collective-permute-done.1
  172.9 7.7 multiply_convert_fusion.1
  180.6 2.3 fusion.60
  184.8 2.5 multiply_reduce_fusion.7
  199.1 64.8 %shard_map.358 = (f32[512,1024]{1,0:T(8,128)}, bf16[512,1024]{1,0:T(8,128)(2,1)}, bf16[512,1536]{1,0:T(8,128)(2,1)}, bf16[512,1536]{1,0:T(8,128)(2,1)}, bf16[512...) custom-call(bf16[512,1024]{1,0:T(8,128)(2,1)} %get-tuple-element.118, ...), custom_call_target="tpu_custom_call" | custom-call | flops 25769803776 | bytes 26214400 | tf_op jit(solution)/shard_map/pallas_call | solution.py:1358
  263.9 3.1 fusion.31.gy.refs_1_
  268.5 14.4 %shard_map.359 = (bf16[512,512]{1,0:T(8,128)(2,1)}, f32[4,512,1]{2,1,0:T(8,128)}, bf16[512,512]{1,0:T(8,128)(2,1)}, f32[4,512,1]{2,1,0:T(8,128)}) custom-call(s32[1]{0:T(128)} %bitcast.16.open_ref, bf16[512,1536]{1,0:T(8,128)(2,1)} %copy-done.3, bf16[512,1536]{1,0:T(8,128)(2,1)} %copy-done.3, bf16[512,1536]{1,0:T(8,128)(2,1)} %copy-done.3, ...), custom_call_target="tpu_custom_call" | custom-call | flops 3221225472 | bytes 8388608 | tf_op jit(solution)/shard_map/pallas_call | solution.py:935
  287.7 28.0 %shard_map.360 = (bf16[512,2048]{1,0:T(8,128)(2,1)}, bf16[512,2048]{1,0:T(8,128)(2,1)}, bf16[512,2048]{1,0:T(8,128)(2,1)}, bf16[512,2048]{1,0:T(8,128)(2,1)}, bf...) custom-call(s32[1]{0:T(128)S(6)} %broadcast_in_dim.117.alive, bf16[512,1024]{1,0:T(8,128)(2,1)} %multiply_convert_fusion.2.h.refs_0_, ...), custom_call_target="tpu_custom_call" | custom-call | flops 17179869184 | bytes 33554432 | tf_op jit(solution)/shard_map/pallas_call | solution.py:2012
  315.6 3.0 multiply_reduce_fusion
  323.7 23.2 %shard_map.361 = (bf16[512,512]{1,0:T(8,128)(2,1)}, f32[512,512]{1,0:T(8,128)}, f32[512,512]{1,0:T(8,128)}, bf16[512,512]{1,0:T(8,128)(2,1)}, bf16[512,512]{1,0:...) custom-call(s32[1]{0:T(128)} %bitcast.16.open_ref, ...), custom_call_target="tpu_custom_call" | custom-call | flops 8053063680 | bytes 25165824 | tf_op jit(solution)/shard_map/pallas_call | solution.py:1023
  352.4 122.9 %shard_map.362 = (bf16[512,1024]{1,0:T(8,128)(2,1)}, bf16[512,1536]{1,0:T(8,128)(2,1)}, bf16[512,1536]{1,0:T(8,128)(2,1)}, f32[512,1024]{1,0:T(8,128)}, f32[512,...) custom-call(f32[1,1024]{1,0:T(1,128)} %broadcast_in_dim.109.starts, ...), custom_call_target="tpu_custom_call" | custom-call | flops 51539607552 | bytes 47185920 | tf_op jit(solution)/shard_map/pallas_call | solution.py:1558
  476.0 2.4 slice.117
  481.6 3.9 fusion.30
  490.4 2.3 fusion.56
  494.2 4.7 fusion.13.refs_21_
  499.0 4.9 fusion.6.refs_12_
  503.9 2.4 fusion.62
  507.5 2.8 multiply_reduce_fusion.2
  518.8 15.8 %shard_map.363 = (bf16[512,512]{1,0:T(8,128)(2,1)}, f32[512,512]{1,0:T(8,128)}, f32[512,512]{1,0:T(8,128)}, bf16[512,512]{1,0:T(8,128)(2,1)}, bf16[512,512]{1,0:...) custom-call(s32[1]{0:T(128)} %bitcast.16.open_ref, ...), custom_call_target="tpu_custom_call" | custom-call | flops 5368709120 | bytes 25165824 | tf_op jit(solution)/shard_map/pallas_call | solution.py:1023
  534.6 316.8 %shard_map.364 = (bf16[256,2048]{1,0:T(8,128)(2,1)}, bf16[2048,256]{1,0:T(8,128)(2,1)}, bf16[256,2048]{1,0:T(8,128)(2,1)}, bf16[2048,256]{1,0:T(8,128)(2,1)}, bf...) custom-call(bf16[512,1024]{1,0:T(8,128)(2,1)} %multiply_convert_fusi, ...), custom_call_target="tpu_custom_call" | custom-call | flops 31138512896 | bytes 152043520 | tf_op jit(solution)/shard_map/pallas_call | solution.py:1917
  (283 shorter events, 84.3 us)
Async XLA Ops:
  7.2 280.2 %all-gather.3.cloned.1.call-start = ((), (), s32[]{:S(2)}) async-start(), calls=%async_computation | async-start | bytes 5242880 | tf_op jit(solution)/shard_map/all_gather | solution.py:2100
  10.1 5.2 copy-start.23
  10.1 5.2 copy-start.26
  10.1 182.1 %copy-start.21 = (bf16[1024,512]{1,0:T(8,128)(2,1)}, bf16[1024,512]{1,0:T(8,128)(2,1)S(1)}, u32[]{:S(2)}) copy-start(bf16[1024,512]{1,0:T(8,128)(2,1)S(1)} %get-tuple-element.273) | copy-start | bytes 3145732
  118.4 6.7 copy-start.13
  120.8 4.6 copy-start.69
  120.8 41.5 %collective-permute-start = (bf16[256,2048]{1,0:T(8,128)(2,1)}, bf16[256,2048]{1,0:T(8,128)(2,1)}, u32[]{:S(2)}, u32[]{:S(2)}) collective-permute-start(bf16[256,2048]{1,0:T(8,128)(2,1)} %constant_dynamic-slice_fusion.1), channel_id=1, source_target_pairs={{0,1},{1,0},{2,3},{3,2},{4,5},{5,4},{6,7},{7,6},{8,9},{9,8},{10,11... | collective-permute-start | bytes 3145736 | tf_op jit(solution)/shard_map/ppermute | solution.py:2063
  123.6 45.4 %collective-permute-start.1 = (bf16[512,1024]{1,0:T(8,128)(2,1)}, bf16[512,1024]{1,0:T(8,128)(2,1)}, u32[]{:S(2)}, u32[]{:S(2)}) collective-permute-start(bf16[512,1024]{1,0:T(8,128)(2,1)} %constant_dynamic-slice_fusion), channel_id=1, source_target_pairs={{0,1},{1,0},{2,3},{3,2},{4,5},{5,4},{6,7},{7,6},{8,9},{9,8},{10,11... | collective-permute-start | bytes 3145736 | tf_op jit(solution)/shard_map/ppermute | solution.py:2063
  125.4 9.7 %copy-start.68 = (f32[1024]{0:T(1024)}, f32[1024]{0:T(1024)S(1)}, u32[]{:S(2)}) copy-start(f32[1024]{0:T(1024)S(1)} %convert_element_type.175) | copy-start | bytes 12292
  140.4 11.2 %copy-start.19 = (bf16[512,1024]{1,0:T(8,128)(2,1)S(1)}, bf16[512,1024]{1,0:T(8,128)(2,1)}, u32[]{:S(2)}) copy-start(bf16[512,1024]{1,0:T(8,128)(2,1)} %refs_0_.1) | copy-start | bytes 3145732
  156.0 16.8 %copy-start.50 = (bf16[512,1024]{1,0:T(8,128)(2,1)}, bf16[512,1024]{1,0:T(8,128)(2,1)S(1)}, u32[]{:S(2)}) copy-start(bf16[512,1024]{1,0:T(8,128)(2,1)S(1)} %multiply_convert_fusion.4.refs_2_) | copy-start | bytes 3145732
  156.5 13.9 %copy-start.71 = (bf16[1024]{0:T(1024)(128)(2,1)S(1)}, bf16[1024]{0:T(1024)(128)(2,1)}, u32[]{:S(2)}) copy-start(bf16[1024]{0:T(1024)(128)(2,1)} %param.31) | copy-start | bytes 6148
  156.5 13.9 %copy-start.72 = (bf16[1024]{0:T(1024)(128)(2,1)S(1)}, bf16[1024]{0:T(1024)(128)(2,1)}, u32[]{:S(2)}) copy-start(bf16[1024]{0:T(1024)(128)(2,1)} %param.32) | copy-start | bytes 6148
  156.5 14.5 %copy-start.73 = (bf16[1024]{0:T(1024)(128)(2,1)S(1)}, bf16[1024]{0:T(1024)(128)(2,1)}, u32[]{:S(2)}) copy-start(bf16[1024]{0:T(1024)(128)(2,1)} %param.39) | copy-start | bytes 6148
  156.5 15.8 %copy-start.74 = (bf16[1024]{0:T(1024)(128)(2,1)S(1)}, bf16[1024]{0:T(1024)(128)(2,1)}, u32[]{:S(2)}) copy-start(bf16[1024]{0:T(1024)(128)(2,1)} %param.37) | copy-start | bytes 6148
  169.1 118.4 %all-gather.5.cloned.1.call-start = ((), (), s32[]{:S(2)}) async-start(), calls=%async_computation.1 | async-start | bytes 5242880 | tf_op jit(solution)/shard_map/all_gather | solution.py:2100
  172.9 7.7 copy-start.14
  180.6 4.2 copy-start.88
  196.7 70.3 %collective-permute-start.2 = (bf16[2,512,1024]{2,1,0:T(8,128)(2,1)}, bf16[2,512,1024]{2,1,0:T(8,128)(2,1)S(1)}, u32[]{:S(2)}, u32[]{:S(2)}) collective-permute-start(bf16[2,512,1024]{2,1,0:T(8,128)(2,1)} %pad_maximum_fusion.3), channel_id=1, source_target_pairs={{0,8},{8,1},{1,9},{9,17},{17,25},{25,16},{16,24},{2,10},{10,3},{3,... | collective-permute-start | bytes 6291464 | tf_op jit(solution)/shard_map/ppermute | solution.py:2105
  268.5 14.5 %copy-start.17 = (bf16[512,1024]{1,0:T(8,128)(2,1)S(1)}, bf16[512,1024]{1,0:T(8,128)(2,1)}, u32[]{:S(2)}) copy-start(bf16[512,1024]{1,0:T(8,128)(2,1)} %refs_2_.1) | copy-start | bytes 3145732
  287.7 31.0 %copy-start.12 = (bf16[512,1024]{1,0:T(8,128)(2,1)S(1)}, bf16[512,1024]{1,0:T(8,128)(2,1)}, u32[]{:S(2)}) copy-start(bf16[512,1024]{1,0:T(8,128)(2,1)} %get-tuple-element.128) | copy-start | bytes 3145732
  350.5 131.0 %collective-permute-start.3 = (bf16[2,512,1024]{2,1,0:T(8,128)(2,1)}, bf16[2,512,1024]{2,1,0:T(8,128)(2,1)}, u32[]{:S(2)}, u32[]{:S(2)}) collective-permute-start(bf16[2,512,1024]{2,1,0:T(8,128)(2,1)} %pad_maximum_fusion.4), channel_id=1, source_target_pairs={{8,0},{1,8},{9,1},{17,9},{25,17},{16,25},{24,16},{10,2},{3,10},{11... | collective-permute-start | bytes 6291464 | tf_op jit(solution)/shard_map/ppermute | solution.py:2155
  476.0 5.5 copy-start.36
  481.5 3.9 copy-start.22
  481.5 3.9 copy-start.25
  481.5 3.9 copy-start.28
  492.7 6.3 copy-start.42
  494.2 4.7 copy-start.15
  494.2 4.7 copy-start.90
  498.9 7.4 copy-start.87
  499.0 4.9 copy-start.16
  864.5 4.5 copy-start.60
  (67 other events, 155.6 us)
Sparse Core Ops, SparseCore 0:
  169.2 33.7 all-gather.2
  204.5 39.2 all-gather.4
